TPU v7x, 512 devices: a whole 4x8x8 slice. The times are simulated.
512 devices in a mesh: gx: 128 (over x, z, y_lo, core), gy: 4 (over y_hi).
Axes of the slice: x: 4, y: 8 (y_hi: 4, y_lo: 2; y = y_hi * 2 + y_lo), z: 8, core: 2. Of those that a mesh axis runs over, the one named last changes fastest.
Arguments:
- displacement: float32 [3, 3, 4096, 512], P(None, None, 'gx', 'gy'), may hold values from -6 to 6
- previous: float32 [3, 3, 4096, 512], P(None, None, 'gx', 'gy'), may hold values from -6 to 6
- moduli: float32 [2, 3, 4096, 512], P(None, None, 'gx', 'gy'), may hold values from 0.5 to 2
- density: float32 [3, 4096, 512], P(None, 'gx', 'gy'), may hold values from 0.5 to 2
- bins: float32 [2, 3, 2, 4096, 512], P(None, None, None, 'gx', 'gy'), may hold values from -6 to 6
- omega: float32 [2], replicated, may hold values from 0.1 to 1
- phase: float32 [2], replicated, may hold values from -3.140625 to 3.140625
Outputs:
- updated: float32 [3, 3, 4096, 512], P(None, None, 'gx', 'gy')
- middle: float32 [3, 3, 4096, 512], P(None, None, 'gx', 'gy')
- spectrum: float32 [2, 3, 2, 4096, 512], P(None, None, None, 'gx', 'gy')
All inputs are finite; a program needn't handle non-finite values.
Results may differ from a plain program's by a relative error of at most 0.0001.
Values sent between devices are 32-bit elements; how exact they have to be, the bound alone decides.
No kernel may reach another device: no remote copies, remote signals or barrier semaphores. Data moves between devices by JAX's collectives and lax.ppermute only.
A program may use at most 64 MiB of HBM per device.

v0:
```python
import functools

import jax
import jax.numpy as jnp
import numpy as np
from jax import lax
from jax.experimental import pallas as pl
from jax.experimental.pallas import tpu as pltpu
from jax.sharding import PartitionSpec as P

time_step = 0.03
HALO = 4
EDGE = 8
HIGHEST = lax.Precision.HIGHEST


def edge_columns(width):
    table = np.zeros((EDGE, width), np.float32)
    for h in range(HALO):
        table[h, h] = 1.0
        table[HALO + h, width - HALO + h] = 1.0
    return table


def fourier_tables(length):
    index = np.arange(length)
    angle = 2.0 * np.pi * (index[:, None] * index[None, :] % length) / length
    return np.cos(angle), np.sin(angle)


def pack_rows_kernel(disp, prev, moduli, density, select, up, down, main):
    start = 0
    for ref in (disp, prev, moduli, density):
        planes, rows, width = ref.shape
        for i in range(planes):
            at = (start + i) * HALO
            up[at : at + HALO, :] = ref[i, rows - HALO : rows, :]
            down[at : at + HALO, :] = ref[i, :HALO, :]
        flat = ref[...].reshape(planes * rows, width)
        packed = lax.dot_general(
            select[...], flat, (((1,), (1,)), ((), ())), precision=HIGHEST, preferred_element_type=jnp.float32
        )
        main[:, start * rows : (start + planes) * rows] = packed
        start += planes
    used = start * rows
    main[:, used:] = jnp.zeros((EDGE, main.shape[1] - used), jnp.float32)


def pack_columns_kernel(main, before, after, select, first, last):
    width = main.shape[1]
    lanes = select.shape[1]
    first[:, :width] = main[:HALO, :]
    last[:, :width] = main[HALO:, :]
    count = before.shape[0]
    fill = jnp.zeros((lanes - count, lanes), jnp.float32)
    for n, ref in enumerate((after, before)):
        rows = jnp.concatenate([ref[...], fill], axis=0)
        packed = lax.dot_general(
            select[...], rows, (((1,), (1,)), ((), ())), precision=HIGHEST, preferred_element_type=jnp.float32
        )
        at = width + n * lanes
        first[:, at : at + lanes] = packed[:HALO]
        last[:, at : at + lanes] = packed[HALO:]


def shift(value, amount, axis):
    return pltpu.roll(value, (-amount) % value.shape[axis], axis)


def slopes(value, axis, even):
    ahead, ahead2 = shift(value, 1, axis), shift(value, 2, axis)
    back, back2 = shift(value, -1, axis), shift(value, -2, axis)
    right = jnp.where(even, 4.0 * ahead - 3.0 * value - ahead2, ahead - back)
    left = 3.0 * value - 4.0 * back + back2
    return right, left, jnp.where(even, right + left, right)


def spread(right, left, axis, even):
    ahead = jnp.where(even, -4.0 * left, -right)
    back = jnp.where(even, 4.0 * right, right)
    ahead = ahead + shift(jnp.where(even, left, 0.0), 1, axis)
    back = back - shift(jnp.where(even, right, 0.0), -1, axis)
    own = jnp.where(even, 3.0 * (left - right), 0.0)
    return own + shift(ahead, 1, axis) + shift(back, -1, axis)


def slopes_z(layers):
    a, b, c = layers
    return 4.0 * b - 3.0 * a - c, c - a, a - 4.0 * b + 3.0 * c


def spread_z(layers):
    a, b, c = layers
    return c - b - 3.0 * a, 4.0 * (a - c), b - a + 3.0 * c


def step_kernel(
    omega, phase, disp, prev, moduli, density, bins, before, after, east, west, select,
    updated, middle, operand, field, coef, strip, mid,
):
    rows, width = disp.shape[1], disp.shape[2]
    tall, wide = rows + EDGE, 2 * width
    halo_at = east.shape[1] - 2 * width
    both = jnp.concatenate([east[...], west[...]], axis=0)
    strip[...] = lax.dot_general(
        both, select[...], (((0,), (0,)), ((), ())), precision=HIGHEST, preferred_element_type=jnp.float32
    )
    start = 0
    for ref in (disp, prev, moduli, density):
        for i in range(ref.shape[0]):
            n = start + i
            field[n, :rows, :width] = ref[i]
            field[n, rows : rows + HALO, :width] = after[n * HALO : (n + 1) * HALO, :]
            field[n, rows + HALO :, :width] = before[n * HALO : (n + 1) * HALO, :]
            field[n, :rows, width:] = strip[n * rows : (n + 1) * rows, :]
            field[n, rows : rows + HALO, width:] = strip[halo_at + n * HALO : halo_at + (n + 1) * HALO, :]
            field[n, rows + HALO :, width:] = strip[
                halo_at + width + n * HALO : halo_at + width + (n + 1) * HALO, :
            ]
        start += ref.shape[0]

    row = lax.broadcasted_iota(jnp.int32, (tall, wide), 0)
    lane = lax.broadcasted_iota(jnp.int32, (tall, wide), 1)
    even_x = row % 2 == 0
    even_y = lane % 2 == 0
    two_x = jnp.where(even_x, 2.0, 1.0)
    two_y = jnp.where(even_y, 2.0, 1.0)
    weight = jnp.where(even_x, 1.0 / 3.0, 4.0 / 3.0) * jnp.where(even_y, 1.0 / 3.0, 4.0 / 3.0) / 8.0
    unused = (lane >= width + HALO) & (lane < wide - HALO)
    for layer in range(3):
        weight_z = 4.0 / 3.0 if layer == 1 else 1.0 / 3.0
        here = weight * weight_z
        lam = field[18 + layer] * here
        mu = field[21 + layer] * here
        mu_x, mu_y = mu * two_x, mu * two_y
        mu_xy = mu_x * two_y
        lam_x, lam_y = lam * two_x, lam * two_y
        mass = jnp.where(unused, 1.0, field[24 + layer]) * (here * two_x * two_y)
        for n, value in enumerate(
            (lam, lam_x, lam_y, lam_x + 2.0 * mu_x, lam_y + 2.0 * mu_y, lam_x * two_y + 2.0 * mu_xy,
             mu, mu_x, mu_y, mu_xy, time_step * time_step / mass)
        ):
            coef[layer, n] = value

    def advance(source, older, store):
        forces = [[None] * 3 for _ in range(3)]
        z_terms = [[None] * 3 for _ in range(3)]
        for layer in range(3):
            value = [source(c * 3 + layer) for c in range(3)]
            grad_z = []
            for c in range(3):
                a, b, d = (source(c * 3 + n) for n in range(3))
                if layer == 0:
                    grad_z.append(4.0 * b - 3.0 * a - d)
                elif layer == 1:
                    grad_z.append(d - a)
                else:
                    grad_z.append(a - 4.0 * b + 3.0 * d)
            lam, lam_x, lam_y, stiff_x, stiff_y, stiff_z, mu, mu_x, mu_y, mu_xy = (
                coef[layer, n] for n in range(10)
            )
            rx, lx, sx = zip(*(slopes(v, 0, even_x) for v in value))
            ry, ly, sy = zip(*(slopes(v, 1, even_y) for v in value))
            common = lam_y * grad_z[2] + lam * sy[1]
            force_x = spread(stiff_y * rx[0] + common, stiff_y * lx[0] + common, 0, even_x)
            common = mu * sx[1]
            force_x += spread(mu_x * ry[0] + common, mu_x * ly[0] + common, 1, even_y)
            common = mu * sy[0]
            force_y = spread(mu_y * rx[1] + common, mu_y * lx[1] + common, 0, even_x)
            common = lam_x * grad_z[2] + lam * sx[0]
            force_y += spread(stiff_x * ry[1] + common, stiff_x * ly[1] + common, 1, even_y)
            force_z = spread(mu_y * (rx[2] + grad_z[0]), mu_y * (lx[2] + grad_z[0]), 0, even_x)
            force_z += spread(mu_x * (ry[2] + grad_z[1]), mu_x * (ly[2] + grad_z[1]), 1, even_y)
            for c, value in enumerate((force_x, force_y, force_z)):
                forces[c][layer] = value
            z_terms[0][layer] = mu_xy * grad_z[0] + mu_y * sx[2]
            z_terms[1][layer] = mu_xy * grad_z[1] + mu_x * sy[2]
            z_terms[2][layer] = lam_y * sx[0] + lam_x * sy[1] + stiff_z * grad_z[2]
        for c in range(3):
            along_z = spread_z(z_terms[c])
            for layer in range(3):
                n = c * 3 + layer
                total = (forces[c][layer] + along_z[layer]) * coef[layer, 10]
                store(n, 2.0 * source(n) - older(n) - total)

    def keep_middle(n, value):
        mid[n] = value
        middle[n] = value[:rows, :width]

    def keep_updated(n, value):
        updated[n] = value[:rows, :width]

    advance(lambda n: field[n], lambda n: field[9 + n], keep_middle)
    advance(lambda n: mid[n], lambda n: field[n], keep_updated)

    slot = lax.broadcasted_iota(jnp.int32, (8, width), 0)
    angles = jnp.zeros((8, width), jnp.float32)
    for s in range(2):
        for b in range(2):
            angles = jnp.where(slot == 2 * s + b, phase[b] + (s + 1.0) * omega[b], angles)
    cosines, sines = jnp.cos(angles), jnp.sin(angles)
    low = lax.broadcasted_iota(jnp.int32, (rows, width), 1) < width // 2
    half = width // 2
    for b in range(2):
        for c in range(3):
            one, two = middle[c * 3 + 2], updated[c * 3 + 2]
            item = b * 3 + c
            real = bins[2 * item] + cosines[b : b + 1] * one + cosines[2 + b : 3 + b] * two
            imag = bins[2 * item + 1] - sines[b : b + 1] * one - sines[2 + b : 3 + b] * two
            if item < 4:
                operand[pl.ds(3 * item * rows, rows, stride=3), :] = real
                operand[pl.ds(3 * item * rows + 1, rows, stride=3), :] = imag
            else:
                at = 3 * (item - 4) * rows + 2
                operand[pl.ds(at, rows, stride=3), :] = jnp.where(low, real, pltpu.roll(imag, half, 1))
                operand[pl.ds(at + 6 * rows, rows, stride=3), :] = jnp.where(
                    low, pltpu.roll(real, half, 1), imag
                )


def first_transform_kernel(received, cosine, sine, out):
    count = cosine.shape[0]
    width = received.shape[1]
    parts = [received[pl.ds(n, count, stride=3), :] for n in range(3)]
    joined = jnp.concatenate(parts, axis=1)
    by_cos = jnp.dot(cosine[...], joined, precision=HIGHEST, preferred_element_type=jnp.float32)
    by_sin = jnp.dot(sine[...], joined, precision=HIGHEST, preferred_element_type=jnp.float32)
    out[pl.ds(0, count, stride=3), :] = by_cos[:, :width] + by_sin[:, width : 2 * width]
    out[pl.ds(1, count, stride=3), :] = by_cos[:, width : 2 * width] - by_sin[:, :width]
    turned = pltpu.roll(by_sin[:, 2 * width :], width // 2, 1)
    low = lax.broadcasted_iota(jnp.int32, turned.shape, 1) < width // 2
    out[pl.ds(2, count, stride=3), :] = by_cos[:, 2 * width :] + jnp.where(low, turned, -turned)


def second_transform_kernel(position, received, straight, turned, out):
    items, parts, rows, width = out.shape
    half = width // 2
    count = received.shape[0] // 3
    low = lax.broadcasted_iota(jnp.int32, (rows, width), 1) < half
    real, imag = [], []
    for item in range(items):
        if item < 4:
            real.append(received[pl.ds(3 * item * rows, rows, stride=3), :])
            imag.append(received[pl.ds(3 * item * rows + 1, rows, stride=3), :])
        else:
            at = 3 * (item - 4) * rows + 2
            one = received[pl.ds(at, rows, stride=3), :]
            two = received[pl.ds(at + 6 * rows, rows, stride=3), :]
            real.append(jnp.where(low, one, pltpu.roll(two, half, 1)))
            imag.append(jnp.where(low, pltpu.roll(one, half, 1), two))
    joined = jnp.concatenate([jnp.concatenate(real, axis=1), jnp.concatenate(imag, axis=1)], axis=0)
    node = lax.broadcasted_iota(jnp.int32, straight.shape, 1) % rows
    angle = (node * position[0]).astype(jnp.float32) * (2.0 * np.pi / (rows * count))
    matrix = straight[...] * jnp.cos(angle) + turned[...] * jnp.sin(angle)
    waves = jnp.dot(matrix, joined, precision=HIGHEST, preferred_element_type=jnp.float32)
    for item in range(items):
        for part in range(parts):
            out[item, part] = waves[part * rows : (part + 1) * rows, item * width : (item + 1) * width]


def exchange(value):
    peers = lax.axis_size("gx")
    rows, width = value.shape
    shaped = value.reshape(peers, 1, rows // peers * width)
    return lax.all_to_all(shaped, "gx", split_axis=0, concat_axis=0, tiled=True).reshape(rows, width)


def both_ways(forward, backward, axis):
    peers = lax.axis_size(axis)
    up = [(i, (i + 1) % peers) for i in range(peers)]
    down = [(j, i) for i, j in up]
    return lax.ppermute(forward, axis, up), lax.ppermute(backward, axis, down)


def f32(*shape):
    return jax.ShapeDtypeStruct(shape, jnp.float32)


def on_device(displacement, previous, moduli, density, bins, omega, phase):
    groups = lax.axis_size("gx")
    rows, width = density.shape[1:]
    items = bins.shape[0] * bins.shape[1]
    block = (rows, width)
    arrays = [a.reshape((-1,) + block) for a in (displacement, previous, moduli, density)]
    planes = sum(a.shape[0] for a in arrays)
    packed = -(-planes * rows // width) * width
    total = packed + 2 * width
    select = jnp.asarray(edge_columns(width))
    vmem = pl.BlockSpec(memory_space=pltpu.VMEM)
    smem = pl.BlockSpec(memory_space=pltpu.SMEM)
    params = pltpu.CompilerParams(vmem_limit_bytes=48 * 1024 * 1024)

    up, down, main = pl.pallas_call(
        pack_rows_kernel,
        out_shape=(f32(planes * HALO, width), f32(planes * HALO, width), f32(EDGE, packed)),
        in_specs=[vmem] * 5,
        out_specs=(vmem,) * 3,
        compiler_params=params,
    )(*arrays, select)
    before, after = both_ways(up, down, "gx")
    first, last = pl.pallas_call(
        pack_columns_kernel,
        out_shape=(f32(HALO, total), f32(HALO, total)),
        in_specs=[vmem] * 4,
        out_specs=(vmem,) * 2,
        compiler_params=params,
    )(main, before, after, select)
    west, east = both_ways(last, first, "gy")
    tall, wide = rows + EDGE, 2 * width
    updated, middle, operand = pl.pallas_call(
        step_kernel,
        out_shape=(f32(9, *block), f32(9, *block), f32(3 * groups, width)),
        in_specs=[smem] * 2 + [vmem] * 10,
        out_specs=(vmem,) * 3,
        scratch_shapes=[
            pltpu.VMEM((planes, tall, wide), jnp.float32),
            pltpu.VMEM((3, 11, tall, wide), jnp.float32),
            pltpu.VMEM((total, width), jnp.float32),
            pltpu.VMEM((9, tall, wide), jnp.float32),
        ],
        compiler_params=params,
    )(omega, phase, *arrays, bins.reshape((-1,) + block), before, after, east, west, select)

    cosine, sine = (jnp.asarray(t, jnp.float32) for t in fourier_tables(groups))
    sections = pl.pallas_call(
        first_transform_kernel,
        out_shape=f32(3 * groups, width),
        in_specs=[vmem] * 3,
        out_specs=vmem,
        compiler_params=params,
    )(exchange(operand), cosine, sine)
    scale = (groups * rows) ** -0.5
    c, s = (t * scale for t in fourier_tables(rows))
    straight = jnp.asarray(np.block([[c, s], [-s, c]]), jnp.float32)
    turned = jnp.asarray(np.block([[-s, c], [-c, -s]]), jnp.float32)
    position = lax.axis_index("gx").astype(jnp.int32).reshape(1)
    spectrum = pl.pallas_call(
        second_transform_kernel,
        out_shape=f32(items, 2, *block),
        in_specs=[smem] + [vmem] * 3,
        out_specs=vmem,
        compiler_params=params,
    )(position, exchange(sections), straight, turned)
    return (
        updated.reshape(displacement.shape),
        middle.reshape(displacement.shape),
        spectrum.reshape(bins.shape),
    )


def solution(mesh):
    placed = (
        P(None, None, "gx", "gy"),
        P(None, None, "gx", "gy"),
        P(None, None, "gx", "gy"),
        P(None, "gx", "gy"),
        P(None, None, None, "gx", "gy"),
        P(),
        P(),
    )
    return jax.shard_map(
        on_device,
        mesh=mesh,
        in_specs=placed,
        out_specs=(
            P(None, None, "gx", "gy"),
            P(None, None, "gx", "gy"),
            P(None, None, None, "gx", "gy"),
        ),
        check_vma=False,
    )
```

profile of v0, /device:TPU:1, one launch (start us, length us, event | category | flops | bytes accessed | tf_op | source)
XLA Modules:
  0.0 82.5 jit_solution(9183137805574768814)
XLA Ops:
  0.6 0.0 copy-start.9
  0.6 0.7 copy-done.9
  1.3 0.0 copy-start
  1.3 0.9 %copy-done = f32[3,3,32,128]{3,2,1,0:T(8,128)S(1)} copy-done((f32[3,3,32,128]{3,2,1,0:T(8,128)S(1)}, f32[3,3,32,128]{3,2,1,0:T(8,128)}, u32[]{:S(2)}) %copy-start) | copy-done | bytes 147480
  2.2 0.0 copy-start.2
  2.2 0.9 %copy-done.2 = f32[3,3,32,128]{3,2,1,0:T(8,128)S(1)} copy-done((f32[3,3,32,128]{3,2,1,0:T(8,128)S(1)}, f32[3,3,32,128]{3,2,1,0:T(8,128)}, u32[]{:S(2)}) %copy-start.2) | copy-done | bytes 147480
  3.1 0.0 copy-start.4
  3.1 0.9 %copy-done.4 = f32[2,3,32,128]{3,2,1,0:T(8,128)S(1)} copy-done((f32[2,3,32,128]{3,2,1,0:T(8,128)S(1)}, f32[2,3,32,128]{3,2,1,0:T(8,128)}, u32[]{:S(2)}) %copy-start.4) | copy-done | bytes 98328
  4.0 0.0 copy-start.5
  4.0 0.8 copy-done.5
  4.8 0.0 copy-start.3
  4.8 0.0 copy-start.6
  4.8 0.6 shard_map.139
  5.5 0.0 copy-start.1
  5.5 4.7 %collective-permute-start = (f32[108,128]{1,0:T(8,128)S(1)}, f32[108,128]{1,0:T(8,128)S(1)}, u32[]{:S(2)}, u32[]{:S(2)}) collective-permute-start(f32[108,128]{1,0:T(8,128)S(1)} %get-tuple-element.11), channel_id=1, source_target_pairs={{0,4},{4,8},{8,12},{12,16},{16,20},{20,24},{24,28},{28,32},{32,36}... | collective-permute-start | bytes 165896 | tf_op jit(solution)/shard_map/ppermute | solution.py:272
  10.2 6.1 %collective-permute-start.1 = (f32[108,128]{1,0:T(8,128)S(1)}, f32[108,128]{1,0:T(8,128)S(1)}, u32[]{:S(2)}, u32[]{:S(2)}) collective-permute-start(f32[108,128]{1,0:T(8,128)S(1)} %get-tuple-element.12), channel_id=1, source_target_pairs={{4,0},{8,4},{12,8},{16,12},{20,16},{24,20},{28,24},{32,28},{36,32}... | collective-permute-start | bytes 165896 | tf_op jit(solution)/shard_map/ppermute | solution.py:272
  16.4 0.0 collective-permute-done.before
  16.4 0.9 %collective-permute-done.1.after = f32[108,128]{1,0:T(8,128)S(1)} collective-permute-done((f32[108,128]{1,0:T(8,128)S(1)}, f32[108,128]{1,0:T(8,128)S(1)}, u32[]{:S(2)}, u32[]{:S(2)}) %collective-permute-start.1) | collective-permute-done | bytes 55328 | tf_op jit(solution)/shard_map/ppermute | solution.py:272
  17.2 0.3 shard_map.140
  17.5 3.5 %collective-permute-start.2 = (f32[4,1152]{1,0:T(4,128)S(1)}, f32[4,1152]{1,0:T(4,128)S(1)}, u32[]{:S(2)}, u32[]{:S(2)}) collective-permute-start(f32[4,1152]{1,0:T(4,128)S(1)} %get-tuple-element.14), channel_id=1, source_target_pairs={{1,0},{2,1},{3,2},{0,3},{5,4},{6,5},{7,6},{4,7},{9,8},{10,9},{11,1... | collective-permute-start | bytes 55304 | tf_op jit(solution)/shard_map/ppermute | solution.py:272
  21.0 0.0 copy-start.12
  21.0 0.0 copy-start.13
  21.0 2.7 %collective-permute-start.3 = (f32[4,1152]{1,0:T(4,128)S(1)}, f32[4,1152]{1,0:T(4,128)S(1)}, u32[]{:S(2)}, u32[]{:S(2)}) collective-permute-start(f32[4,1152]{1,0:T(4,128)S(1)} %get-tuple-element.15), channel_id=1, source_target_pairs={{0,1},{1,2},{2,3},{3,0},{4,5},{5,6},{6,7},{7,4},{8,9},{9,10},{10,1... | collective-permute-start | bytes 55304 | tf_op jit(solution)/shard_map/ppermute | solution.py:272
  23.7 0.0 collective-permute-done.2.east
  23.7 3.9 %collective-permute-done.3.west = f32[4,1152]{1,0:T(4,128)S(1)} collective-permute-done((f32[4,1152]{1,0:T(4,128)S(1)}, f32[4,1152]{1,0:T(4,128)S(1)}, u32[]{:S(2)}, u32[]{:S(2)}) %collective-permute-start.3) | collective-permute-done | bytes 18464 | tf_op jit(solution)/shard_map/ppermute | solution.py:272
  27.7 0.0 copy-done.3
  27.7 0.0 copy-done.6
  27.7 0.0 copy-done.1
  27.7 0.0 copy-done.12
  27.7 0.0 copy-done.13
  27.7 4.4 %shard_map.141 = (f32[9,32,128]{2,1,0:T(8,128)}, f32[9,32,128]{2,1,0:T(8,128)}, f32[384,128]{1,0:T(8,128)S(1)}) custom-call(f32[2]{0:T(128)S(1)} %copy-done.12, f32[2]{0:T(128)S(1)} %copy-done.13, f32[9,32,128]{2,1,0:T(8,128)S(1)} %bitcast.15, f32[9,32,128]{2,1,0:T(8,128)S(1)} %bitcast.17, f32[6,32,128]{2,1,0:T(8,128)S(1)} %bitcast.19, ...), custom_call_target="tpu_custom_call" | custom-call | tf_op jit(solution)/shard_map/pallas_call | solution.py:310
  32.1 0.0 copy-start.7
  32.1 0.0 copy-start.8
  32.1 29.5 %all_to_all.10 = f32[128,1,384]{2,1,0:T(1,128)S(1)} all-to-all(f32[128,1,384]{2,1,0:T(1,128)S(1)} %bitcast.20), channel_id=1, replica_groups=mesh['gx'=128,'gy'=4] {'gx'}, dimensions={0} | all-to-all | bytes 393216 | tf_op jit(solution)/shard_map/all_to_all | solution.py:265
  61.6 0.0 copy-done.7
  61.6 0.0 copy-done.8
  61.6 1.2 %shard_map.142 = f32[384,128]{1,0:T(8,128)} custom-call(f32[384,128]{1,0:T(8,128)S(1)} %bitcast.13, f32[128,128]{1,0:T(8,128)S(1)} %copy-done.7, f32[128,128]{1,0:T(8,128)S(1)} %copy-done.8), custom_call_target="tpu_custom_call" | custom-call | tf_op jit(solution)/shard_map/pallas_call | solution.py:325
  62.8 0.0 copy-start.10
  62.8 0.0 copy-start.11
  62.8 6.4 %all-to-all-start.1 = ((f32[128,1,384]{2,1,0:T(1,128)}), f32[128,1,384]{2,1,0:T(1,128)S(1)}, u32[]{:S(2)}, u32[]{:S(2)}) async-start(f32[128,1,384]{2,1,0:T(1,128)} %bitcast.9), calls=%async_computation.1 | async-start | bytes 393216 | tf_op jit(solution)/shard_map/all_to_all | solution.py:265
  69.2 12.2 %all-to-all-done.1 = f32[128,1,384]{2,1,0:T(1,128)S(1)} async-done(((f32[128,1,384]{2,1,0:T(1,128)}), f32[128,1,384]{2,1,0:T(1,128)S(1)}, u32[]{:S(2)}, u32[]{:S(2)}) %all-to-all-start.1) | async-done | bytes 196640 | tf_op jit(solution)/shard_map/all_to_all | solution.py:265
  81.4 0.0 copy-done.10
  81.4 0.0 copy-done.11
  81.4 1.0 %shard_map.143 = f32[6,2,32,128]{3,2,1,0:T(8,128)} custom-call(s32[1]{0:T(128)} %bitcast.6.position, f32[384,128]{1,0:T(8,128)S(1)} %bitcast.12, f32[64,64]{1,0:T(8,128)S(1)} %copy-done.10, f32[64,64]{1,0:T(8,128)S(1)} %copy-done.11), custom_call_target="tpu_custom_call" | custom-call | tf_op jit(solution)/shard_map/pallas_call | solution.py:337
Async XLA Ops:
  0.6 0.7 copy-start.9
  1.3 0.9 %copy-start = (f32[3,3,32,128]{3,2,1,0:T(8,128)S(1)}, f32[3,3,32,128]{3,2,1,0:T(8,128)}, u32[]{:S(2)}) copy-start(f32[3,3,32,128]{3,2,1,0:T(8,128)} %param.12) | copy-start | bytes 442372
  2.2 0.9 %copy-start.2 = (f32[3,3,32,128]{3,2,1,0:T(8,128)S(1)}, f32[3,3,32,128]{3,2,1,0:T(8,128)}, u32[]{:S(2)}) copy-start(f32[3,3,32,128]{3,2,1,0:T(8,128)} %param.13) | copy-start | bytes 442372
  3.1 0.9 %copy-start.4 = (f32[2,3,32,128]{3,2,1,0:T(8,128)S(1)}, f32[2,3,32,128]{3,2,1,0:T(8,128)}, u32[]{:S(2)}) copy-start(f32[2,3,32,128]{3,2,1,0:T(8,128)} %param.14) | copy-start | bytes 294916
  4.0 0.8 copy-start.5
  4.8 22.8 %copy-start.3 = (f32[3,3,32,128]{3,2,1,0:T(8,128)S(1)}, f32[3,3,32,128]{3,2,1,0:T(8,128)}, u32[]{:S(2)}) copy-start(f32[3,3,32,128]{3,2,1,0:T(8,128)} %param.13) | copy-start | bytes 442372
  4.8 22.8 %copy-start.6 = (f32[2,3,2,32,128]{4,3,2,1,0:T(8,128)S(1)}, f32[2,3,2,32,128]{4,3,2,1,0:T(8,128)}, u32[]{:S(2)}) copy-start(f32[2,3,2,32,128]{4,3,2,1,0:T(8,128)} %param.16) | copy-start | bytes 589828
  5.5 22.2 %copy-start.1 = (f32[3,3,32,128]{3,2,1,0:T(8,128)S(1)}, f32[3,3,32,128]{3,2,1,0:T(8,128)}, u32[]{:S(2)}) copy-start(f32[3,3,32,128]{3,2,1,0:T(8,128)} %param.12) | copy-start | bytes 442372
  5.5 10.9 %collective-permute-start = (f32[108,128]{1,0:T(8,128)S(1)}, f32[108,128]{1,0:T(8,128)S(1)}, u32[]{:S(2)}, u32[]{:S(2)}) collective-permute-start(f32[108,128]{1,0:T(8,128)S(1)} %get-tuple-element.11), channel_id=1, source_target_pairs={{0,4},{4,8},{8,12},{12,16},{16,20},{20,24},{24,28},{28,32},{32,36}... | collective-permute-start | bytes 165896 | tf_op jit(solution)/shard_map/ppermute | solution.py:272
  10.2 7.0 %collective-permute-start.1 = (f32[108,128]{1,0:T(8,128)S(1)}, f32[108,128]{1,0:T(8,128)S(1)}, u32[]{:S(2)}, u32[]{:S(2)}) collective-permute-start(f32[108,128]{1,0:T(8,128)S(1)} %get-tuple-element.12), channel_id=1, source_target_pairs={{4,0},{8,4},{12,8},{16,12},{20,16},{24,20},{28,24},{32,28},{36,32}... | collective-permute-start | bytes 165896 | tf_op jit(solution)/shard_map/ppermute | solution.py:272
  17.5 6.2 %collective-permute-start.2 = (f32[4,1152]{1,0:T(4,128)S(1)}, f32[4,1152]{1,0:T(4,128)S(1)}, u32[]{:S(2)}, u32[]{:S(2)}) collective-permute-start(f32[4,1152]{1,0:T(4,128)S(1)} %get-tuple-element.14), channel_id=1, source_target_pairs={{1,0},{2,1},{3,2},{0,3},{5,4},{6,5},{7,6},{4,7},{9,8},{10,9},{11,1... | collective-permute-start | bytes 55304 | tf_op jit(solution)/shard_map/ppermute | solution.py:272
  21.0 6.7 %copy-start.12 = (f32[2]{0:T(128)S(1)}, f32[2]{0:T(128)}, u32[]{:S(2)}) copy-start(f32[2]{0:T(128)} %omega.1) | copy-start | bytes 28
  21.0 6.7 %copy-start.13 = (f32[2]{0:T(128)S(1)}, f32[2]{0:T(128)}, u32[]{:S(2)}) copy-start(f32[2]{0:T(128)} %phase.1) | copy-start | bytes 28
  21.0 6.6 %collective-permute-start.3 = (f32[4,1152]{1,0:T(4,128)S(1)}, f32[4,1152]{1,0:T(4,128)S(1)}, u32[]{:S(2)}, u32[]{:S(2)}) collective-permute-start(f32[4,1152]{1,0:T(4,128)S(1)} %get-tuple-element.15), channel_id=1, source_target_pairs={{0,1},{1,2},{2,3},{3,0},{4,5},{5,6},{6,7},{7,4},{8,9},{9,10},{10,1... | collective-permute-start | bytes 55304 | tf_op jit(solution)/shard_map/ppermute | solution.py:272
  32.1 29.5 %copy-start.7 = (f32[128,128]{1,0:T(8,128)S(1)}, f32[128,128]{1,0:T(8,128)}, u32[]{:S(2)}) copy-start(f32[128,128]{1,0:T(8,128)} %constant.17.clone.cosine) | copy-start | bytes 196612
  32.1 29.5 %copy-start.8 = (f32[128,128]{1,0:T(8,128)S(1)}, f32[128,128]{1,0:T(8,128)}, u32[]{:S(2)}) copy-start(f32[128,128]{1,0:T(8,128)} %constant.18.clone.sine) | copy-start | bytes 196612
  62.8 18.6 %copy-start.10 = (f32[64,64]{1,0:T(8,128)S(1)}, f32[64,64]{1,0:T(8,128)}, u32[]{:S(2)}) copy-start(f32[64,64]{1,0:T(8,128)} %constant.19.clone.straight) | copy-start | bytes 49156
  62.8 18.6 %copy-start.11 = (f32[64,64]{1,0:T(8,128)S(1)}, f32[64,64]{1,0:T(8,128)}, u32[]{:S(2)}) copy-start(f32[64,64]{1,0:T(8,128)} %constant.20.clone.turned) | copy-start | bytes 49156
  62.8 18.6 %all-to-all-start.1 = ((f32[128,1,384]{2,1,0:T(1,128)}), f32[128,1,384]{2,1,0:T(1,128)S(1)}, u32[]{:S(2)}, u32[]{:S(2)}) async-start(f32[128,1,384]{2,1,0:T(1,128)} %bitcast.9), calls=%async_computation.1 | async-start | bytes 393216 | tf_op jit(solution)/shard_map/all_to_all | solution.py:265
where the time goes:
time: 83 us; the launch traced here: 82.5 us
  blocking collectives  29.5 us (36%)
  starting transfers between devices  23.4 us (28%)
  waiting for transfers between devices  17 us (20%)
  Pallas kernels  7.59 us (9%)
  local copies, waits for them, and re-layouts  4.23 us (5%)
    all_to_all x1, blocking collectives, exchange(): lax.all_to_all(shaped, 'gx', split_axis=0, concat_axis=0, tiled=True)  29.5 us
    ppermute x4, starting transfers between devices, both_ways(): return (lax.ppermute(forward, axis, up), lax.ppermute(backward, axis, down))  17 us
    all_to_all x1, waiting for transfers between devices, exchange(): lax.all_to_all(shaped, 'gx', split_axis=0, concat_axis=0, tiled=True)  12.2 us
    all_to_all x1, starting transfers between devices, exchange(): lax.all_to_all(shaped, 'gx', split_axis=0, concat_axis=0, tiled=True)  6.35 us
    ppermute x4, waiting for transfers between devices, both_ways(): return (lax.ppermute(forward, axis, up), lax.ppermute(backward, axis, down))  4.79 us
    pallas_call x1, Pallas kernels, on_device(): pl.pallas_call(step_kernel, out_shape=(f32(9, *block), f32(9, *block), f3...  4.41 us
    unnamed x28, local copies, waits for them, and re-layouts  4.23 us
  transfers between devices with their start and end apart: 5, of which 3 were waited for; matrix products, arithmetic and copies ran while one was open for 0% of the time, Pallas kernels for 0%

commit v1 on v0

--- a/solution.py
+++ b/solution.py
@@ -1,7 +1,6 @@
-import functools
-
 import jax
 import jax.numpy as jnp
+import ml_dtypes
 import numpy as np
 from jax import lax
 from jax.experimental import pallas as pl
@@ -11,7 +10,6 @@
 time_step = 0.03
 HALO = 4
 EDGE = 8
-HIGHEST = lax.Precision.HIGHEST
 
 
 def edge_columns(width):
@@ -28,21 +26,45 @@
     return np.cos(angle), np.sin(angle)
 
 
-def pack_rows_kernel(disp, prev, moduli, density, select, up, down, main):
+def halves(value):
+    high = value.astype(jnp.bfloat16)
+    return high, (value - high.astype(jnp.float32)).astype(jnp.bfloat16)
+
+
+def pick_columns(select, rows):
+    chosen = select[...].astype(jnp.bfloat16)
+    return lax.dot_general(
+        jnp.concatenate([chosen, chosen], axis=1),
+        jnp.concatenate(halves(rows), axis=1),
+        (((1,), (1,)), ((), ())),
+        preferred_element_type=jnp.float32,
+    )
+
+
+def pack_rows_kernel(disp, prev, moduli, density, up, down, low, high, sems):
+    copies = []
     start = 0
-    for ref in (disp, prev, moduli, density):
-        planes, rows, width = ref.shape
-        for i in range(planes):
-            at = (start + i) * HALO
-            up[at : at + HALO, :] = ref[i, rows - HALO : rows, :]
-            down[at : at + HALO, :] = ref[i, :HALO, :]
-        flat = ref[...].reshape(planes * rows, width)
-        packed = lax.dot_general(
-            select[...], flat, (((1,), (1,)), ((), ())), precision=HIGHEST, preferred_element_type=jnp.float32
-        )
-        main[:, start * rows : (start + planes) * rows] = packed
+    for n, ref in enumerate((disp, prev, moduli, density)):
+        planes, rows, _ = ref.shape
+        here = pl.ds(start, planes)
+        copies.append(pltpu.make_async_copy(ref.at[:, pl.ds(0, 8), :], low.at[here], sems.at[2 * n]))
+        copies.append(pltpu.make_async_copy(ref.at[:, pl.ds(rows - 8, 8), :], high.at[here], sems.at[2 * n + 1]))
         start += planes
-    used = start * rows
+    for copy in copies:
+        copy.start()
+    for copy in copies:
+        copy.wait()
+    for i in range(start):
+        at = i * HALO
+        up[at : at + HALO, :] = high[i, 8 - HALO :, :]
+        down[at : at + HALO, :] = low[i, :HALO, :]
+
+
+def pack_main_kernel(disp, prev, moduli, density, select, main):
+    width = select.shape[1]
+    whole = jnp.concatenate([ref[...].reshape(-1, width) for ref in (disp, prev, moduli, density)], axis=0)
+    used = whole.shape[0]
+    main[:, :used] = pick_columns(select, whole)
     main[:, used:] = jnp.zeros((EDGE, main.shape[1] - used), jnp.float32)
 
 
@@ -51,16 +73,10 @@
     lanes = select.shape[1]
     first[:, :width] = main[:HALO, :]
     last[:, :width] = main[HALO:, :]
-    count = before.shape[0]
-    fill = jnp.zeros((lanes - count, lanes), jnp.float32)
-    for n, ref in enumerate((after, before)):
-        rows = jnp.concatenate([ref[...], fill], axis=0)
-        packed = lax.dot_general(
-            select[...], rows, (((1,), (1,)), ((), ())), precision=HIGHEST, preferred_element_type=jnp.float32
-        )
-        at = width + n * lanes
-        first[:, at : at + lanes] = packed[:HALO]
-        last[:, at : at + lanes] = packed[HALO:]
+    fill = jnp.zeros((lanes - before.shape[0], lanes), jnp.float32)
+    packed = pick_columns(select, jnp.concatenate([after[...], fill, before[...], fill], axis=0))
+    first[:, width:] = packed[:HALO]
+    last[:, width:] = packed[HALO:]
 
 
 def shift(value, amount, axis):
@@ -102,8 +118,12 @@
     tall, wide = rows + EDGE, 2 * width
     halo_at = east.shape[1] - 2 * width
     both = jnp.concatenate([east[...], west[...]], axis=0)
+    chosen = select[...].astype(jnp.bfloat16)
     strip[...] = lax.dot_general(
-        both, select[...], (((0,), (0,)), ((), ())), precision=HIGHEST, preferred_element_type=jnp.float32
+        jnp.concatenate(halves(both), axis=0),
+        jnp.concatenate([chosen, chosen], axis=0),
+        (((0,), (0,)), ((), ())),
+        preferred_element_type=jnp.float32,
     )
     start = 0
     for ref in (disp, prev, moduli, density):
@@ -119,13 +139,15 @@
             ]
         start += ref.shape[0]
 
-    row = lax.broadcasted_iota(jnp.int32, (tall, wide), 0)
+    def tiled(tile, shape=(tall, wide)):
+        line = jnp.concatenate([tile] * (shape[1] // tile.shape[1]), axis=1)
+        return jnp.concatenate([line] * (shape[0] // tile.shape[0]), axis=0)
+
+    tile_x, tile_y = (lax.broadcasted_iota(jnp.int32, (8, 128), axis) % 2 for axis in range(2))
+    near_x, near_y = tiled(tile_x), tiled(tile_y)
+    two_x, two_y = 2.0 - near_x.astype(jnp.float32), 2.0 - near_y.astype(jnp.float32)
+    weight = (1.0 / 3.0 + near_x.astype(jnp.float32)) * (1.0 / 3.0 + near_y.astype(jnp.float32)) / 8.0
     lane = lax.broadcasted_iota(jnp.int32, (tall, wide), 1)
-    even_x = row % 2 == 0
-    even_y = lane % 2 == 0
-    two_x = jnp.where(even_x, 2.0, 1.0)
-    two_y = jnp.where(even_y, 2.0, 1.0)
-    weight = jnp.where(even_x, 1.0 / 3.0, 4.0 / 3.0) * jnp.where(even_y, 1.0 / 3.0, 4.0 / 3.0) / 8.0
     unused = (lane >= width + HALO) & (lane < wide - HALO)
     for layer in range(3):
         weight_z = 4.0 / 3.0 if layer == 1 else 1.0 / 3.0
@@ -142,7 +164,26 @@
         ):
             coef[layer, n] = value
 
-    def advance(source, older, store):
+    def advance(source, older, store, own):
+        out_rows, out_width = (rows, width) if own else (tall, wide)
+        even_x, even_y = near_x == 0, near_y == 0
+        even_xs, even_ys = even_x[:, :out_width], even_y[:out_rows, :]
+
+        def for_x(value):
+            return value[:, :out_width]
+
+        def for_y(value):
+            return value[:out_rows, :]
+
+        def for_z(value):
+            return value[:out_rows, :out_width]
+
+        def along_x(right, left):
+            return spread(right, left, 0, even_xs)[:out_rows]
+
+        def along_y(right, left):
+            return spread(right, left, 1, even_ys)[:, :out_width]
+
         forces = [[None] * 3 for _ in range(3)]
         z_terms = [[None] * 3 for _ in range(3)]
         for layer in range(3):
@@ -161,37 +202,43 @@
             )
             rx, lx, sx = zip(*(slopes(v, 0, even_x) for v in value))
             ry, ly, sy = zip(*(slopes(v, 1, even_y) for v in value))
-            common = lam_y * grad_z[2] + lam * sy[1]
-            force_x = spread(stiff_y * rx[0] + common, stiff_y * lx[0] + common, 0, even_x)
-            common = mu * sx[1]
-            force_x += spread(mu_x * ry[0] + common, mu_x * ly[0] + common, 1, even_y)
-            common = mu * sy[0]
-            force_y = spread(mu_y * rx[1] + common, mu_y * lx[1] + common, 0, even_x)
-            common = lam_x * grad_z[2] + lam * sx[0]
-            force_y += spread(stiff_x * ry[1] + common, stiff_x * ly[1] + common, 1, even_y)
-            force_z = spread(mu_y * (rx[2] + grad_z[0]), mu_y * (lx[2] + grad_z[0]), 0, even_x)
-            force_z += spread(mu_x * (ry[2] + grad_z[1]), mu_x * (ly[2] + grad_z[1]), 1, even_y)
+            common = for_x(lam_y * grad_z[2] + lam * sy[1])
+            scale = for_x(stiff_y)
+            force_x = along_x(scale * for_x(rx[0]) + common, scale * for_x(lx[0]) + common)
+            common = for_x(mu * sy[0])
+            scale = for_x(mu_y)
+            force_y = along_x(scale * for_x(rx[1]) + common, scale * for_x(lx[1]) + common)
+            common = for_x(grad_z[0])
+            force_z = along_x(scale * (for_x(rx[2]) + common), scale * (for_x(lx[2]) + common))
+            common = for_y(lam_x * grad_z[2] + lam * sx[0])
+            scale = for_y(stiff_x)
+            force_y += along_y(scale * for_y(ry[1]) + common, scale * for_y(ly[1]) + common)
+            common = for_y(mu * sx[1])
+            scale = for_y(mu_x)
+            force_x += along_y(scale * for_y(ry[0]) + common, scale * for_y(ly[0]) + common)
+            common = for_y(grad_z[1])
+            force_z += along_y(scale * (for_y(ry[2]) + common), scale * (for_y(ly[2]) + common))
             for c, value in enumerate((force_x, force_y, force_z)):
                 forces[c][layer] = value
-            z_terms[0][layer] = mu_xy * grad_z[0] + mu_y * sx[2]
-            z_terms[1][layer] = mu_xy * grad_z[1] + mu_x * sy[2]
-            z_terms[2][layer] = lam_y * sx[0] + lam_x * sy[1] + stiff_z * grad_z[2]
+            z_terms[0][layer] = for_z(mu_xy * grad_z[0] + mu_y * sx[2])
+            z_terms[1][layer] = for_z(mu_xy * grad_z[1] + mu_x * sy[2])
+            z_terms[2][layer] = for_z(lam_y * sx[0] + lam_x * sy[1] + stiff_z * grad_z[2])
         for c in range(3):
             along_z = spread_z(z_terms[c])
             for layer in range(3):
                 n = c * 3 + layer
-                total = (forces[c][layer] + along_z[layer]) * coef[layer, 10]
-                store(n, 2.0 * source(n) - older(n) - total)
+                total = (forces[c][layer] + along_z[layer]) * for_z(coef[layer, 10])
+                store(n, 2.0 * for_z(source(n)) - for_z(older(n)) - total)
 
     def keep_middle(n, value):
         mid[n] = value
         middle[n] = value[:rows, :width]
 
     def keep_updated(n, value):
-        updated[n] = value[:rows, :width]
-
-    advance(lambda n: field[n], lambda n: field[9 + n], keep_middle)
-    advance(lambda n: mid[n], lambda n: field[n], keep_updated)
+        updated[n] = value
+
+    advance(lambda n: field[n], lambda n: field[9 + n], keep_middle, False)
+    advance(lambda n: mid[n], lambda n: field[n], keep_updated, True)
 
     slot = lax.broadcasted_iota(jnp.int32, (8, width), 0)
     angles = jnp.zeros((8, width), jnp.float32)
@@ -218,13 +265,14 @@
                 )
 
 
-def first_transform_kernel(received, cosine, sine, out):
-    count = cosine.shape[0]
-    width = received.shape[1]
-    parts = [received[pl.ds(n, count, stride=3), :] for n in range(3)]
-    joined = jnp.concatenate(parts, axis=1)
-    by_cos = jnp.dot(cosine[...], joined, precision=HIGHEST, preferred_element_type=jnp.float32)
-    by_sin = jnp.dot(sine[...], joined, precision=HIGHEST, preferred_element_type=jnp.float32)
+def first_transform_kernel(received, table, out):
+    count, width = received.shape[0] // 3, received.shape[1]
+    joined = jnp.concatenate([received[pl.ds(n, count, stride=3), :] for n in range(3)], axis=1)
+    high, rest = halves(joined)
+    both = jnp.dot(
+        table[...], jnp.concatenate([high, rest, high], axis=0), preferred_element_type=jnp.float32
+    )
+    by_cos, by_sin = both[:count], both[count:]
     out[pl.ds(0, count, stride=3), :] = by_cos[:, :width] + by_sin[:, width : 2 * width]
     out[pl.ds(1, count, stride=3), :] = by_cos[:, width : 2 * width] - by_sin[:, :width]
     turned = pltpu.roll(by_sin[:, 2 * width :], width // 2, 1)
@@ -252,7 +300,13 @@
     node = lax.broadcasted_iota(jnp.int32, straight.shape, 1) % rows
     angle = (node * position[0]).astype(jnp.float32) * (2.0 * np.pi / (rows * count))
     matrix = straight[...] * jnp.cos(angle) + turned[...] * jnp.sin(angle)
-    waves = jnp.dot(matrix, joined, precision=HIGHEST, preferred_element_type=jnp.float32)
+    left, left_rest = halves(matrix)
+    high, rest = halves(joined)
+    waves = jnp.dot(
+        jnp.concatenate([left, left, left_rest], axis=1),
+        jnp.concatenate([high, rest, high], axis=0),
+        preferred_element_type=jnp.float32,
+    )
     for item in range(items):
         for part in range(parts):
             out[item, part] = waves[part * rows : (part + 1) * rows, item * width : (item + 1) * width]
@@ -290,12 +344,26 @@
     smem = pl.BlockSpec(memory_space=pltpu.SMEM)
     params = pltpu.CompilerParams(vmem_limit_bytes=48 * 1024 * 1024)
 
-    up, down, main = pl.pallas_call(
+    hbm = pl.BlockSpec(memory_space=pltpu.HBM)
+    up, down = pl.pallas_call(
         pack_rows_kernel,
-        out_shape=(f32(planes * HALO, width), f32(planes * HALO, width), f32(EDGE, packed)),
+        out_shape=(f32(planes * HALO, width), f32(planes * HALO, width)),
+        in_specs=[hbm] * 4,
+        out_specs=(vmem,) * 2,
+        scratch_shapes=[
+            pltpu.VMEM((planes, 8, width), jnp.float32),
+            pltpu.VMEM((planes, 8, width), jnp.float32),
+            pltpu.SemaphoreType.DMA((8,)),
+        ],
+        compiler_params=pltpu.CompilerParams(vmem_limit_bytes=62 * 1024 * 1024),
+    )(*arrays)
+    main = pl.pallas_call(
+        pack_main_kernel,
+        out_shape=f32(EDGE, packed),
         in_specs=[vmem] * 5,
-        out_specs=(vmem,) * 3,
+        out_specs=vmem,
         compiler_params=params,
+        cost_estimate=pl.CostEstimate(flops=50_000_000, bytes_accessed=2_000_000, transcendentals=0),
     )(*arrays, select)
     before, after = both_ways(up, down, "gx")
     first, last = pl.pallas_call(
@@ -321,14 +389,17 @@
         compiler_params=params,
     )(omega, phase, *arrays, bins.reshape((-1,) + block), before, after, east, west, select)
 
-    cosine, sine = (jnp.asarray(t, jnp.float32) for t in fourier_tables(groups))
+    stacked = np.concatenate(fourier_tables(groups), axis=0)
+    high = stacked.astype(ml_dtypes.bfloat16)
+    rest = (stacked - high.astype(np.float64)).astype(ml_dtypes.bfloat16)
+    table = jnp.asarray(np.concatenate([high, high, rest], axis=1))
     sections = pl.pallas_call(
         first_transform_kernel,
         out_shape=f32(3 * groups, width),
-        in_specs=[vmem] * 3,
+        in_specs=[vmem] * 2,
         out_specs=vmem,
         compiler_params=params,
-    )(exchange(operand), cosine, sine)
+    )(exchange(operand), table)
     scale = (groups * rows) ** -0.5
     c, s = (t * scale for t in fourier_tables(rows))
     straight = jnp.asarray(np.block([[c, s], [-s, c]]), jnp.float32)

time: 83 us -> 79.3 us (0.955)
  local copies, waits for them, and re-layouts: 4.23 us -> 0.05 us
    unnamed x28 -> x22, local copies, waits for them, and re-layouts: 4.23 us -> 0.05 us
    pallas_call x1, Pallas kernels: 0.65 us -> 1.62 us  [on_device(): pl.pallas_call(pack_rows_kernel, out_shape=(f32(planes * HALO, width), f3...]
where the time goes in v1:
time: 79.3 us; the launch traced here: 78.9 us
  blocking collectives  29.5 us (37%)
  starting transfers between devices  23.4 us (30%)
  waiting for transfers between devices  17.1 us (22%)
  Pallas kernels  8.14 us (10%)
  between operations  0.81 us (1%)
    all_to_all x1, blocking collectives, exchange(): lax.all_to_all(shaped, 'gx', split_axis=0, concat_axis=0, tiled=True)  29.5 us
    ppermute x4, starting transfers between devices, both_ways(): return (lax.ppermute(forward, axis, up), lax.ppermute(backward, axis, down))  17 us
    all_to_all x1, waiting for transfers between devices, exchange(): lax.all_to_all(shaped, 'gx', split_axis=0, concat_axis=0, tiled=True)  12.2 us
    all_to_all x1, starting transfers between devices, exchange(): lax.all_to_all(shaped, 'gx', split_axis=0, concat_axis=0, tiled=True)  6.36 us
    ppermute x4, waiting for transfers between devices, both_ways(): return (lax.ppermute(forward, axis, up), lax.ppermute(backward, axis, down))  4.84 us
    pallas_call x1, Pallas kernels, on_device(): pl.pallas_call(step_kernel, out_shape=(f32(9, *block), f32(9, *block), f3...  4.16 us
    pallas_call x1, Pallas kernels, on_device(): pl.pallas_call(pack_rows_kernel, out_shape=(f32(planes * HALO, width), f3...  1.62 us
  transfers between devices with their start and end apart: 5, of which 3 were waited for; matrix products, arithmetic and copies ran while one was open for 0% of the time, Pallas kernels for 0%

profile of v1, /device:TPU:1, one launch (start us, length us, event | category | flops | bytes accessed | tf_op | source)
XLA Modules:
  0.0 78.9 jit_solution(10602319563802678665)
XLA Ops:
  0.6 0.0 copy-start.6
  0.6 0.0 copy-start
  0.7 0.0 copy-start.1
  0.7 0.0 copy-start.2
  0.7 0.0 copy-start.3
  0.7 1.6 %shard_map.130 = (f32[108,128]{1,0:T(8,128)}, f32[108,128]{1,0:T(8,128)}) custom-call(f32[9,32,128]{2,1,0:T(8,128)} %bitcast.12, f32[9,32,128]{2,1,0:T(8,128)} %bitcast.15, f32[6,32,128]{2,1,0:T(8,128)} %bitcast.18, f32[3,32,128]{2,1,0:T(8,128)} %density.5), custom_call_target="tpu_custom_call" | custom-call | tf_op jit(solution)/shard_map/pallas_call | solution.py:348
  2.3 4.6 %collective-permute-start = (f32[108,128]{1,0:T(8,128)}, f32[108,128]{1,0:T(8,128)S(1)}, u32[]{:S(2)}, u32[]{:S(2)}) collective-permute-start(f32[108,128]{1,0:T(8,128)} %get-tuple-element.10), channel_id=1, source_target_pairs={{0,4},{4,8},{8,12},{12,16},{16,20},{20,24},{24,28},{28,32},{32,36}... | collective-permute-start | bytes 165896 | tf_op jit(solution)/shard_map/ppermute | solution.py:326
  6.9 0.0 copy-start.4
  6.9 6.2 %collective-permute-start.1 = (f32[108,128]{1,0:T(8,128)}, f32[108,128]{1,0:T(8,128)S(1)}, u32[]{:S(2)}, u32[]{:S(2)}) collective-permute-start(f32[108,128]{1,0:T(8,128)} %get-tuple-element.11), channel_id=1, source_target_pairs={{4,0},{8,4},{12,8},{16,12},{20,16},{24,20},{28,24},{32,28},{36,32}... | collective-permute-start | bytes 165896 | tf_op jit(solution)/shard_map/ppermute | solution.py:326
  13.2 0.0 copy-done.6
  13.2 0.0 copy-done
  13.2 0.0 copy-done.1
  13.2 0.0 copy-done.2
  13.2 0.0 copy-done.3
  13.2 0.2 shard_map.131.main
  13.4 0.0 collective-permute-done.before
  13.5 0.8 %collective-permute-done.1.after = f32[108,128]{1,0:T(8,128)S(1)} collective-permute-done((f32[108,128]{1,0:T(8,128)}, f32[108,128]{1,0:T(8,128)S(1)}, u32[]{:S(2)}, u32[]{:S(2)}) %collective-permute-start.1) | collective-permute-done | bytes 55328 | tf_op jit(solution)/shard_map/ppermute | solution.py:326
  14.3 0.2 shard_map.132
  14.4 3.5 %collective-permute-start.2 = (f32[4,1152]{1,0:T(4,128)S(1)}, f32[4,1152]{1,0:T(4,128)S(1)}, u32[]{:S(2)}, u32[]{:S(2)}) collective-permute-start(f32[4,1152]{1,0:T(4,128)S(1)} %get-tuple-element.12), channel_id=1, source_target_pairs={{1,0},{2,1},{3,2},{0,3},{5,4},{6,5},{7,6},{4,7},{9,8},{10,9},{11,1... | collective-permute-start | bytes 55304 | tf_op jit(solution)/shard_map/ppermute | solution.py:326
  17.9 0.0 copy-start.9
  17.9 0.0 copy-start.10
  18.0 2.7 %collective-permute-start.3 = (f32[4,1152]{1,0:T(4,128)S(1)}, f32[4,1152]{1,0:T(4,128)S(1)}, u32[]{:S(2)}, u32[]{:S(2)}) collective-permute-start(f32[4,1152]{1,0:T(4,128)S(1)} %get-tuple-element.13), channel_id=1, source_target_pairs={{0,1},{1,2},{2,3},{3,0},{4,5},{5,6},{6,7},{7,4},{8,9},{9,10},{10,1... | collective-permute-start | bytes 55304 | tf_op jit(solution)/shard_map/ppermute | solution.py:326
  20.7 0.0 collective-permute-done.2.east
  20.7 4.0 %collective-permute-done.3.west = f32[4,1152]{1,0:T(4,128)S(1)} collective-permute-done((f32[4,1152]{1,0:T(4,128)S(1)}, f32[4,1152]{1,0:T(4,128)S(1)}, u32[]{:S(2)}, u32[]{:S(2)}) %collective-permute-start.3) | collective-permute-done | bytes 18464 | tf_op jit(solution)/shard_map/ppermute | solution.py:326
  24.7 0.0 copy-done.4
  24.7 0.0 copy-done.9
  24.7 0.0 copy-done.10
  24.7 4.2 %shard_map.133 = (f32[9,32,128]{2,1,0:T(8,128)}, f32[9,32,128]{2,1,0:T(8,128)}, f32[384,128]{1,0:T(8,128)S(1)}) custom-call(f32[2]{0:T(128)S(1)} %copy-done.9, f32[2]{0:T(128)S(1)} %copy-done.10, f32[9,32,128]{2,1,0:T(8,128)S(1)} %bitcast.14, f32[9,32,128]{2,1,0:T(8,128)S(1)} %bitcast.17, f32[6,32,128]{2,1,0:T(8,128)S(1)} %bitcast.20, ...), custom_call_target="tpu_custom_call" | custom-call | tf_op jit(solution)/shard_map/pallas_call | solution.py:378
  28.9 0.0 copy-start.5
  28.9 29.5 %all_to_all.10 = f32[128,1,384]{2,1,0:T(1,128)S(1)} all-to-all(f32[128,1,384]{2,1,0:T(1,128)S(1)} %bitcast.23), channel_id=1, replica_groups=mesh['gx'=128,'gy'=4] {'gx'}, dimensions={0} | all-to-all | bytes 393216 | tf_op jit(solution)/shard_map/all_to_all | solution.py:319
  58.4 0.0 copy-done.5
  58.4 1.0 %shard_map.134 = f32[384,128]{1,0:T(8,128)} custom-call(f32[384,128]{1,0:T(8,128)S(1)} %bitcast.22, bf16[256,384]{1,0:T(8,128)(2,1)S(1)} %copy-done.5), custom_call_target="tpu_custom_call" | custom-call | tf_op jit(solution)/shard_map/pallas_call | solution.py:396
  59.4 0.0 copy-start.7
  59.4 0.0 copy-start.8
  59.4 6.4 %all-to-all-start.1 = ((f32[128,1,384]{2,1,0:T(1,128)}), f32[128,1,384]{2,1,0:T(1,128)S(1)}, u32[]{:S(2)}, u32[]{:S(2)}) async-start(f32[128,1,384]{2,1,0:T(1,128)} %bitcast.9), calls=%async_computation.1 | async-start | bytes 393216 | tf_op jit(solution)/shard_map/all_to_all | solution.py:319
  65.8 12.2 %all-to-all-done.1 = f32[128,1,384]{2,1,0:T(1,128)S(1)} async-done(((f32[128,1,384]{2,1,0:T(1,128)}), f32[128,1,384]{2,1,0:T(1,128)S(1)}, u32[]{:S(2)}, u32[]{:S(2)}) %all-to-all-start.1) | async-done | bytes 196640 | tf_op jit(solution)/shard_map/all_to_all | solution.py:319
  78.0 0.0 copy-done.7
  78.0 0.0 copy-done.8
  78.0 1.0 %shard_map.135 = f32[6,2,32,128]{3,2,1,0:T(8,128)} custom-call(s32[1]{0:T(128)} %bitcast.6.position, f32[384,128]{1,0:T(8,128)S(1)} %bitcast.21, f32[64,64]{1,0:T(8,128)S(1)} %copy-done.7, f32[64,64]{1,0:T(8,128)S(1)} %copy-done.8), custom_call_target="tpu_custom_call" | custom-call | tf_op jit(solution)/shard_map/pallas_call | solution.py:408
Async XLA Ops:
  0.6 12.6 %copy-start.6 = (f32[8,128]{1,0:T(8,128)S(1)}, f32[8,128]{1,0:T(8,128)}, u32[]{:S(2)}) copy-start(f32[8,128]{1,0:T(8,128)} %constant.14.clone.select) | copy-start | bytes 12292
  0.6 12.5 %copy-start = (f32[3,3,32,128]{3,2,1,0:T(8,128)S(1)}, f32[3,3,32,128]{3,2,1,0:T(8,128)}, u32[]{:S(2)}) copy-start(f32[3,3,32,128]{3,2,1,0:T(8,128)} %param.11) | copy-start | bytes 442372
  0.7 12.5 %copy-start.1 = (f32[3,3,32,128]{3,2,1,0:T(8,128)S(1)}, f32[3,3,32,128]{3,2,1,0:T(8,128)}, u32[]{:S(2)}) copy-start(f32[3,3,32,128]{3,2,1,0:T(8,128)} %param.12) | copy-start | bytes 442372
  0.7 12.5 %copy-start.2 = (f32[2,3,32,128]{3,2,1,0:T(8,128)S(1)}, f32[2,3,32,128]{3,2,1,0:T(8,128)}, u32[]{:S(2)}) copy-start(f32[2,3,32,128]{3,2,1,0:T(8,128)} %param.13) | copy-start | bytes 294916
  0.7 12.5 %copy-start.3 = (f32[3,32,128]{2,1,0:T(8,128)S(1)}, f32[3,32,128]{2,1,0:T(8,128)}, u32[]{:S(2)}) copy-start(f32[3,32,128]{2,1,0:T(8,128)} %density.5) | copy-start | bytes 147460
  2.3 11.1 %collective-permute-start = (f32[108,128]{1,0:T(8,128)}, f32[108,128]{1,0:T(8,128)S(1)}, u32[]{:S(2)}, u32[]{:S(2)}) collective-permute-start(f32[108,128]{1,0:T(8,128)} %get-tuple-element.10), channel_id=1, source_target_pairs={{0,4},{4,8},{8,12},{12,16},{16,20},{20,24},{24,28},{28,32},{32,36}... | collective-permute-start | bytes 165896 | tf_op jit(solution)/shard_map/ppermute | solution.py:326
  6.9 17.8 %copy-start.4 = (f32[2,3,2,32,128]{4,3,2,1,0:T(8,128)S(1)}, f32[2,3,2,32,128]{4,3,2,1,0:T(8,128)}, u32[]{:S(2)}) copy-start(f32[2,3,2,32,128]{4,3,2,1,0:T(8,128)} %param.15) | copy-start | bytes 589828
  6.9 7.3 %collective-permute-start.1 = (f32[108,128]{1,0:T(8,128)}, f32[108,128]{1,0:T(8,128)S(1)}, u32[]{:S(2)}, u32[]{:S(2)}) collective-permute-start(f32[108,128]{1,0:T(8,128)} %get-tuple-element.11), channel_id=1, source_target_pairs={{4,0},{8,4},{12,8},{16,12},{20,16},{24,20},{28,24},{32,28},{36,32}... | collective-permute-start | bytes 165896 | tf_op jit(solution)/shard_map/ppermute | solution.py:326
  14.4 6.2 %collective-permute-start.2 = (f32[4,1152]{1,0:T(4,128)S(1)}, f32[4,1152]{1,0:T(4,128)S(1)}, u32[]{:S(2)}, u32[]{:S(2)}) collective-permute-start(f32[4,1152]{1,0:T(4,128)S(1)} %get-tuple-element.12), channel_id=1, source_target_pairs={{1,0},{2,1},{3,2},{0,3},{5,4},{6,5},{7,6},{4,7},{9,8},{10,9},{11,1... | collective-permute-start | bytes 55304 | tf_op jit(solution)/shard_map/ppermute | solution.py:326
  17.9 6.8 %copy-start.9 = (f32[2]{0:T(128)S(1)}, f32[2]{0:T(128)}, u32[]{:S(2)}) copy-start(f32[2]{0:T(128)} %omega.1) | copy-start | bytes 28
  17.9 6.8 %copy-start.10 = (f32[2]{0:T(128)S(1)}, f32[2]{0:T(128)}, u32[]{:S(2)}) copy-start(f32[2]{0:T(128)} %phase.1) | copy-start | bytes 28
  18.0 6.7 %collective-permute-start.3 = (f32[4,1152]{1,0:T(4,128)S(1)}, f32[4,1152]{1,0:T(4,128)S(1)}, u32[]{:S(2)}, u32[]{:S(2)}) collective-permute-start(f32[4,1152]{1,0:T(4,128)S(1)} %get-tuple-element.13), channel_id=1, source_target_pairs={{0,1},{1,2},{2,3},{3,0},{4,5},{5,6},{6,7},{7,4},{8,9},{9,10},{10,1... | collective-permute-start | bytes 55304 | tf_op jit(solution)/shard_map/ppermute | solution.py:326
  28.9 29.5 %copy-start.5 = (bf16[256,384]{1,0:T(8,128)(2,1)S(1)}, bf16[256,384]{1,0:T(8,128)(2,1)}, u32[]{:S(2)}) copy-start(bf16[256,384]{1,0:T(8,128)(2,1)} %constant.15.clone.table) | copy-start | bytes 589828
  59.4 18.6 %copy-start.7 = (f32[64,64]{1,0:T(8,128)S(1)}, f32[64,64]{1,0:T(8,128)}, u32[]{:S(2)}) copy-start(f32[64,64]{1,0:T(8,128)} %constant.16.clone.straight) | copy-start | bytes 49156
  59.4 18.6 %copy-start.8 = (f32[64,64]{1,0:T(8,128)S(1)}, f32[64,64]{1,0:T(8,128)}, u32[]{:S(2)}) copy-start(f32[64,64]{1,0:T(8,128)} %constant.17.clone.turned) | copy-start | bytes 49156
  59.4 18.6 %all-to-all-start.1 = ((f32[128,1,384]{2,1,0:T(1,128)}), f32[128,1,384]{2,1,0:T(1,128)S(1)}, u32[]{:S(2)}, u32[]{:S(2)}) async-start(f32[128,1,384]{2,1,0:T(1,128)} %bitcast.9), calls=%async_computation.1 | async-start | bytes 393216 | tf_op jit(solution)/shard_map/all_to_all | solution.py:319

commit v2 on v1

--- a/solution.py
+++ b/solution.py
@@ -10,6 +10,7 @@
 time_step = 0.03
 HALO = 4
 EDGE = 8
+BINS = 12
 
 
 def edge_columns(width):
@@ -41,23 +42,19 @@
     )
 
 
-def pack_rows_kernel(disp, prev, moduli, density, up, down, low, high, sems):
+def pack_rows_kernel(disp, prev, moduli, density, bins, out, sems):
     copies = []
     start = 0
-    for n, ref in enumerate((disp, prev, moduli, density)):
-        planes, rows, _ = ref.shape
-        here = pl.ds(start, planes)
-        copies.append(pltpu.make_async_copy(ref.at[:, pl.ds(0, 8), :], low.at[here], sems.at[2 * n]))
-        copies.append(pltpu.make_async_copy(ref.at[:, pl.ds(rows - 8, 8), :], high.at[here], sems.at[2 * n + 1]))
+    for n, ref in enumerate((disp, prev, moduli, density, bins)):
+        planes = ref.shape[0]
+        copies.append(
+            pltpu.make_async_copy(ref.at[:, pl.ds(0, EDGE), :], out.at[pl.ds(start, planes)], sems.at[n])
+        )
         start += planes
     for copy in copies:
         copy.start()
     for copy in copies:
         copy.wait()
-    for i in range(start):
-        at = i * HALO
-        up[at : at + HALO, :] = high[i, 8 - HALO :, :]
-        down[at : at + HALO, :] = low[i, :HALO, :]
 
 
 def pack_main_kernel(disp, prev, moduli, density, select, main):
@@ -68,15 +65,22 @@
     main[:, used:] = jnp.zeros((EDGE, main.shape[1] - used), jnp.float32)
 
 
-def pack_columns_kernel(main, before, after, select, first, last):
+def pack_columns_kernel(position, main, ahead, select, out):
+    peers, _, total = out.shape
     width = main.shape[1]
-    lanes = select.shape[1]
-    first[:, :width] = main[:HALO, :]
-    last[:, :width] = main[HALO:, :]
-    fill = jnp.zeros((lanes - before.shape[0], lanes), jnp.float32)
-    packed = pick_columns(select, jnp.concatenate([after[...], fill, before[...], fill], axis=0))
-    first[:, width:] = packed[:HALO]
-    last[:, width:] = packed[HALO:]
+    planes = ahead.shape[0] - BINS
+    rows = ahead[:planes].reshape(planes * EDGE, select.shape[1])
+    fill = jnp.zeros((total - width - rows.shape[0], rows.shape[1]), jnp.float32)
+    packed = pick_columns(select, jnp.concatenate([rows, fill], axis=0))
+    me = position[1]
+    for step in range(peers):
+        slot = lax.rem(me + step, peers)
+        if step in (1, peers - 1):
+            at = HALO if step == 1 else 0
+            out[slot, :, :width] = main[at : at + HALO, :]
+            out[slot, :, width:] = packed[at : at + HALO]
+        else:
+            out[slot] = jnp.zeros((HALO, total), jnp.float32)
 
 
 def shift(value, amount, axis):
@@ -111,13 +115,15 @@
 
 
 def step_kernel(
-    omega, phase, disp, prev, moduli, density, bins, before, after, east, west, select,
-    updated, middle, operand, field, coef, strip, mid,
+    position, omega, phase, disp, prev, moduli, density, bins, ahead, beside, select,
+    updated, middle, tail, operand, field, coef, strip, mid,
 ):
     rows, width = disp.shape[1], disp.shape[2]
     tall, wide = rows + EDGE, 2 * width
-    halo_at = east.shape[1] - 2 * width
-    both = jnp.concatenate([east[...], west[...]], axis=0)
+    peers = beside.shape[0]
+    halo_at = beside.shape[2] - 2 * width
+    me = position[1]
+    both = jnp.concatenate([beside[lax.rem(me + 1, peers)], beside[lax.rem(me + peers - 1, peers)]], axis=0)
     chosen = select[...].astype(jnp.bfloat16)
     strip[...] = lax.dot_general(
         jnp.concatenate(halves(both), axis=0),
@@ -130,13 +136,9 @@
         for i in range(ref.shape[0]):
             n = start + i
             field[n, :rows, :width] = ref[i]
-            field[n, rows : rows + HALO, :width] = after[n * HALO : (n + 1) * HALO, :]
-            field[n, rows + HALO :, :width] = before[n * HALO : (n + 1) * HALO, :]
+            field[n, rows:, :width] = ahead[n]
             field[n, :rows, width:] = strip[n * rows : (n + 1) * rows, :]
-            field[n, rows : rows + HALO, width:] = strip[halo_at + n * HALO : halo_at + (n + 1) * HALO, :]
-            field[n, rows + HALO :, width:] = strip[
-                halo_at + width + n * HALO : halo_at + width + (n + 1) * HALO, :
-            ]
+            field[n, rows:, width:] = strip[halo_at + n * EDGE : halo_at + (n + 1) * EDGE, :]
         start += ref.shape[0]
 
     def tiled(tile, shape=(tall, wide)):
@@ -165,24 +167,18 @@
             coef[layer, n] = value
 
     def advance(source, older, store, own):
-        out_rows, out_width = (rows, width) if own else (tall, wide)
+        out_width = width if own else wide
         even_x, even_y = near_x == 0, near_y == 0
-        even_xs, even_ys = even_x[:, :out_width], even_y[:out_rows, :]
+        even_xs = even_x[:, :out_width]
 
         def for_x(value):
             return value[:, :out_width]
 
-        def for_y(value):
-            return value[:out_rows, :]
-
-        def for_z(value):
-            return value[:out_rows, :out_width]
-
         def along_x(right, left):
-            return spread(right, left, 0, even_xs)[:out_rows]
+            return spread(right, left, 0, even_xs)
 
         def along_y(right, left):
-            return spread(right, left, 1, even_ys)[:, :out_width]
+            return spread(right, left, 1, even_y)[:, :out_width]
 
         forces = [[None] * 3 for _ in range(3)]
         z_terms = [[None] * 3 for _ in range(3)]
@@ -210,32 +206,43 @@
             force_y = along_x(scale * for_x(rx[1]) + common, scale * for_x(lx[1]) + common)
             common = for_x(grad_z[0])
             force_z = along_x(scale * (for_x(rx[2]) + common), scale * (for_x(lx[2]) + common))
-            common = for_y(lam_x * grad_z[2] + lam * sx[0])
-            scale = for_y(stiff_x)
-            force_y += along_y(scale * for_y(ry[1]) + common, scale * for_y(ly[1]) + common)
-            common = for_y(mu * sx[1])
-            scale = for_y(mu_x)
-            force_x += along_y(scale * for_y(ry[0]) + common, scale * for_y(ly[0]) + common)
-            common = for_y(grad_z[1])
-            force_z += along_y(scale * (for_y(ry[2]) + common), scale * (for_y(ly[2]) + common))
+            common = (lam_x * grad_z[2] + lam * sx[0])
+            scale = (stiff_x)
+            force_y += along_y(scale * (ry[1]) + common, scale * (ly[1]) + common)
+            common = (mu * sx[1])
+            scale = (mu_x)
+            force_x += along_y(scale * (ry[0]) + common, scale * (ly[0]) + common)
+            common = (grad_z[1])
+            force_z += along_y(scale * ((ry[2]) + common), scale * ((ly[2]) + common))
             for c, value in enumerate((force_x, force_y, force_z)):
                 forces[c][layer] = value
-            z_terms[0][layer] = for_z(mu_xy * grad_z[0] + mu_y * sx[2])
-            z_terms[1][layer] = for_z(mu_xy * grad_z[1] + mu_x * sy[2])
-            z_terms[2][layer] = for_z(lam_y * sx[0] + lam_x * sy[1] + stiff_z * grad_z[2])
+            z_terms[0][layer] = for_x(mu_xy * grad_z[0] + mu_y * sx[2])
+            z_terms[1][layer] = for_x(mu_xy * grad_z[1] + mu_x * sy[2])
+            z_terms[2][layer] = for_x(lam_y * sx[0] + lam_x * sy[1] + stiff_z * grad_z[2])
         for c in range(3):
             along_z = spread_z(z_terms[c])
             for layer in range(3):
                 n = c * 3 + layer
-                total = (forces[c][layer] + along_z[layer]) * for_z(coef[layer, 10])
-                store(n, 2.0 * for_z(source(n)) - for_z(older(n)) - total)
+                total = (forces[c][layer] + along_z[layer]) * for_x(coef[layer, 10])
+                store(n, 2.0 * for_x(source(n)) - for_x(older(n)) - total)
+
+    is_tail = lax.broadcasted_iota(jnp.int32, (EDGE, width), 0) < HALO
+    tops = {}
+
+    def keep(ref, n, value):
+        ref[n] = value[:rows]
+        if n % 3 == 2:
+            first = jnp.where(is_tail, value[rows:], value[:EDGE])
+            tops.setdefault(n // 3, []).append(jnp.concatenate([first, value[EDGE:rows]], axis=0))
 
     def keep_middle(n, value):
         mid[n] = value
-        middle[n] = value[:rows, :width]
+        tail[(9 + n) * HALO : (10 + n) * HALO, :] = value[rows : rows + HALO, :width]
+        keep(middle, n, value[:, :width])
 
     def keep_updated(n, value):
-        updated[n] = value
+        tail[n * HALO : (n + 1) * HALO, :] = value[rows : rows + HALO]
+        keep(updated, n, value)
 
     advance(lambda n: field[n], lambda n: field[9 + n], keep_middle, False)
     advance(lambda n: mid[n], lambda n: field[n], keep_updated, True)
@@ -250,10 +257,14 @@
     half = width // 2
     for b in range(2):
         for c in range(3):
-            one, two = middle[c * 3 + 2], updated[c * 3 + 2]
+            one, two = tops[c]
             item = b * 3 + c
-            real = bins[2 * item] + cosines[b : b + 1] * one + cosines[2 + b : 3 + b] * two
-            imag = bins[2 * item + 1] - sines[b : b + 1] * one - sines[2 + b : 3 + b] * two
+            old = []
+            for n in (2 * item, 2 * item + 1):
+                first = jnp.where(is_tail, ahead[start + n], bins[n, :EDGE])
+                old.append(jnp.concatenate([first, bins[n, EDGE:]], axis=0))
+            real = old[0] + cosines[b : b + 1] * one + cosines[2 + b : 3 + b] * two
+            imag = old[1] - sines[b : b + 1] * one - sines[2 + b : 3 + b] * two
             if item < 4:
                 operand[pl.ds(3 * item * rows, rows, stride=3), :] = real
                 operand[pl.ds(3 * item * rows + 1, rows, stride=3), :] = imag
@@ -265,7 +276,8 @@
                 )
 
 
-def first_transform_kernel(received, table, out):
+def first_transform_kernel(received, table, tail, out, tail_out):
+    tail_out[...] = tail[...]
     count, width = received.shape[0] // 3, received.shape[1]
     joined = jnp.concatenate([received[pl.ds(n, count, stride=3), :] for n in range(3)], axis=1)
     high, rest = halves(joined)
@@ -297,8 +309,9 @@
             real.append(jnp.where(low, one, pltpu.roll(two, half, 1)))
             imag.append(jnp.where(low, pltpu.roll(one, half, 1), two))
     joined = jnp.concatenate([jnp.concatenate(real, axis=1), jnp.concatenate(imag, axis=1)], axis=0)
-    node = lax.broadcasted_iota(jnp.int32, straight.shape, 1) % rows
-    angle = (node * position[0]).astype(jnp.float32) * (2.0 * np.pi / (rows * count))
+    slot = lax.broadcasted_iota(jnp.int32, straight.shape, 1) % rows
+    node = jnp.where(slot < HALO, slot + rows, slot)
+    angle = (node * position[0] % (rows * count)).astype(jnp.float32) * (2.0 * np.pi / (rows * count))
     matrix = straight[...] * jnp.cos(angle) + turned[...] * jnp.sin(angle)
     left, left_rest = halves(matrix)
     high, rest = halves(joined)
@@ -312,6 +325,13 @@
             out[item, part] = waves[part * rows : (part + 1) * rows, item * width : (item + 1) * width]
 
 
+def set_in_kernel(updated, middle, tail, updated_out, middle_out):
+    for k, (ref, out) in enumerate(((updated, updated_out), (middle, middle_out))):
+        for n in range(ref.shape[0]):
+            out[n] = ref[n]
+            out[n, :HALO, :] = tail[(k * ref.shape[0] + n) * HALO : (k * ref.shape[0] + n + 1) * HALO, :]
+
+
 def exchange(value):
     peers = lax.axis_size("gx")
     rows, width = value.shape
@@ -319,11 +339,13 @@
     return lax.all_to_all(shaped, "gx", split_axis=0, concat_axis=0, tiled=True).reshape(rows, width)
 
 
-def both_ways(forward, backward, axis):
+def exchange_gy(value):
+    return lax.all_to_all(value, "gy", split_axis=0, concat_axis=0, tiled=True)
+
+
+def pass_on(value, axis, step):
     peers = lax.axis_size(axis)
-    up = [(i, (i + 1) % peers) for i in range(peers)]
-    down = [(j, i) for i, j in up]
-    return lax.ppermute(forward, axis, up), lax.ppermute(backward, axis, down)
+    return lax.ppermute(value, axis, [(i, (i + step) % peers) for i in range(peers)])
 
 
 def f32(*shape):
@@ -335,26 +357,23 @@
     rows, width = density.shape[1:]
     items = bins.shape[0] * bins.shape[1]
     block = (rows, width)
-    arrays = [a.reshape((-1,) + block) for a in (displacement, previous, moduli, density)]
-    planes = sum(a.shape[0] for a in arrays)
+    arrays = [a.reshape((-1,) + block) for a in (displacement, previous, moduli, density, bins)]
+    planes = sum(a.shape[0] for a in arrays) - BINS
     packed = -(-planes * rows // width) * width
     total = packed + 2 * width
     select = jnp.asarray(edge_columns(width))
+    position = jnp.stack([lax.axis_index("gx"), lax.axis_index("gy")]).astype(jnp.int32)
     vmem = pl.BlockSpec(memory_space=pltpu.VMEM)
     smem = pl.BlockSpec(memory_space=pltpu.SMEM)
+    hbm = pl.BlockSpec(memory_space=pltpu.HBM)
     params = pltpu.CompilerParams(vmem_limit_bytes=48 * 1024 * 1024)
 
-    hbm = pl.BlockSpec(memory_space=pltpu.HBM)
-    up, down = pl.pallas_call(
+    edge = pl.pallas_call(
         pack_rows_kernel,
-        out_shape=(f32(planes * HALO, width), f32(planes * HALO, width)),
-        in_specs=[hbm] * 4,
-        out_specs=(vmem,) * 2,
-        scratch_shapes=[
-            pltpu.VMEM((planes, 8, width), jnp.float32),
-            pltpu.VMEM((planes, 8, width), jnp.float32),
-            pltpu.SemaphoreType.DMA((8,)),
-        ],
+        out_shape=f32(planes + BINS, EDGE, width),
+        in_specs=[hbm] * 5,
+        out_specs=hbm,
+        scratch_shapes=[pltpu.SemaphoreType.DMA((5,))],
         compiler_params=pltpu.CompilerParams(vmem_limit_bytes=62 * 1024 * 1024),
     )(*arrays)
     main = pl.pallas_call(
@@ -364,22 +383,21 @@
         out_specs=vmem,
         compiler_params=params,
         cost_estimate=pl.CostEstimate(flops=50_000_000, bytes_accessed=2_000_000, transcendentals=0),
-    )(*arrays, select)
-    before, after = both_ways(up, down, "gx")
-    first, last = pl.pallas_call(
+    )(*arrays[:4], select)
+    ahead = pass_on(edge, "gx", -1)
+    sides = pl.pallas_call(
         pack_columns_kernel,
-        out_shape=(f32(HALO, total), f32(HALO, total)),
-        in_specs=[vmem] * 4,
-        out_specs=(vmem,) * 2,
-        compiler_params=params,
-    )(main, before, after, select)
-    west, east = both_ways(last, first, "gy")
+        out_shape=f32(lax.axis_size("gy"), HALO, total),
+        in_specs=[smem] + [vmem] * 3,
+        out_specs=vmem,
+        compiler_params=params,
+    )(position, main, ahead, select)
     tall, wide = rows + EDGE, 2 * width
-    updated, middle, operand = pl.pallas_call(
+    updated, middle, tail, operand = pl.pallas_call(
         step_kernel,
-        out_shape=(f32(9, *block), f32(9, *block), f32(3 * groups, width)),
-        in_specs=[smem] * 2 + [vmem] * 10,
-        out_specs=(vmem,) * 3,
+        out_shape=(f32(9, *block), f32(9, *block), f32(18 * HALO, width), f32(3 * groups, width)),
+        in_specs=[smem] * 3 + [vmem] * 8,
+        out_specs=(vmem,) * 4,
         scratch_shapes=[
             pltpu.VMEM((planes, tall, wide), jnp.float32),
             pltpu.VMEM((3, 11, tall, wide), jnp.float32),
@@ -387,24 +405,31 @@
             pltpu.VMEM((9, tall, wide), jnp.float32),
         ],
         compiler_params=params,
-    )(omega, phase, *arrays, bins.reshape((-1,) + block), before, after, east, west, select)
+    )(position, omega, phase, *arrays, ahead, exchange_gy(sides), select)
 
     stacked = np.concatenate(fourier_tables(groups), axis=0)
     high = stacked.astype(ml_dtypes.bfloat16)
     rest = (stacked - high.astype(np.float64)).astype(ml_dtypes.bfloat16)
     table = jnp.asarray(np.concatenate([high, high, rest], axis=1))
-    sections = pl.pallas_call(
+    sections, tail = pl.pallas_call(
         first_transform_kernel,
-        out_shape=f32(3 * groups, width),
-        in_specs=[vmem] * 2,
-        out_specs=vmem,
-        compiler_params=params,
-    )(exchange(operand), table)
+        out_shape=(f32(3 * groups, width), f32(*tail.shape)),
+        in_specs=[vmem] * 3,
+        out_specs=(vmem,) * 2,
+        compiler_params=params,
+    )(exchange(operand), table, tail)
+    updated, middle = pl.pallas_call(
+        set_in_kernel,
+        out_shape=(f32(9, *block), f32(9, *block)),
+        in_specs=[vmem] * 3,
+        out_specs=(vmem,) * 2,
+        compiler_params=params,
+        cost_estimate=pl.CostEstimate(flops=1_000_000, bytes_accessed=1_200_000, transcendentals=0),
+    )(updated, middle, pass_on(tail, "gx", 1))
     scale = (groups * rows) ** -0.5
     c, s = (t * scale for t in fourier_tables(rows))
     straight = jnp.asarray(np.block([[c, s], [-s, c]]), jnp.float32)
     turned = jnp.asarray(np.block([[-s, c], [-c, -s]]), jnp.float32)
-    position = lax.axis_index("gx").astype(jnp.int32).reshape(1)
     spectrum = pl.pallas_call(
         second_transform_kernel,
         out_shape=f32(items, 2, *block),

time: 79.3 us -> 85.2 us (1.074)
  blocking collectives: 29.5 us -> 42.7 us
  waiting for transfers between devices: 17.1 us -> 8.16 us
  Pallas kernels: 8.14 us -> 13.9 us
  starting transfers between devices: 23.4 us -> 18.6 us
    all_to_all x0 -> x1, blocking collectives: none -> 11.8 us  [exchange_gy(): return lax.all_to_all(value, 'gy', split_axis=0, concat_axis=0, tiled=True)]
    pallas_call x3 -> x4, Pallas kernels: 2.8 us -> 8.44 us  [the longest x1 5.99 us: on_device(): pl.pallas_call(pack_rows_kernel, out_shape=f32(planes + BINS, EDGE, width...]
    all_to_all x1, waiting for transfers between devices: 12.2 us -> 6.9 us  [exchange(): lax.all_to_all(shaped, 'gx', split_axis=0, concat_axis=0, tiled=True)]
    ppermute x4 -> x2, starting transfers between devices: 17 us -> 12.3 us  [pass_on(): lax.ppermute(value, axis, [(i, (i + step) % peers) for i in range(peers)])]
    ppermute x4 -> x2, waiting for transfers between devices: 4.84 us -> 1.26 us  [pass_on(): lax.ppermute(value, axis, [(i, (i + step) % peers) for i in range(peers)])]
    all_to_all x1, blocking collectives: 29.5 us -> 30.9 us  [exchange(): lax.all_to_all(shaped, 'gx', split_axis=0, concat_axis=0, tiled=True)]
  transfers between devices with their start and end apart: 5 -> 3, of which waited for: 3 -> 3; matrix products, arithmetic and copies ran while one was open for 0% -> 0% of each run, Pallas kernels for 0% -> 1%
where the time goes in v2:
time: 85.2 us; the launch traced here: 84.8 us
  blocking collectives  42.7 us (50%)
  starting transfers between devices  18.6 us (22%)
  Pallas kernels  13.9 us (16%)
  waiting for transfers between devices  8.16 us (10%)
    all_to_all x1, blocking collectives, exchange(): lax.all_to_all(shaped, 'gx', split_axis=0, concat_axis=0, tiled=True)  30.9 us
    ppermute x2, starting transfers between devices, pass_on(): lax.ppermute(value, axis, [(i, (i + step) % peers) for i in range(peers)])  12.3 us
    all_to_all x1, blocking collectives, exchange_gy(): return lax.all_to_all(value, 'gy', split_axis=0, concat_axis=0, tiled=True)  11.8 us
    all_to_all x1, waiting for transfers between devices, exchange(): lax.all_to_all(shaped, 'gx', split_axis=0, concat_axis=0, tiled=True)  6.9 us
    all_to_all x1, starting transfers between devices, exchange(): lax.all_to_all(shaped, 'gx', split_axis=0, concat_axis=0, tiled=True)  6.22 us
    pallas_call x1, Pallas kernels, on_device(): pl.pallas_call(pack_rows_kernel, out_shape=f32(planes + BINS, EDGE, width...  5.99 us
    pallas_call x1, Pallas kernels, on_device(): pl.pallas_call(step_kernel, out_shape=(f32(9, *block), f32(9, *block), f3...  3.72 us
  transfers between devices with their start and end apart: 3, of which 3 were waited for; matrix products, arithmetic and copies ran while one was open for 0% of the time, Pallas kernels for 1%

profile of v2, /device:TPU:1, one launch (start us, length us, event | category | flops | bytes accessed | tf_op | source)
XLA Modules:
  0.0 84.8 jit_solution(13706476668578498207)
XLA Ops:
  0.6 0.0 copy-start
  0.6 0.0 copy-start.1
  0.7 0.0 copy-start.2
  0.7 0.0 copy-start.4
  0.7 6.0 %shard_map.130 = f32[39,8,128]{2,1,0:T(8,128)} custom-call(f32[9,32,128]{2,1,0:T(8,128)} %bitcast.13, f32[9,32,128]{2,1,0:T(8,128)} %bitcast.16, f32[6,32,128]{2,1,0:T(8,128)} %bitcast.19, f32[3,32,128]{2,1,0:T(8,128)} %density.5, f32[12,32,128]{2,1,0:T(8,128)} %bitcast.24), custom_call_target="tpu_custom_call" | custom-call | tf_op jit(solution)/shard_map/pallas_call | solution.py:371
  6.7 8.8 %collective-permute-start = (f32[39,8,128]{2,1,0:T(8,128)}, f32[39,8,128]{2,1,0:T(8,128)S(1)}, u32[]{:S(2)}, u32[]{:S(2)}) collective-permute-start(f32[39,8,128]{2,1,0:T(8,128)} %shard_map.130), channel_id=1, source_target_pairs={{0,508},{4,0},{8,4},{12,8},{16,12},{20,16},{24,20},{28,24},{32,28}... | collective-permute-start | bytes 479240 | tf_op jit(solution)/shard_map/ppermute | solution.py:348
  15.5 0.0 copy-start.6
  15.5 0.0 copy-done
  15.5 0.0 copy-done.1
  15.5 0.0 copy-done.2
  15.5 0.0 copy-done.4
  15.5 0.6 copy-done.6
  16.2 0.2 shard_map.131.main
  16.4 0.1 pad_add_fusion.position
  16.4 0.0 copy-start.3
  16.5 0.2 collective-permute-done.ahead
  16.7 0.7 shard_map.132
  17.4 0.0 copy-start.9
  17.4 0.0 copy-start.10
  17.4 11.8 %all_to_all.15.beside = f32[4,4,1152]{2,1,0:T(4,128)S(1)} all-to-all(f32[4,4,1152]{2,1,0:T(4,128)S(1)} %shard_map.132), channel_id=1, replica_groups=mesh['gx'=128,'gy'=4] {'gy'}, dimensions={0} | all-to-all | bytes 147456 | tf_op jit(solution)/shard_map/all_to_all | solution.py:343
  29.1 0.0 copy-done.3
  29.1 0.0 copy-done.9
  29.1 0.0 copy-done.10
  29.1 3.7 %shard_map.133 = (f32[9,32,128]{2,1,0:T(8,128)S(1)}, f32[9,32,128]{2,1,0:T(8,128)S(1)}, f32[72,128]{1,0:T(8,128)S(1)}, f32[384,128]{1,0:T(8,128)S(1)}) custom-call(s32[2]{0:T(128)S(1)} %pad_add_fusion.position, f32[2]{0:T(128)S(1)} %copy-done.9, f32[2]{0:T(128)S(1)} %copy-done.10, f32[9,32,128]{2,1,0:T(8,128)S(1)} %bitcast.15, f32[9,32,128]{2,1,0:T(8,128)S(1)} %bitcast.18, ...), custom_call_target="tpu_custom_call" | custom-call | tf_op jit(solution)/shard_map/pallas_call | solution.py:396
  32.9 0.0 copy-start.5
  32.9 30.9 %all_to_all.16 = f32[128,1,384]{2,1,0:T(1,128)S(1)} all-to-all(f32[128,1,384]{2,1,0:T(1,128)S(1)} %bitcast.26), channel_id=1, replica_groups=mesh['gx'=128,'gy'=4] {'gx'}, dimensions={0} | all-to-all | bytes 393216 | tf_op jit(solution)/shard_map/all_to_all | solution.py:339
  63.8 0.0 copy-done.5
  63.8 1.0 %shard_map.134 = (f32[384,128]{1,0:T(8,128)}, f32[72,128]{1,0:T(8,128)S(1)}) custom-call(f32[384,128]{1,0:T(8,128)S(1)} %bitcast.23, bf16[256,384]{1,0:T(8,128)(2,1)S(1)} %copy-done.5, f32[72,128]{1,0:T(8,128)S(1)} %get-tuple-element.14.tail), custom_call_target="tpu_custom_call" | custom-call | tf_op jit(solution)/shard_map/pallas_call | solution.py:414
  64.8 6.2 %all-to-all-start.2 = ((f32[128,1,384]{2,1,0:T(1,128)}), f32[128,1,384]{2,1,0:T(1,128)S(1)}, u32[]{:S(2)}, u32[]{:S(2)}) async-start(f32[128,1,384]{2,1,0:T(1,128)} %bitcast.10), calls=%async_computation.2 | async-start | bytes 393216 | tf_op jit(solution)/shard_map/all_to_all | solution.py:339
  71.1 3.5 %collective-permute-start.1 = (f32[72,128]{1,0:T(8,128)S(1)}, f32[72,128]{1,0:T(8,128)S(1)}, u32[]{:S(2)}, u32[]{:S(2)}) collective-permute-start(f32[72,128]{1,0:T(8,128)S(1)} %get-tuple-element.15), channel_id=1, source_target_pairs={{0,4},{4,8},{8,12},{12,16},{16,20},{20,24},{24,28},{28,32},{32,36}... | collective-permute-start | bytes 110600 | tf_op jit(solution)/shard_map/ppermute | solution.py:348
  74.6 1.0 %collective-permute-done.1.tail = f32[72,128]{1,0:T(8,128)S(1)} collective-permute-done((f32[72,128]{1,0:T(8,128)S(1)}, f32[72,128]{1,0:T(8,128)S(1)}, u32[]{:S(2)}, u32[]{:S(2)}) %collective-permute-start.1) | collective-permute-done | bytes 36896 | tf_op jit(solution)/shard_map/ppermute | solution.py:348
  75.7 0.0 copy-start.7
  75.7 0.0 copy-start.8
  75.7 0.7 shard_map.135
  76.4 6.9 %all-to-all-done.2 = f32[128,1,384]{2,1,0:T(1,128)S(1)} async-done(((f32[128,1,384]{2,1,0:T(1,128)}), f32[128,1,384]{2,1,0:T(1,128)S(1)}, u32[]{:S(2)}, u32[]{:S(2)}) %all-to-all-start.2) | async-done | bytes 196640 | tf_op jit(solution)/shard_map/all_to_all | solution.py:339
  83.3 0.0 copy-done.7
  83.3 0.0 copy-done.8
  83.3 1.5 %shard_map.136 = f32[6,2,32,128]{3,2,1,0:T(8,128)} custom-call(s32[2]{0:T(128)S(1)} %pad_add_fusion.position, f32[384,128]{1,0:T(8,128)S(1)} %bitcast.22, f32[64,64]{1,0:T(8,128)S(1)} %copy-done.8, f32[64,64]{1,0:T(8,128)S(1)} %copy-done.7), custom_call_target="tpu_custom_call" | custom-call | tf_op jit(solution)/shard_map/pallas_call | solution.py:433
Async XLA Ops:
  0.6 14.9 %copy-start = (f32[3,3,32,128]{3,2,1,0:T(8,128)S(1)}, f32[3,3,32,128]{3,2,1,0:T(8,128)}, u32[]{:S(2)}) copy-start(f32[3,3,32,128]{3,2,1,0:T(8,128)} %param.11) | copy-start | bytes 442372
  0.6 14.9 %copy-start.1 = (f32[3,3,32,128]{3,2,1,0:T(8,128)S(1)}, f32[3,3,32,128]{3,2,1,0:T(8,128)}, u32[]{:S(2)}) copy-start(f32[3,3,32,128]{3,2,1,0:T(8,128)} %param.12) | copy-start | bytes 442372
  0.7 14.9 %copy-start.2 = (f32[2,3,32,128]{3,2,1,0:T(8,128)S(1)}, f32[2,3,32,128]{3,2,1,0:T(8,128)}, u32[]{:S(2)}) copy-start(f32[2,3,32,128]{3,2,1,0:T(8,128)} %param.13) | copy-start | bytes 294916
  0.7 14.9 %copy-start.4 = (f32[3,32,128]{2,1,0:T(8,128)S(1)}, f32[3,32,128]{2,1,0:T(8,128)}, u32[]{:S(2)}) copy-start(f32[3,32,128]{2,1,0:T(8,128)} %density.5) | copy-start | bytes 147460
  6.7 10.0 %collective-permute-start = (f32[39,8,128]{2,1,0:T(8,128)}, f32[39,8,128]{2,1,0:T(8,128)S(1)}, u32[]{:S(2)}, u32[]{:S(2)}) collective-permute-start(f32[39,8,128]{2,1,0:T(8,128)} %shard_map.130), channel_id=1, source_target_pairs={{0,508},{4,0},{8,4},{12,8},{16,12},{20,16},{24,20},{28,24},{32,28}... | collective-permute-start | bytes 479240 | tf_op jit(solution)/shard_map/ppermute | solution.py:348
  15.5 0.7 copy-start.6
  16.4 12.7 %copy-start.3 = (f32[2,3,2,32,128]{4,3,2,1,0:T(8,128)S(1)}, f32[2,3,2,32,128]{4,3,2,1,0:T(8,128)}, u32[]{:S(2)}) copy-start(f32[2,3,2,32,128]{4,3,2,1,0:T(8,128)} %param.15) | copy-start | bytes 589828
  17.4 11.8 %copy-start.9 = (f32[2]{0:T(128)S(1)}, f32[2]{0:T(128)}, u32[]{:S(2)}) copy-start(f32[2]{0:T(128)} %omega.1) | copy-start | bytes 28
  17.4 11.8 %copy-start.10 = (f32[2]{0:T(128)S(1)}, f32[2]{0:T(128)}, u32[]{:S(2)}) copy-start(f32[2]{0:T(128)} %phase.1) | copy-start | bytes 28
  32.9 31.0 %copy-start.5 = (bf16[256,384]{1,0:T(8,128)(2,1)S(1)}, bf16[256,384]{1,0:T(8,128)(2,1)}, u32[]{:S(2)}) copy-start(bf16[256,384]{1,0:T(8,128)(2,1)} %constant.18.clone.table) | copy-start | bytes 589828
  64.8 18.5 %all-to-all-start.2 = ((f32[128,1,384]{2,1,0:T(1,128)}), f32[128,1,384]{2,1,0:T(1,128)S(1)}, u32[]{:S(2)}, u32[]{:S(2)}) async-start(f32[128,1,384]{2,1,0:T(1,128)} %bitcast.10), calls=%async_computation.2 | async-start | bytes 393216 | tf_op jit(solution)/shard_map/all_to_all | solution.py:339
  71.1 4.6 %collective-permute-start.1 = (f32[72,128]{1,0:T(8,128)S(1)}, f32[72,128]{1,0:T(8,128)S(1)}, u32[]{:S(2)}, u32[]{:S(2)}) collective-permute-start(f32[72,128]{1,0:T(8,128)S(1)} %get-tuple-element.15), channel_id=1, source_target_pairs={{0,4},{4,8},{8,12},{12,16},{16,20},{20,24},{24,28},{28,32},{32,36}... | collective-permute-start | bytes 110600 | tf_op jit(solution)/shard_map/ppermute | solution.py:348
  75.7 7.6 %copy-start.7 = (f32[64,64]{1,0:T(8,128)S(1)}, f32[64,64]{1,0:T(8,128)}, u32[]{:S(2)}) copy-start(f32[64,64]{1,0:T(8,128)} %constant.20.clone.turned) | copy-start | bytes 49156
  75.7 7.6 %copy-start.8 = (f32[64,64]{1,0:T(8,128)S(1)}, f32[64,64]{1,0:T(8,128)}, u32[]{:S(2)}) copy-start(f32[64,64]{1,0:T(8,128)} %constant.19.clone.straight) | copy-start | bytes 49156

commit v3 on v2

--- a/solution.py
+++ b/solution.py
@@ -65,22 +65,18 @@
     main[:, used:] = jnp.zeros((EDGE, main.shape[1] - used), jnp.float32)
 
 
-def pack_columns_kernel(position, main, ahead, select, out):
+def pack_columns_kernel(facts, main, ahead, select, out):
     peers, _, total = out.shape
     width = main.shape[1]
     planes = ahead.shape[0] - BINS
     rows = ahead[:planes].reshape(planes * EDGE, select.shape[1])
     fill = jnp.zeros((total - width - rows.shape[0], rows.shape[1]), jnp.float32)
     packed = pick_columns(select, jnp.concatenate([rows, fill], axis=0))
-    me = position[1]
-    for step in range(peers):
-        slot = lax.rem(me + step, peers)
-        if step in (1, peers - 1):
-            at = HALO if step == 1 else 0
-            out[slot, :, :width] = main[at : at + HALO, :]
-            out[slot, :, width:] = packed[at : at + HALO]
-        else:
-            out[slot] = jnp.zeros((HALO, total), jnp.float32)
+    for slot in range(peers):
+        after, before = (facts[n : n + 1, :1] > 0.5 for n in (slot, peers + slot))
+        for source, at in ((main[...], 0), (packed, width)):
+            chosen = jnp.where(after, source[HALO:], jnp.where(before, source[:HALO], 0.0))
+            out[slot, :, at : at + source.shape[1]] = chosen
 
 
 def shift(value, amount, axis):
@@ -88,25 +84,21 @@
 
 
 def slopes(value, axis, even):
-    ahead, ahead2 = shift(value, 1, axis), shift(value, 2, axis)
-    back, back2 = shift(value, -1, axis), shift(value, -2, axis)
-    right = jnp.where(even, 4.0 * ahead - 3.0 * value - ahead2, ahead - back)
-    left = 3.0 * value - 4.0 * back + back2
+    step = shift(value, 1, axis) - value
+    before = shift(step, -1, axis)
+    right = jnp.where(even, 3.0 * step - shift(step, 1, axis), step + before)
+    left = shift(3.0 * step - before, -1, axis)
     return right, left, jnp.where(even, right + left, right)
 
 
 def spread(right, left, axis, even):
-    ahead = jnp.where(even, -4.0 * left, -right)
-    back = jnp.where(even, 4.0 * right, right)
-    ahead = ahead + shift(jnp.where(even, left, 0.0), 1, axis)
-    back = back - shift(jnp.where(even, right, 0.0), -1, axis)
-    own = jnp.where(even, 3.0 * (left - right), 0.0)
-    return own + shift(ahead, 1, axis) + shift(back, -1, axis)
-
-
-def slopes_z(layers):
-    a, b, c = layers
-    return 4.0 * b - 3.0 * a - c, c - a, a - 4.0 * b + 3.0 * c
+    left = shift(left, 1, axis)
+    step = jnp.where(
+        even,
+        3.0 * right + shift(right - left, 1, axis),
+        right + 3.0 * left - shift(right, -1, axis),
+    )
+    return shift(step, -1, axis) - step
 
 
 def spread_z(layers):
@@ -115,15 +107,18 @@
 
 
 def step_kernel(
-    position, omega, phase, disp, prev, moduli, density, bins, ahead, beside, select,
+    facts, disp, prev, moduli, density, bins, ahead, beside, select,
     updated, middle, tail, operand, field, coef, strip, mid,
 ):
     rows, width = disp.shape[1], disp.shape[2]
     tall, wide = rows + EDGE, 2 * width
     peers = beside.shape[0]
     halo_at = beside.shape[2] - 2 * width
-    me = position[1]
-    both = jnp.concatenate([beside[lax.rem(me + 1, peers)], beside[lax.rem(me + peers - 1, peers)]], axis=0)
+    east = west = beside[0]
+    for slot in range(1, peers):
+        east = jnp.where(facts[slot : slot + 1, :1] > 0.5, beside[slot], east)
+        west = jnp.where(facts[peers + slot : peers + slot + 1, :1] > 0.5, beside[slot], west)
+    both = jnp.concatenate([east, west], axis=0)
     chosen = select[...].astype(jnp.bfloat16)
     strip[...] = lax.dot_general(
         jnp.concatenate(halves(both), axis=0),
@@ -247,11 +242,7 @@
     advance(lambda n: field[n], lambda n: field[9 + n], keep_middle, False)
     advance(lambda n: mid[n], lambda n: field[n], keep_updated, True)
 
-    slot = lax.broadcasted_iota(jnp.int32, (8, width), 0)
-    angles = jnp.zeros((8, width), jnp.float32)
-    for s in range(2):
-        for b in range(2):
-            angles = jnp.where(slot == 2 * s + b, phase[b] + (s + 1.0) * omega[b], angles)
+    angles = facts[2 * peers : 2 * peers + 8]
     cosines, sines = jnp.cos(angles), jnp.sin(angles)
     low = lax.broadcasted_iota(jnp.int32, (rows, width), 1) < width // 2
     half = width // 2
@@ -292,7 +283,7 @@
     out[pl.ds(2, count, stride=3), :] = by_cos[:, 2 * width :] + jnp.where(low, turned, -turned)
 
 
-def second_transform_kernel(position, received, straight, turned, out):
+def second_transform_kernel(facts, received, straight, turned, out):
     items, parts, rows, width = out.shape
     half = width // 2
     count = received.shape[0] // 3
@@ -310,8 +301,9 @@
             imag.append(jnp.where(low, pltpu.roll(one, half, 1), two))
     joined = jnp.concatenate([jnp.concatenate(real, axis=1), jnp.concatenate(imag, axis=1)], axis=0)
     slot = lax.broadcasted_iota(jnp.int32, straight.shape, 1) % rows
-    node = jnp.where(slot < HALO, slot + rows, slot)
-    angle = (node * position[0] % (rows * count)).astype(jnp.float32) * (2.0 * np.pi / (rows * count))
+    node = jnp.where(slot < HALO, slot + rows, slot).astype(jnp.float32)
+    place = facts[facts.shape[0] - 1 :, : slot.shape[1]]
+    angle = node * place * (2.0 * np.pi / (rows * count))
     matrix = straight[...] * jnp.cos(angle) + turned[...] * jnp.sin(angle)
     left, left_rest = halves(matrix)
     high, rest = halves(joined)
@@ -362,9 +354,20 @@
     packed = -(-planes * rows // width) * width
     total = packed + 2 * width
     select = jnp.asarray(edge_columns(width))
-    position = jnp.stack([lax.axis_index("gx"), lax.axis_index("gy")]).astype(jnp.int32)
+    peers = lax.axis_size("gy")
+    distance = jnp.arange(peers) - lax.axis_index("gy")
+    steps = jnp.arange(1, 3).astype(jnp.float32)
+    facts = jnp.concatenate(
+        [
+            (distance == 1) | (distance == 1 - peers),
+            (distance == -1) | (distance == peers - 1),
+            (phase[None, :] + steps[:, None] * omega[None, :]).reshape(-1),
+            jnp.full((4,), lax.axis_index("gx")),
+        ],
+        dtype=jnp.float32,
+    )
+    facts = jnp.broadcast_to(facts[:, None], (facts.shape[0], width))
     vmem = pl.BlockSpec(memory_space=pltpu.VMEM)
-    smem = pl.BlockSpec(memory_space=pltpu.SMEM)
     hbm = pl.BlockSpec(memory_space=pltpu.HBM)
     params = pltpu.CompilerParams(vmem_limit_bytes=48 * 1024 * 1024)
 
@@ -372,7 +375,7 @@
         pack_rows_kernel,
         out_shape=f32(planes + BINS, EDGE, width),
         in_specs=[hbm] * 5,
-        out_specs=hbm,
+        out_specs=vmem,
         scratch_shapes=[pltpu.SemaphoreType.DMA((5,))],
         compiler_params=pltpu.CompilerParams(vmem_limit_bytes=62 * 1024 * 1024),
     )(*arrays)
@@ -387,16 +390,16 @@
     ahead = pass_on(edge, "gx", -1)
     sides = pl.pallas_call(
         pack_columns_kernel,
-        out_shape=f32(lax.axis_size("gy"), HALO, total),
-        in_specs=[smem] + [vmem] * 3,
+        out_shape=f32(peers, HALO, total),
+        in_specs=[vmem] * 4,
         out_specs=vmem,
         compiler_params=params,
-    )(position, main, ahead, select)
+    )(facts, main, ahead, select)
     tall, wide = rows + EDGE, 2 * width
     updated, middle, tail, operand = pl.pallas_call(
         step_kernel,
         out_shape=(f32(9, *block), f32(9, *block), f32(18 * HALO, width), f32(3 * groups, width)),
-        in_specs=[smem] * 3 + [vmem] * 8,
+        in_specs=[vmem] * 9,
         out_specs=(vmem,) * 4,
         scratch_shapes=[
             pltpu.VMEM((planes, tall, wide), jnp.float32),
@@ -405,7 +408,7 @@
             pltpu.VMEM((9, tall, wide), jnp.float32),
         ],
         compiler_params=params,
-    )(position, omega, phase, *arrays, ahead, exchange_gy(sides), select)
+    )(facts, *arrays, ahead, exchange_gy(sides), select)
 
     stacked = np.concatenate(fourier_tables(groups), axis=0)
     high = stacked.astype(ml_dtypes.bfloat16)
@@ -433,10 +436,10 @@
     spectrum = pl.pallas_call(
         second_transform_kernel,
         out_shape=f32(items, 2, *block),
-        in_specs=[smem] + [vmem] * 3,
+        in_specs=[vmem] * 4,
         out_specs=vmem,
         compiler_params=params,
-    )(position, exchange(sections), straight, turned)
+    )(facts, exchange(sections), straight, turned)
     return (
         updated.reshape(displacement.shape),
         middle.reshape(displacement.shape),

time: 85.2 us -> 80.4 us (0.944)
  Pallas kernels: 13.9 us -> 9.45 us
  blocking collectives: 42.7 us -> 41.7 us
    pallas_call x1, Pallas kernels: 5.99 us -> 1.63 us  [on_device(): pl.pallas_call(pack_rows_kernel, out_shape=f32(planes + BINS, EDGE, width...]
    pallas_call x1, Pallas kernels: 3.72 us -> 4.68 us  [on_device(): pl.pallas_call(step_kernel, out_shape=(f32(9, *block), f32(9, *block), f3...]
  transfers between devices with their start and end apart: 3 -> 3, of which waited for: 3 -> 2; matrix products, arithmetic and copies ran while one was open for 0% -> 0% of each run, Pallas kernels for 1% -> 1%
where the time goes in v3:
time: 80.4 us; the launch traced here: 80 us
  blocking collectives  41.7 us (52%)
  starting transfers between devices  18.6 us (23%)
  Pallas kernels  9.45 us (12%)
  waiting for transfers between devices  7.94 us (10%)
  local copies, waits for them, and re-layouts  1.43 us (2%)
    all_to_all x1, blocking collectives, exchange(): lax.all_to_all(shaped, 'gx', split_axis=0, concat_axis=0, tiled=True)  30.4 us
    ppermute x2, starting transfers between devices, pass_on(): lax.ppermute(value, axis, [(i, (i + step) % peers) for i in range(peers)])  12.3 us
    all_to_all x1, blocking collectives, exchange_gy(): return lax.all_to_all(value, 'gy', split_axis=0, concat_axis=0, tiled=True)  11.3 us
    all_to_all x1, waiting for transfers between devices, exchange(): lax.all_to_all(shaped, 'gx', split_axis=0, concat_axis=0, tiled=True)  6.9 us
    all_to_all x1, starting transfers between devices, exchange(): lax.all_to_all(shaped, 'gx', split_axis=0, concat_axis=0, tiled=True)  6.22 us
    pallas_call x1, Pallas kernels, on_device(): pl.pallas_call(step_kernel, out_shape=(f32(9, *block), f32(9, *block), f3...  4.68 us
    pallas_call x1, Pallas kernels, on_device(): pl.pallas_call(pack_rows_kernel, out_shape=f32(planes + BINS, EDGE, width...  1.63 us
  transfers between devices with their start and end apart: 3, of which 2 were waited for; matrix products, arithmetic and copies ran while one was open for 0% of the time, Pallas kernels for 1%

profile of v3, /device:TPU:1, one launch (start us, length us, event | category | flops | bytes accessed | tf_op | source)
XLA Modules:
  0.0 80.0 jit_solution(9902585800791124756)
XLA Ops:
  0.6 0.0 copy-start
  0.6 0.0 copy-start.1
  0.7 0.0 copy-start.2
  0.7 0.0 copy-start.4
  0.7 1.6 %shard_map.130 = f32[39,8,128]{2,1,0:T(8,128)} custom-call(f32[9,32,128]{2,1,0:T(8,128)} %bitcast.11, f32[9,32,128]{2,1,0:T(8,128)} %bitcast.14, f32[6,32,128]{2,1,0:T(8,128)} %bitcast.17, f32[3,32,128]{2,1,0:T(8,128)} %density.5, f32[12,32,128]{2,1,0:T(8,128)} %bitcast.21), custom_call_target="tpu_custom_call" | custom-call | tf_op jit(solution)/shard_map/pallas_call | solution.py:374
  2.3 8.8 %collective-permute-start = (f32[39,8,128]{2,1,0:T(8,128)}, f32[39,8,128]{2,1,0:T(8,128)S(1)}, u32[]{:S(2)}, u32[]{:S(2)}) collective-permute-start(f32[39,8,128]{2,1,0:T(8,128)} %shard_map.130), channel_id=1, source_target_pairs={{0,508},{4,0},{8,4},{12,8},{16,12},{20,16},{24,20},{28,24},{32,28}... | collective-permute-start | bytes 479240 | tf_op jit(solution)/shard_map/ppermute | solution.py:340
  11.1 0.0 copy-start.9
  11.1 0.0 copy-start.10
  11.1 0.6 copy-done.9
  11.8 0.0 copy-done.10
  11.8 0.1 multiply_add_fusion
  11.9 0.0 copy-start.6
  11.9 0.1 add.22
  12.0 0.0 copy-done
  12.0 0.0 copy-done.1
  12.0 0.0 copy-done.2
  12.0 0.0 copy-done.4
  12.0 0.6 copy-done.6
  12.6 0.2 shard_map.131.main
  12.8 0.1 pad_maximum_fusion
  12.9 0.0 collective-permute-done.ahead
  12.9 0.1 broadcast_in_dim.5.facts
  13.0 0.0 copy-start.3
  13.0 0.2 shard_map.132
  13.2 11.3 %all_to_all.15.beside = f32[4,4,1152]{2,1,0:T(4,128)S(1)} all-to-all(f32[4,4,1152]{2,1,0:T(4,128)S(1)} %shard_map.132), channel_id=1, replica_groups=mesh['gx'=128,'gy'=4] {'gy'}, dimensions={0} | all-to-all | bytes 147456 | tf_op jit(solution)/shard_map/all_to_all | solution.py:335
  24.5 0.0 copy-done.3
  24.5 4.7 %shard_map.133 = (f32[9,32,128]{2,1,0:T(8,128)S(1)}, f32[9,32,128]{2,1,0:T(8,128)S(1)}, f32[72,128]{1,0:T(8,128)S(1)}, f32[384,128]{1,0:T(8,128)S(1)}) custom-call(f32[16,128]{1,0:T(8,128)S(1)} %broadcast_in_dim.5.facts, f32[9,32,128]{2,1,0:T(8,128)S(1)} %bitcast.13, f32[9,32,128]{2,1,0:T(8,128)S(1)} %bitcast.16, f32[6,32,128]{2,1,0:T(8,128)S(1)} %bitcast.19, ...), custom_call_target="tpu_custom_call" | custom-call | tf_op jit(solution)/shard_map/pallas_call | solution.py:399
  29.2 0.0 copy-start.5
  29.2 30.4 %all_to_all.16 = f32[128,1,384]{2,1,0:T(1,128)S(1)} all-to-all(f32[128,1,384]{2,1,0:T(1,128)S(1)} %bitcast.24), channel_id=1, replica_groups=mesh['gx'=128,'gy'=4] {'gx'}, dimensions={0} | all-to-all | bytes 393216 | tf_op jit(solution)/shard_map/all_to_all | solution.py:331
  59.6 0.0 copy-done.5
  59.6 1.0 %shard_map.134 = (f32[384,128]{1,0:T(8,128)}, f32[72,128]{1,0:T(8,128)S(1)}) custom-call(f32[384,128]{1,0:T(8,128)S(1)} %bitcast.23, bf16[256,384]{1,0:T(8,128)(2,1)S(1)} %copy-done.5, f32[72,128]{1,0:T(8,128)S(1)} %get-tuple-element.14.tail), custom_call_target="tpu_custom_call" | custom-call | tf_op jit(solution)/shard_map/pallas_call | solution.py:417
  60.6 6.2 %all-to-all-start.2 = ((f32[128,1,384]{2,1,0:T(1,128)}), f32[128,1,384]{2,1,0:T(1,128)S(1)}, u32[]{:S(2)}, u32[]{:S(2)}) async-start(f32[128,1,384]{2,1,0:T(1,128)} %bitcast.8), calls=%async_computation.2 | async-start | bytes 393216 | tf_op jit(solution)/shard_map/all_to_all | solution.py:331
  66.8 3.5 %collective-permute-start.1 = (f32[72,128]{1,0:T(8,128)S(1)}, f32[72,128]{1,0:T(8,128)S(1)}, u32[]{:S(2)}, u32[]{:S(2)}) collective-permute-start(f32[72,128]{1,0:T(8,128)S(1)} %get-tuple-element.15), channel_id=1, source_target_pairs={{0,4},{4,8},{8,12},{12,16},{16,20},{20,24},{24,28},{28,32},{32,36}... | collective-permute-start | bytes 110600 | tf_op jit(solution)/shard_map/ppermute | solution.py:340
  70.4 1.0 %collective-permute-done.1.tail = f32[72,128]{1,0:T(8,128)S(1)} collective-permute-done((f32[72,128]{1,0:T(8,128)S(1)}, f32[72,128]{1,0:T(8,128)S(1)}, u32[]{:S(2)}, u32[]{:S(2)}) %collective-permute-start.1) | collective-permute-done | bytes 36896 | tf_op jit(solution)/shard_map/ppermute | solution.py:340
  71.4 0.0 copy-start.7
  71.4 0.0 copy-start.8
  71.4 0.7 shard_map.135
  72.2 6.9 %all-to-all-done.2 = f32[128,1,384]{2,1,0:T(1,128)S(1)} async-done(((f32[128,1,384]{2,1,0:T(1,128)}), f32[128,1,384]{2,1,0:T(1,128)S(1)}, u32[]{:S(2)}, u32[]{:S(2)}) %all-to-all-start.2) | async-done | bytes 196640 | tf_op jit(solution)/shard_map/all_to_all | solution.py:331
  79.1 0.0 copy-done.7
  79.1 0.0 copy-done.8
  79.1 1.0 %shard_map.136 = f32[6,2,32,128]{3,2,1,0:T(8,128)} custom-call(f32[16,128]{1,0:T(8,128)S(1)} %broadcast_in_dim.5.facts, f32[384,128]{1,0:T(8,128)S(1)} %bitcast.20, f32[64,64]{1,0:T(8,128)S(1)} %copy-done.8, f32[64,64]{1,0:T(8,128)S(1)} %copy-done.7), custom_call_target="tpu_custom_call" | custom-call | tf_op jit(solution)/shard_map/pallas_call | solution.py:436
  (3 shorter events, 0.0 us)
Async XLA Ops:
  0.6 11.3 %copy-start = (f32[3,3,32,128]{3,2,1,0:T(8,128)S(1)}, f32[3,3,32,128]{3,2,1,0:T(8,128)}, u32[]{:S(2)}) copy-start(f32[3,3,32,128]{3,2,1,0:T(8,128)} %param.11) | copy-start | bytes 442372
  0.6 11.3 %copy-start.1 = (f32[3,3,32,128]{3,2,1,0:T(8,128)S(1)}, f32[3,3,32,128]{3,2,1,0:T(8,128)}, u32[]{:S(2)}) copy-start(f32[3,3,32,128]{3,2,1,0:T(8,128)} %param.12) | copy-start | bytes 442372
  0.7 11.3 %copy-start.2 = (f32[2,3,32,128]{3,2,1,0:T(8,128)S(1)}, f32[2,3,32,128]{3,2,1,0:T(8,128)}, u32[]{:S(2)}) copy-start(f32[2,3,32,128]{3,2,1,0:T(8,128)} %param.13) | copy-start | bytes 294916
  0.7 11.3 %copy-start.4 = (f32[3,32,128]{2,1,0:T(8,128)S(1)}, f32[3,32,128]{2,1,0:T(8,128)}, u32[]{:S(2)}) copy-start(f32[3,32,128]{2,1,0:T(8,128)} %density.5) | copy-start | bytes 147460
  2.3 10.6 %collective-permute-start = (f32[39,8,128]{2,1,0:T(8,128)}, f32[39,8,128]{2,1,0:T(8,128)S(1)}, u32[]{:S(2)}, u32[]{:S(2)}) collective-permute-start(f32[39,8,128]{2,1,0:T(8,128)} %shard_map.130), channel_id=1, source_target_pairs={{0,508},{4,0},{8,4},{12,8},{16,12},{20,16},{24,20},{28,24},{32,28}... | collective-permute-start | bytes 479240 | tf_op jit(solution)/shard_map/ppermute | solution.py:340
  11.1 0.7 copy-start.9
  11.1 0.7 copy-start.10
  11.9 0.7 copy-start.6
  13.0 11.5 %copy-start.3 = (f32[2,3,2,32,128]{4,3,2,1,0:T(8,128)S(1)}, f32[2,3,2,32,128]{4,3,2,1,0:T(8,128)}, u32[]{:S(2)}) copy-start(f32[2,3,2,32,128]{4,3,2,1,0:T(8,128)} %param.15) | copy-start | bytes 589828
  29.2 30.4 %copy-start.5 = (bf16[256,384]{1,0:T(8,128)(2,1)S(1)}, bf16[256,384]{1,0:T(8,128)(2,1)}, u32[]{:S(2)}) copy-start(bf16[256,384]{1,0:T(8,128)(2,1)} %constant.27.clone.table) | copy-start | bytes 589828
  60.6 18.5 %all-to-all-start.2 = ((f32[128,1,384]{2,1,0:T(1,128)}), f32[128,1,384]{2,1,0:T(1,128)S(1)}, u32[]{:S(2)}, u32[]{:S(2)}) async-start(f32[128,1,384]{2,1,0:T(1,128)} %bitcast.8), calls=%async_computation.2 | async-start | bytes 393216 | tf_op jit(solution)/shard_map/all_to_all | solution.py:331
  66.8 4.6 %collective-permute-start.1 = (f32[72,128]{1,0:T(8,128)S(1)}, f32[72,128]{1,0:T(8,128)S(1)}, u32[]{:S(2)}, u32[]{:S(2)}) collective-permute-start(f32[72,128]{1,0:T(8,128)S(1)} %get-tuple-element.15), channel_id=1, source_target_pairs={{0,4},{4,8},{8,12},{12,16},{16,20},{20,24},{24,28},{28,32},{32,36}... | collective-permute-start | bytes 110600 | tf_op jit(solution)/shard_map/ppermute | solution.py:340
  71.4 7.6 %copy-start.7 = (f32[64,64]{1,0:T(8,128)S(1)}, f32[64,64]{1,0:T(8,128)}, u32[]{:S(2)}) copy-start(f32[64,64]{1,0:T(8,128)} %constant.29.clone.turned) | copy-start | bytes 49156
  71.4 7.6 %copy-start.8 = (f32[64,64]{1,0:T(8,128)S(1)}, f32[64,64]{1,0:T(8,128)}, u32[]{:S(2)}) copy-start(f32[64,64]{1,0:T(8,128)} %constant.28.clone.straight) | copy-start | bytes 49156

commit v4 on v3

--- a/solution.py
+++ b/solution.py
@@ -42,19 +42,21 @@
     )
 
 
-def pack_rows_kernel(disp, prev, moduli, density, bins, out, sems):
+def pack_rows_kernel(disp, prev, moduli, density, bins, out, last, sems):
     copies = []
     start = 0
     for n, ref in enumerate((disp, prev, moduli, density, bins)):
-        planes = ref.shape[0]
-        copies.append(
-            pltpu.make_async_copy(ref.at[:, pl.ds(0, EDGE), :], out.at[pl.ds(start, planes)], sems.at[n])
-        )
-        start += planes
+        planes, rows, _ = ref.shape
+        here = out.at[pl.ds(start, planes)] if n < 4 else last
+        copies.append(pltpu.make_async_copy(ref.at[:, pl.ds(rows - EDGE, EDGE), :], here, sems.at[n]))
+        start += planes if n < 4 else 0
     for copy in copies:
         copy.start()
     for copy in copies:
         copy.wait()
+    for n in range(last.shape[0]):
+        at = n % 2 * HALO
+        out[start + n // 2, at : at + HALO, :] = last[n, EDGE - HALO :, :]
 
 
 def pack_main_kernel(disp, prev, moduli, density, select, main):
@@ -65,11 +67,11 @@
     main[:, used:] = jnp.zeros((EDGE, main.shape[1] - used), jnp.float32)
 
 
-def pack_columns_kernel(facts, main, ahead, select, out):
+def pack_columns_kernel(facts, main, behind, select, out):
     peers, _, total = out.shape
     width = main.shape[1]
-    planes = ahead.shape[0] - BINS
-    rows = ahead[:planes].reshape(planes * EDGE, select.shape[1])
+    planes = behind.shape[0] - BINS // 2
+    rows = behind[:planes].reshape(planes * EDGE, select.shape[1])
     fill = jnp.zeros((total - width - rows.shape[0], rows.shape[1]), jnp.float32)
     packed = pick_columns(select, jnp.concatenate([rows, fill], axis=0))
     for slot in range(peers):
@@ -84,21 +86,20 @@
 
 
 def slopes(value, axis, even):
-    step = shift(value, 1, axis) - value
-    before = shift(step, -1, axis)
-    right = jnp.where(even, 3.0 * step - shift(step, 1, axis), step + before)
-    left = shift(3.0 * step - before, -1, axis)
+    ahead, ahead2 = shift(value, 1, axis), shift(value, 2, axis)
+    back, back2 = shift(value, -1, axis), shift(value, -2, axis)
+    right = jnp.where(even, 4.0 * ahead - 3.0 * value - ahead2, ahead - back)
+    left = 3.0 * value - 4.0 * back + back2
     return right, left, jnp.where(even, right + left, right)
 
 
 def spread(right, left, axis, even):
-    left = shift(left, 1, axis)
-    step = jnp.where(
-        even,
-        3.0 * right + shift(right - left, 1, axis),
-        right + 3.0 * left - shift(right, -1, axis),
-    )
-    return shift(step, -1, axis) - step
+    ahead = jnp.where(even, -4.0 * left, -right)
+    back = jnp.where(even, 4.0 * right, right)
+    ahead = ahead + shift(jnp.where(even, left, 0.0), 1, axis)
+    back = back - shift(jnp.where(even, right, 0.0), -1, axis)
+    own = jnp.where(even, 3.0 * (left - right), 0.0)
+    return own + shift(ahead, 1, axis) + shift(back, -1, axis)
 
 
 def spread_z(layers):
@@ -107,7 +108,7 @@
 
 
 def step_kernel(
-    facts, disp, prev, moduli, density, bins, ahead, beside, select,
+    facts, disp, prev, moduli, density, bins, behind, beside, select,
     updated, middle, tail, operand, field, coef, strip, mid,
 ):
     rows, width = disp.shape[1], disp.shape[2]
@@ -131,7 +132,7 @@
         for i in range(ref.shape[0]):
             n = start + i
             field[n, :rows, :width] = ref[i]
-            field[n, rows:, :width] = ahead[n]
+            field[n, rows:, :width] = behind[n]
             field[n, :rows, width:] = strip[n * rows : (n + 1) * rows, :]
             field[n, rows:, width:] = strip[halo_at + n * EDGE : halo_at + (n + 1) * EDGE, :]
         start += ref.shape[0]
@@ -221,22 +222,22 @@
                 total = (forces[c][layer] + along_z[layer]) * for_x(coef[layer, 10])
                 store(n, 2.0 * for_x(source(n)) - for_x(older(n)) - total)
 
-    is_tail = lax.broadcasted_iota(jnp.int32, (EDGE, width), 0) < HALO
+    is_tail = lax.broadcasted_iota(jnp.int32, (EDGE, width), 0) >= HALO
     tops = {}
 
     def keep(ref, n, value):
         ref[n] = value[:rows]
         if n % 3 == 2:
-            first = jnp.where(is_tail, value[rows:], value[:EDGE])
-            tops.setdefault(n // 3, []).append(jnp.concatenate([first, value[EDGE:rows]], axis=0))
+            last = jnp.where(is_tail, value[rows:], value[rows - EDGE : rows])
+            tops.setdefault(n // 3, []).append(jnp.concatenate([value[: rows - EDGE], last], axis=0))
 
     def keep_middle(n, value):
         mid[n] = value
-        tail[(9 + n) * HALO : (10 + n) * HALO, :] = value[rows : rows + HALO, :width]
+        tail[(9 + n) * HALO : (10 + n) * HALO, :] = value[rows + HALO :, :width]
         keep(middle, n, value[:, :width])
 
     def keep_updated(n, value):
-        tail[n * HALO : (n + 1) * HALO, :] = value[rows : rows + HALO]
+        tail[n * HALO : (n + 1) * HALO, :] = value[rows + HALO :]
         keep(updated, n, value)
 
     advance(lambda n: field[n], lambda n: field[9 + n], keep_middle, False)
@@ -251,9 +252,10 @@
             one, two = tops[c]
             item = b * 3 + c
             old = []
-            for n in (2 * item, 2 * item + 1):
-                first = jnp.where(is_tail, ahead[start + n], bins[n, :EDGE])
-                old.append(jnp.concatenate([first, bins[n, EDGE:]], axis=0))
+            rest = behind[start + item]
+            for n, other in ((2 * item, pltpu.roll(rest, HALO, 0)), (2 * item + 1, rest)):
+                last = jnp.where(is_tail, other, bins[n, rows - EDGE :])
+                old.append(jnp.concatenate([bins[n, : rows - EDGE], last], axis=0))
             real = old[0] + cosines[b : b + 1] * one + cosines[2 + b : 3 + b] * two
             imag = old[1] - sines[b : b + 1] * one - sines[2 + b : 3 + b] * two
             if item < 4:
@@ -301,7 +303,7 @@
             imag.append(jnp.where(low, pltpu.roll(one, half, 1), two))
     joined = jnp.concatenate([jnp.concatenate(real, axis=1), jnp.concatenate(imag, axis=1)], axis=0)
     slot = lax.broadcasted_iota(jnp.int32, straight.shape, 1) % rows
-    node = jnp.where(slot < HALO, slot + rows, slot).astype(jnp.float32)
+    node = jnp.where(slot < rows - HALO, slot, slot - rows).astype(jnp.float32)
     place = facts[facts.shape[0] - 1 :, : slot.shape[1]]
     angle = node * place * (2.0 * np.pi / (rows * count))
     matrix = straight[...] * jnp.cos(angle) + turned[...] * jnp.sin(angle)
@@ -321,7 +323,7 @@
     for k, (ref, out) in enumerate(((updated, updated_out), (middle, middle_out))):
         for n in range(ref.shape[0]):
             out[n] = ref[n]
-            out[n, :HALO, :] = tail[(k * ref.shape[0] + n) * HALO : (k * ref.shape[0] + n + 1) * HALO, :]
+            out[n, -HALO:, :] = tail[(k * ref.shape[0] + n) * HALO : (k * ref.shape[0] + n + 1) * HALO, :]
 
 
 def exchange(value):
@@ -373,10 +375,10 @@
 
     edge = pl.pallas_call(
         pack_rows_kernel,
-        out_shape=f32(planes + BINS, EDGE, width),
+        out_shape=f32(planes + BINS // 2, EDGE, width),
         in_specs=[hbm] * 5,
         out_specs=vmem,
-        scratch_shapes=[pltpu.SemaphoreType.DMA((5,))],
+        scratch_shapes=[pltpu.VMEM((BINS, EDGE, width), jnp.float32), pltpu.SemaphoreType.DMA((5,))],
         compiler_params=pltpu.CompilerParams(vmem_limit_bytes=62 * 1024 * 1024),
     )(*arrays)
     main = pl.pallas_call(
@@ -387,14 +389,14 @@
         compiler_params=params,
         cost_estimate=pl.CostEstimate(flops=50_000_000, bytes_accessed=2_000_000, transcendentals=0),
     )(*arrays[:4], select)
-    ahead = pass_on(edge, "gx", -1)
+    behind = pass_on(edge, "gx", 1)
     sides = pl.pallas_call(
         pack_columns_kernel,
         out_shape=f32(peers, HALO, total),
         in_specs=[vmem] * 4,
         out_specs=vmem,
         compiler_params=params,
-    )(facts, main, ahead, select)
+    )(facts, main, behind, select)
     tall, wide = rows + EDGE, 2 * width
     updated, middle, tail, operand = pl.pallas_call(
         step_kernel,
@@ -408,7 +410,7 @@
             pltpu.VMEM((9, tall, wide), jnp.float32),
         ],
         compiler_params=params,
-    )(facts, *arrays, ahead, exchange_gy(sides), select)
+    )(facts, *arrays, behind, exchange_gy(sides), select)
 
     stacked = np.concatenate(fourier_tables(groups), axis=0)
     high = stacked.astype(ml_dtypes.bfloat16)
@@ -428,7 +430,7 @@
         out_specs=(vmem,) * 2,
         compiler_params=params,
         cost_estimate=pl.CostEstimate(flops=1_000_000, bytes_accessed=1_200_000, transcendentals=0),
-    )(updated, middle, pass_on(tail, "gx", 1))
+    )(updated, middle, pass_on(tail, "gx", -1))
     scale = (groups * rows) ** -0.5
     c, s = (t * scale for t in fourier_tables(rows))
     straight = jnp.asarray(np.block([[c, s], [-s, c]]), jnp.float32)

time: 80.4 us -> 78.1 us (0.971)
  starting transfers between devices: 18.6 us -> 13.7 us
  waiting for transfers between devices: 7.94 us -> 12 us
  Pallas kernels: 9.45 us -> 7.93 us
    ppermute x2, waiting for transfers between devices: 1.04 us -> 6.1 us  [pass_on(): lax.ppermute(value, axis, [(i, (i + step) % peers) for i in range(peers)])]
    ppermute x2, starting transfers between devices: 12.3 us -> 7.51 us  [pass_on(): lax.ppermute(value, axis, [(i, (i + step) % peers) for i in range(peers)])]
    all_to_all x1, blocking collectives: 11.3 us -> 9.69 us  [exchange_gy(): return lax.all_to_all(value, 'gy', split_axis=0, concat_axis=0, tiled=True)]
    all_to_all x1, blocking collectives: 30.4 us -> 32 us  [exchange(): lax.all_to_all(shaped, 'gx', split_axis=0, concat_axis=0, tiled=True)]
    pallas_call x1, Pallas kernels: 4.68 us -> 3.17 us  [on_device(): pl.pallas_call(step_kernel, out_shape=(f32(9, *block), f32(9, *block), f3...]
    all_to_all x1, waiting for transfers between devices: 6.9 us -> 5.92 us  [exchange(): lax.all_to_all(shaped, 'gx', split_axis=0, concat_axis=0, tiled=True)]
  transfers between devices with their start and end apart: 3 -> 3, of which waited for: 2 -> 3; matrix products, arithmetic and copies ran while one was open for 0% -> 0% of each run, Pallas kernels for 1% -> 1%
where the time goes in v4:
time: 78.1 us; the launch traced here: 77.7 us
  blocking collectives  41.6 us (53%)
  starting transfers between devices  13.7 us (18%)
  waiting for transfers between devices  12 us (15%)
  Pallas kernels  7.93 us (10%)
  local copies, waits for them, and re-layouts  1.43 us (2%)
    all_to_all x1, blocking collectives, exchange(): lax.all_to_all(shaped, 'gx', split_axis=0, concat_axis=0, tiled=True)  32 us
    all_to_all x1, blocking collectives, exchange_gy(): return lax.all_to_all(value, 'gy', split_axis=0, concat_axis=0, tiled=True)  9.69 us
    ppermute x2, starting transfers between devices, pass_on(): lax.ppermute(value, axis, [(i, (i + step) % peers) for i in range(peers)])  7.51 us
    all_to_all x1, starting transfers between devices, exchange(): lax.all_to_all(shaped, 'gx', split_axis=0, concat_axis=0, tiled=True)  6.22 us
    ppermute x2, waiting for transfers between devices, pass_on(): lax.ppermute(value, axis, [(i, (i + step) % peers) for i in range(peers)])  6.1 us
    all_to_all x1, waiting for transfers between devices, exchange(): lax.all_to_all(shaped, 'gx', split_axis=0, concat_axis=0, tiled=True)  5.92 us
    pallas_call x1, Pallas kernels, on_device(): pl.pallas_call(step_kernel, out_shape=(f32(9, *block), f32(9, *block), f3...  3.17 us
    pallas_call x1, Pallas kernels, on_device(): pl.pallas_call(pack_rows_kernel, out_shape=f32(planes + BINS // 2, EDGE,...  1.63 us
  transfers between devices with their start and end apart: 3, of which 3 were waited for; matrix products, arithmetic and copies ran while one was open for 0% of the time, Pallas kernels for 1%

profile of v4, /device:TPU:1, one launch (start us, length us, event | category | flops | bytes accessed | tf_op | source)
XLA Modules:
  0.0 77.7 jit_solution(7305052467935496771)
XLA Ops:
  0.6 0.0 copy-start
  0.6 0.0 copy-start.1
  0.7 0.0 copy-start.2
  0.7 0.0 copy-start.4
  0.7 1.6 %shard_map.130 = f32[33,8,128]{2,1,0:T(8,128)} custom-call(f32[9,32,128]{2,1,0:T(8,128)} %bitcast.11, f32[9,32,128]{2,1,0:T(8,128)} %bitcast.14, f32[6,32,128]{2,1,0:T(8,128)} %bitcast.17, f32[3,32,128]{2,1,0:T(8,128)} %density.5, f32[12,32,128]{2,1,0:T(8,128)} %bitcast.22), custom_call_target="tpu_custom_call" | custom-call | tf_op jit(solution)/shard_map/pallas_call | solution.py:376
  2.3 4.6 %collective-permute-start = (f32[33,8,128]{2,1,0:T(8,128)}, f32[33,8,128]{2,1,0:T(8,128)S(1)}, u32[]{:S(2)}, u32[]{:S(2)}) collective-permute-start(f32[33,8,128]{2,1,0:T(8,128)} %shard_map.130), channel_id=1, source_target_pairs={{0,4},{4,8},{8,12},{12,16},{16,20},{20,24},{24,28},{28,32},{32,36}... | collective-permute-start | bytes 405512 | tf_op jit(solution)/shard_map/ppermute | solution.py:342
  6.9 0.0 copy-start.9
  6.9 0.0 copy-start.10
  6.9 0.6 copy-done.9
  7.6 0.0 copy-done.10
  7.6 0.1 multiply_add_fusion
  7.7 0.0 copy-start.6
  7.7 0.1 add.22
  7.8 0.0 copy-done
  7.8 0.0 copy-done.1
  7.8 0.0 copy-done.2
  7.8 0.0 copy-done.4
  7.8 0.6 copy-done.6
  8.4 0.2 shard_map.131.main
  8.6 0.1 pad_maximum_fusion
  8.7 3.5 %collective-permute-done.behind = f32[33,8,128]{2,1,0:T(8,128)S(1)} collective-permute-done((f32[33,8,128]{2,1,0:T(8,128)}, f32[33,8,128]{2,1,0:T(8,128)S(1)}, u32[]{:S(2)}, u32[]{:S(2)}) %collective-permute-start) | collective-permute-done | bytes 135200 | tf_op jit(solution)/shard_map/ppermute | solution.py:342
  12.1 0.1 broadcast_in_dim.5.facts
  12.2 0.0 copy-start.3
  12.2 0.2 shard_map.132
  12.4 9.7 %all_to_all.15.beside = f32[4,4,1152]{2,1,0:T(4,128)S(1)} all-to-all(f32[4,4,1152]{2,1,0:T(4,128)S(1)} %shard_map.132), channel_id=1, replica_groups=mesh['gx'=128,'gy'=4] {'gy'}, dimensions={0} | all-to-all | bytes 147456 | tf_op jit(solution)/shard_map/all_to_all | solution.py:337
  22.1 0.0 copy-done.3
  22.1 3.2 %shard_map.133 = (f32[9,32,128]{2,1,0:T(8,128)S(1)}, f32[9,32,128]{2,1,0:T(8,128)S(1)}, f32[72,128]{1,0:T(8,128)S(1)}, f32[384,128]{1,0:T(8,128)S(1)}) custom-call(f32[16,128]{1,0:T(8,128)S(1)} %broadcast_in_dim.5.facts, f32[9,32,128]{2,1,0:T(8,128)S(1)} %bitcast.13, f32[9,32,128]{2,1,0:T(8,128)S(1)} %bitcast.16, f32[6,32,128]{2,1,0:T(8,128)S(1)} %bitcast.19, ...), custom_call_target="tpu_custom_call" | custom-call | tf_op jit(solution)/shard_map/pallas_call | solution.py:401
  25.3 0.0 copy-start.5
  25.3 32.0 %all_to_all.16 = f32[128,1,384]{2,1,0:T(1,128)S(1)} all-to-all(f32[128,1,384]{2,1,0:T(1,128)S(1)} %bitcast.24), channel_id=1, replica_groups=mesh['gx'=128,'gy'=4] {'gx'}, dimensions={0} | all-to-all | bytes 393216 | tf_op jit(solution)/shard_map/all_to_all | solution.py:333
  57.2 0.0 copy-done.5
  57.3 1.0 %shard_map.134 = (f32[384,128]{1,0:T(8,128)}, f32[72,128]{1,0:T(8,128)S(1)}) custom-call(f32[384,128]{1,0:T(8,128)S(1)} %bitcast.21, bf16[256,384]{1,0:T(8,128)(2,1)S(1)} %copy-done.5, f32[72,128]{1,0:T(8,128)S(1)} %get-tuple-element.14.tail), custom_call_target="tpu_custom_call" | custom-call | tf_op jit(solution)/shard_map/pallas_call | solution.py:419
  58.3 6.2 %all-to-all-start.2 = ((f32[128,1,384]{2,1,0:T(1,128)}), f32[128,1,384]{2,1,0:T(1,128)S(1)}, u32[]{:S(2)}, u32[]{:S(2)}) async-start(f32[128,1,384]{2,1,0:T(1,128)} %bitcast.8), calls=%async_computation.2 | async-start | bytes 393216 | tf_op jit(solution)/shard_map/all_to_all | solution.py:333
  64.5 2.9 %collective-permute-start.1 = (f32[72,128]{1,0:T(8,128)S(1)}, f32[72,128]{1,0:T(8,128)S(1)}, u32[]{:S(2)}, u32[]{:S(2)}) collective-permute-start(f32[72,128]{1,0:T(8,128)S(1)} %get-tuple-element.15), channel_id=1, source_target_pairs={{0,508},{4,0},{8,4},{12,8},{16,12},{20,16},{24,20},{28,24},{32,28}... | collective-permute-start | bytes 110600 | tf_op jit(solution)/shard_map/ppermute | solution.py:342
  67.4 2.7 %collective-permute-done.1.tail = f32[72,128]{1,0:T(8,128)S(1)} collective-permute-done((f32[72,128]{1,0:T(8,128)S(1)}, f32[72,128]{1,0:T(8,128)S(1)}, u32[]{:S(2)}, u32[]{:S(2)}) %collective-permute-start.1) | collective-permute-done | bytes 36896 | tf_op jit(solution)/shard_map/ppermute | solution.py:342
  70.1 0.0 copy-start.7
  70.1 0.0 copy-start.8
  70.1 0.7 shard_map.135
  70.8 5.9 %all-to-all-done.2 = f32[128,1,384]{2,1,0:T(1,128)S(1)} async-done(((f32[128,1,384]{2,1,0:T(1,128)}), f32[128,1,384]{2,1,0:T(1,128)S(1)}, u32[]{:S(2)}, u32[]{:S(2)}) %all-to-all-start.2) | async-done | bytes 196640 | tf_op jit(solution)/shard_map/all_to_all | solution.py:333
  76.7 0.0 copy-done.7
  76.7 0.0 copy-done.8
  76.7 1.0 %shard_map.136 = f32[6,2,32,128]{3,2,1,0:T(8,128)} custom-call(f32[16,128]{1,0:T(8,128)S(1)} %broadcast_in_dim.5.facts, f32[384,128]{1,0:T(8,128)S(1)} %bitcast.20, f32[64,64]{1,0:T(8,128)S(1)} %copy-done.8, f32[64,64]{1,0:T(8,128)S(1)} %copy-done.7), custom_call_target="tpu_custom_call" | custom-call | tf_op jit(solution)/shard_map/pallas_call | solution.py:438
  (3 shorter events, 0.0 us)
Async XLA Ops:
  0.6 7.1 %copy-start = (f32[3,3,32,128]{3,2,1,0:T(8,128)S(1)}, f32[3,3,32,128]{3,2,1,0:T(8,128)}, u32[]{:S(2)}) copy-start(f32[3,3,32,128]{3,2,1,0:T(8,128)} %param.11) | copy-start | bytes 442372
  0.6 7.1 %copy-start.1 = (f32[3,3,32,128]{3,2,1,0:T(8,128)S(1)}, f32[3,3,32,128]{3,2,1,0:T(8,128)}, u32[]{:S(2)}) copy-start(f32[3,3,32,128]{3,2,1,0:T(8,128)} %param.12) | copy-start | bytes 442372
  0.7 7.1 %copy-start.2 = (f32[2,3,32,128]{3,2,1,0:T(8,128)S(1)}, f32[2,3,32,128]{3,2,1,0:T(8,128)}, u32[]{:S(2)}) copy-start(f32[2,3,32,128]{3,2,1,0:T(8,128)} %param.13) | copy-start | bytes 294916
  0.7 7.1 %copy-start.4 = (f32[3,32,128]{2,1,0:T(8,128)S(1)}, f32[3,32,128]{2,1,0:T(8,128)}, u32[]{:S(2)}) copy-start(f32[3,32,128]{2,1,0:T(8,128)} %density.5) | copy-start | bytes 147460
  2.3 9.8 %collective-permute-start = (f32[33,8,128]{2,1,0:T(8,128)}, f32[33,8,128]{2,1,0:T(8,128)S(1)}, u32[]{:S(2)}, u32[]{:S(2)}) collective-permute-start(f32[33,8,128]{2,1,0:T(8,128)} %shard_map.130), channel_id=1, source_target_pairs={{0,4},{4,8},{8,12},{12,16},{16,20},{20,24},{24,28},{28,32},{32,36}... | collective-permute-start | bytes 405512 | tf_op jit(solution)/shard_map/ppermute | solution.py:342
  6.9 0.7 copy-start.9
  6.9 0.7 copy-start.10
  7.7 0.7 copy-start.6
  12.2 9.9 %copy-start.3 = (f32[2,3,2,32,128]{4,3,2,1,0:T(8,128)S(1)}, f32[2,3,2,32,128]{4,3,2,1,0:T(8,128)}, u32[]{:S(2)}) copy-start(f32[2,3,2,32,128]{4,3,2,1,0:T(8,128)} %param.15) | copy-start | bytes 589828
  25.3 32.0 %copy-start.5 = (bf16[256,384]{1,0:T(8,128)(2,1)S(1)}, bf16[256,384]{1,0:T(8,128)(2,1)}, u32[]{:S(2)}) copy-start(bf16[256,384]{1,0:T(8,128)(2,1)} %constant.27.clone.table) | copy-start | bytes 589828
  58.3 18.5 %all-to-all-start.2 = ((f32[128,1,384]{2,1,0:T(1,128)}), f32[128,1,384]{2,1,0:T(1,128)S(1)}, u32[]{:S(2)}, u32[]{:S(2)}) async-start(f32[128,1,384]{2,1,0:T(1,128)} %bitcast.8), calls=%async_computation.2 | async-start | bytes 393216 | tf_op jit(solution)/shard_map/all_to_all | solution.py:333
  64.5 5.6 %collective-permute-start.1 = (f32[72,128]{1,0:T(8,128)S(1)}, f32[72,128]{1,0:T(8,128)S(1)}, u32[]{:S(2)}, u32[]{:S(2)}) collective-permute-start(f32[72,128]{1,0:T(8,128)S(1)} %get-tuple-element.15), channel_id=1, source_target_pairs={{0,508},{4,0},{8,4},{12,8},{16,12},{20,16},{24,20},{28,24},{32,28}... | collective-permute-start | bytes 110600 | tf_op jit(solution)/shard_map/ppermute | solution.py:342
  70.1 6.7 %copy-start.7 = (f32[64,64]{1,0:T(8,128)S(1)}, f32[64,64]{1,0:T(8,128)}, u32[]{:S(2)}) copy-start(f32[64,64]{1,0:T(8,128)} %constant.29.clone.turned) | copy-start | bytes 49156
  70.1 6.7 %copy-start.8 = (f32[64,64]{1,0:T(8,128)S(1)}, f32[64,64]{1,0:T(8,128)}, u32[]{:S(2)}) copy-start(f32[64,64]{1,0:T(8,128)} %constant.28.clone.straight) | copy-start | bytes 49156

commit v5 on v4

--- a/solution.py
+++ b/solution.py
@@ -375,11 +375,11 @@
 
     edge = pl.pallas_call(
         pack_rows_kernel,
-        out_shape=f32(planes + BINS // 2, EDGE, width),
+        out_shape=pltpu.VMEM((planes + BINS // 2, EDGE, width), jnp.float32),
         in_specs=[hbm] * 5,
         out_specs=vmem,
         scratch_shapes=[pltpu.VMEM((BINS, EDGE, width), jnp.float32), pltpu.SemaphoreType.DMA((5,))],
-        compiler_params=pltpu.CompilerParams(vmem_limit_bytes=62 * 1024 * 1024),
+        compiler_params=pltpu.CompilerParams(vmem_limit_bytes=60 * 1024 * 1024),
     )(*arrays)
     main = pl.pallas_call(
         pack_main_kernel,

time: 78.1 us -> 77.2 us (0.988)
  no operation moved by 1% of the time
where the time goes in v5:
time: 77.2 us; the launch traced here: 76.8 us
  blocking collectives  41.6 us (54%)
  starting transfers between devices  13.7 us (18%)
  waiting for transfers between devices  11.8 us (15%)
  Pallas kernels  7.24 us (9%)
  local copies, waits for them, and re-layouts  1.43 us (2%)
    all_to_all x1, blocking collectives, exchange(): lax.all_to_all(shaped, 'gx', split_axis=0, concat_axis=0, tiled=True)  32.1 us
    all_to_all x1, blocking collectives, exchange_gy(): return lax.all_to_all(value, 'gy', split_axis=0, concat_axis=0, tiled=True)  9.59 us
    ppermute x2, starting transfers between devices, pass_on(): lax.ppermute(value, axis, [(i, (i + step) % peers) for i in range(peers)])  7.51 us
    all_to_all x1, starting transfers between devices, exchange(): lax.all_to_all(shaped, 'gx', split_axis=0, concat_axis=0, tiled=True)  6.22 us
    all_to_all x1, waiting for transfers between devices, exchange(): lax.all_to_all(shaped, 'gx', split_axis=0, concat_axis=0, tiled=True)  5.92 us
    ppermute x2, waiting for transfers between devices, pass_on(): lax.ppermute(value, axis, [(i, (i + step) % peers) for i in range(peers)])  5.89 us
    pallas_call x1, Pallas kernels, on_device(): pl.pallas_call(step_kernel, out_shape=(f32(9, *block), f32(9, *block), f3...  3.14 us
  transfers between devices with their start and end apart: 3, of which 3 were waited for; matrix products, arithmetic and copies ran while one was open for 0% of the time, Pallas kernels for 1%

profile of v5, /device:TPU:1, one launch (start us, length us, event | category | flops | bytes accessed | tf_op | source)
XLA Modules:
  0.0 76.8 jit_solution(11395443238597888016)
XLA Ops:
  0.6 0.0 copy-start
  0.6 0.0 copy-start.1
  0.7 0.0 copy-start.2
  0.7 0.0 copy-start.4
  0.7 1.0 %shard_map.130 = f32[33,8,128]{2,1,0:T(8,128)S(1)} custom-call(f32[9,32,128]{2,1,0:T(8,128)} %bitcast.11, f32[9,32,128]{2,1,0:T(8,128)} %bitcast.14, f32[6,32,128]{2,1,0:T(8,128)} %bitcast.17, f32[3,32,128]{2,1,0:T(8,128)} %density.5, f32[12,32,128]{2,1,0:T(8,128)} %bitcast.22), custom_call_target="tpu_custom_call" | custom-call | tf_op jit(solution)/shard_map/pallas_call | solution.py:376
  1.7 4.6 %collective-permute-start = (f32[33,8,128]{2,1,0:T(8,128)S(1)}, f32[33,8,128]{2,1,0:T(8,128)S(1)}, u32[]{:S(2)}, u32[]{:S(2)}) collective-permute-start(f32[33,8,128]{2,1,0:T(8,128)S(1)} %shard_map.130), channel_id=1, source_target_pairs={{0,4},{4,8},{8,12},{12,16},{16,20},{20,24},{24,28},{28,32},{32,36}... | collective-permute-start | bytes 405512 | tf_op jit(solution)/shard_map/ppermute | solution.py:342
  6.3 0.0 copy-start.9
  6.3 0.0 copy-start.10
  6.3 0.6 copy-done.9
  6.9 0.0 copy-done.10
  6.9 0.1 multiply_add_fusion
  7.0 0.0 copy-start.6
  7.0 0.1 add.22
  7.1 0.0 copy-done
  7.1 0.0 copy-done.1
  7.1 0.0 copy-done.2
  7.1 0.0 copy-done.4
  7.1 0.6 copy-done.6
  7.7 0.2 shard_map.131.main
  7.9 0.1 pad_maximum_fusion
  8.0 3.2 %collective-permute-done.behind = f32[33,8,128]{2,1,0:T(8,128)S(1)} collective-permute-done((f32[33,8,128]{2,1,0:T(8,128)S(1)}, f32[33,8,128]{2,1,0:T(8,128)S(1)}, u32[]{:S(2)}, u32[]{:S(2)}) %collective-permute-start) | collective-permute-done | bytes 135200 | tf_op jit(solution)/shard_map/ppermute | solution.py:342
  11.3 0.1 broadcast_in_dim.5.facts
  11.3 0.0 copy-start.3
  11.4 0.2 shard_map.132
  11.5 9.6 %all_to_all.15.beside = f32[4,4,1152]{2,1,0:T(4,128)S(1)} all-to-all(f32[4,4,1152]{2,1,0:T(4,128)S(1)} %shard_map.132), channel_id=1, replica_groups=mesh['gx'=128,'gy'=4] {'gy'}, dimensions={0} | all-to-all | bytes 147456 | tf_op jit(solution)/shard_map/all_to_all | solution.py:337
  21.1 0.0 copy-done.3
  21.1 3.1 %shard_map.133 = (f32[9,32,128]{2,1,0:T(8,128)S(1)}, f32[9,32,128]{2,1,0:T(8,128)S(1)}, f32[72,128]{1,0:T(8,128)S(1)}, f32[384,128]{1,0:T(8,128)S(1)}) custom-call(f32[16,128]{1,0:T(8,128)S(1)} %broadcast_in_dim.5.facts, f32[9,32,128]{2,1,0:T(8,128)S(1)} %bitcast.13, f32[9,32,128]{2,1,0:T(8,128)S(1)} %bitcast.16, f32[6,32,128]{2,1,0:T(8,128)S(1)} %bitcast.19, ...), custom_call_target="tpu_custom_call" | custom-call | tf_op jit(solution)/shard_map/pallas_call | solution.py:401
  24.3 0.0 copy-start.5
  24.3 32.1 %all_to_all.16 = f32[128,1,384]{2,1,0:T(1,128)S(1)} all-to-all(f32[128,1,384]{2,1,0:T(1,128)S(1)} %bitcast.24), channel_id=1, replica_groups=mesh['gx'=128,'gy'=4] {'gx'}, dimensions={0} | all-to-all | bytes 393216 | tf_op jit(solution)/shard_map/all_to_all | solution.py:333
  56.3 0.0 copy-done.5
  56.3 1.0 %shard_map.134 = (f32[384,128]{1,0:T(8,128)}, f32[72,128]{1,0:T(8,128)S(1)}) custom-call(f32[384,128]{1,0:T(8,128)S(1)} %bitcast.21, bf16[256,384]{1,0:T(8,128)(2,1)S(1)} %copy-done.5, f32[72,128]{1,0:T(8,128)S(1)} %get-tuple-element.14.tail), custom_call_target="tpu_custom_call" | custom-call | tf_op jit(solution)/shard_map/pallas_call | solution.py:419
  57.4 6.2 %all-to-all-start.2 = ((f32[128,1,384]{2,1,0:T(1,128)}), f32[128,1,384]{2,1,0:T(1,128)S(1)}, u32[]{:S(2)}, u32[]{:S(2)}) async-start(f32[128,1,384]{2,1,0:T(1,128)} %bitcast.8), calls=%async_computation.2 | async-start | bytes 393216 | tf_op jit(solution)/shard_map/all_to_all | solution.py:333
  63.6 2.9 %collective-permute-start.1 = (f32[72,128]{1,0:T(8,128)S(1)}, f32[72,128]{1,0:T(8,128)S(1)}, u32[]{:S(2)}, u32[]{:S(2)}) collective-permute-start(f32[72,128]{1,0:T(8,128)S(1)} %get-tuple-element.15), channel_id=1, source_target_pairs={{0,508},{4,0},{8,4},{12,8},{16,12},{20,16},{24,20},{28,24},{32,28}... | collective-permute-start | bytes 110600 | tf_op jit(solution)/shard_map/ppermute | solution.py:342
  66.5 2.7 %collective-permute-done.1.tail = f32[72,128]{1,0:T(8,128)S(1)} collective-permute-done((f32[72,128]{1,0:T(8,128)S(1)}, f32[72,128]{1,0:T(8,128)S(1)}, u32[]{:S(2)}, u32[]{:S(2)}) %collective-permute-start.1) | collective-permute-done | bytes 36896 | tf_op jit(solution)/shard_map/ppermute | solution.py:342
  69.2 0.0 copy-start.7
  69.2 0.0 copy-start.8
  69.2 0.7 shard_map.135
  69.9 5.9 %all-to-all-done.2 = f32[128,1,384]{2,1,0:T(1,128)S(1)} async-done(((f32[128,1,384]{2,1,0:T(1,128)}), f32[128,1,384]{2,1,0:T(1,128)S(1)}, u32[]{:S(2)}, u32[]{:S(2)}) %all-to-all-start.2) | async-done | bytes 196640 | tf_op jit(solution)/shard_map/all_to_all | solution.py:333
  75.8 0.0 copy-done.7
  75.8 0.0 copy-done.8
  75.8 1.0 %shard_map.136 = f32[6,2,32,128]{3,2,1,0:T(8,128)} custom-call(f32[16,128]{1,0:T(8,128)S(1)} %broadcast_in_dim.5.facts, f32[384,128]{1,0:T(8,128)S(1)} %bitcast.20, f32[64,64]{1,0:T(8,128)S(1)} %copy-done.8, f32[64,64]{1,0:T(8,128)S(1)} %copy-done.7), custom_call_target="tpu_custom_call" | custom-call | tf_op jit(solution)/shard_map/pallas_call | solution.py:438
  (3 shorter events, 0.0 us)
Async XLA Ops:
  0.6 6.5 %copy-start = (f32[3,3,32,128]{3,2,1,0:T(8,128)S(1)}, f32[3,3,32,128]{3,2,1,0:T(8,128)}, u32[]{:S(2)}) copy-start(f32[3,3,32,128]{3,2,1,0:T(8,128)} %param.11) | copy-start | bytes 442372
  0.6 6.5 %copy-start.1 = (f32[3,3,32,128]{3,2,1,0:T(8,128)S(1)}, f32[3,3,32,128]{3,2,1,0:T(8,128)}, u32[]{:S(2)}) copy-start(f32[3,3,32,128]{3,2,1,0:T(8,128)} %param.12) | copy-start | bytes 442372
  0.7 6.5 %copy-start.2 = (f32[2,3,32,128]{3,2,1,0:T(8,128)S(1)}, f32[2,3,32,128]{3,2,1,0:T(8,128)}, u32[]{:S(2)}) copy-start(f32[2,3,32,128]{3,2,1,0:T(8,128)} %param.13) | copy-start | bytes 294916
  0.7 6.5 %copy-start.4 = (f32[3,32,128]{2,1,0:T(8,128)S(1)}, f32[3,32,128]{2,1,0:T(8,128)}, u32[]{:S(2)}) copy-start(f32[3,32,128]{2,1,0:T(8,128)} %density.5) | copy-start | bytes 147460
  1.7 9.6 %collective-permute-start = (f32[33,8,128]{2,1,0:T(8,128)S(1)}, f32[33,8,128]{2,1,0:T(8,128)S(1)}, u32[]{:S(2)}, u32[]{:S(2)}) collective-permute-start(f32[33,8,128]{2,1,0:T(8,128)S(1)} %shard_map.130), channel_id=1, source_target_pairs={{0,4},{4,8},{8,12},{12,16},{16,20},{20,24},{24,28},{28,32},{32,36}... | collective-permute-start | bytes 405512 | tf_op jit(solution)/shard_map/ppermute | solution.py:342
  6.3 0.7 copy-start.9
  6.3 0.7 copy-start.10
  7.0 0.7 copy-start.6
  11.3 9.8 %copy-start.3 = (f32[2,3,2,32,128]{4,3,2,1,0:T(8,128)S(1)}, f32[2,3,2,32,128]{4,3,2,1,0:T(8,128)}, u32[]{:S(2)}) copy-start(f32[2,3,2,32,128]{4,3,2,1,0:T(8,128)} %param.15) | copy-start | bytes 589828
  24.3 32.1 %copy-start.5 = (bf16[256,384]{1,0:T(8,128)(2,1)S(1)}, bf16[256,384]{1,0:T(8,128)(2,1)}, u32[]{:S(2)}) copy-start(bf16[256,384]{1,0:T(8,128)(2,1)} %constant.27.clone.table) | copy-start | bytes 589828
  57.4 18.5 %all-to-all-start.2 = ((f32[128,1,384]{2,1,0:T(1,128)}), f32[128,1,384]{2,1,0:T(1,128)S(1)}, u32[]{:S(2)}, u32[]{:S(2)}) async-start(f32[128,1,384]{2,1,0:T(1,128)} %bitcast.8), calls=%async_computation.2 | async-start | bytes 393216 | tf_op jit(solution)/shard_map/all_to_all | solution.py:333
  63.6 5.6 %collective-permute-start.1 = (f32[72,128]{1,0:T(8,128)S(1)}, f32[72,128]{1,0:T(8,128)S(1)}, u32[]{:S(2)}, u32[]{:S(2)}) collective-permute-start(f32[72,128]{1,0:T(8,128)S(1)} %get-tuple-element.15), channel_id=1, source_target_pairs={{0,508},{4,0},{8,4},{12,8},{16,12},{20,16},{24,20},{28,24},{32,28}... | collective-permute-start | bytes 110600 | tf_op jit(solution)/shard_map/ppermute | solution.py:342
  69.2 6.7 %copy-start.7 = (f32[64,64]{1,0:T(8,128)S(1)}, f32[64,64]{1,0:T(8,128)}, u32[]{:S(2)}) copy-start(f32[64,64]{1,0:T(8,128)} %constant.29.clone.turned) | copy-start | bytes 49156
  69.2 6.7 %copy-start.8 = (f32[64,64]{1,0:T(8,128)S(1)}, f32[64,64]{1,0:T(8,128)}, u32[]{:S(2)}) copy-start(f32[64,64]{1,0:T(8,128)} %constant.28.clone.straight) | copy-start | bytes 49156

commit v6 on v5

--- a/solution.py
+++ b/solution.py
@@ -42,43 +42,67 @@
     )
 
 
-def pack_rows_kernel(disp, prev, moduli, density, bins, out, last, sems):
+def row_tiles(whole):
+    planes, rows, width = whole.shape
+    return jnp.concatenate(
+        [whole[:, at : at + EDGE].reshape(planes * EDGE, width) for at in range(0, rows, EDGE)], axis=0
+    )
+
+
+def pack_columns_kernel(disp, prev, moduli, density, masks, select, out, whole, sems):
     copies = []
     start = 0
-    for n, ref in enumerate((disp, prev, moduli, density, bins)):
-        planes, rows, _ = ref.shape
-        here = out.at[pl.ds(start, planes)] if n < 4 else last
-        copies.append(pltpu.make_async_copy(ref.at[:, pl.ds(rows - EDGE, EDGE), :], here, sems.at[n]))
-        start += planes if n < 4 else 0
+    for n, ref in enumerate((disp, prev, moduli, density)):
+        copies.append(pltpu.make_async_copy(ref, whole.at[pl.ds(start, ref.shape[0])], sems.at[n]))
+        start += ref.shape[0]
     for copy in copies:
         copy.start()
     for copy in copies:
         copy.wait()
-    for n in range(last.shape[0]):
-        at = n % 2 * HALO
-        out[start + n // 2, at : at + HALO, :] = last[n, EDGE - HALO :, :]
-
-
-def pack_main_kernel(disp, prev, moduli, density, select, main):
-    width = select.shape[1]
-    whole = jnp.concatenate([ref[...].reshape(-1, width) for ref in (disp, prev, moduli, density)], axis=0)
-    used = whole.shape[0]
-    main[:, :used] = pick_columns(select, whole)
-    main[:, used:] = jnp.zeros((EDGE, main.shape[1] - used), jnp.float32)
-
-
-def pack_columns_kernel(facts, main, behind, select, out):
     peers, _, total = out.shape
-    width = main.shape[1]
-    planes = behind.shape[0] - BINS // 2
-    rows = behind[:planes].reshape(planes * EDGE, select.shape[1])
-    fill = jnp.zeros((total - width - rows.shape[0], rows.shape[1]), jnp.float32)
+    rows = row_tiles(whole[...])
+    fill = jnp.zeros((total - rows.shape[0], rows.shape[1]), jnp.float32)
     packed = pick_columns(select, jnp.concatenate([rows, fill], axis=0))
     for slot in range(peers):
-        after, before = (facts[n : n + 1, :1] > 0.5 for n in (slot, peers + slot))
-        for source, at in ((main[...], 0), (packed, width)):
-            chosen = jnp.where(after, source[HALO:], jnp.where(before, source[:HALO], 0.0))
-            out[slot, :, at : at + source.shape[1]] = chosen
+        after, before = (masks[n : n + 1, :1] > 0.5 for n in (slot, peers + slot))
+        out[slot] = jnp.where(after, packed[HALO:], jnp.where(before, packed[:HALO], 0.0))
+
+
+def both_sides(masks, beside):
+    peers = beside.shape[0]
+    east = west = beside[0]
+    for slot in range(1, peers):
+        east = jnp.where(masks[slot : slot + 1, :1] > 0.5, beside[slot], east)
+        west = jnp.where(masks[peers + slot : peers + slot + 1, :1] > 0.5, beside[slot], west)
+    return jnp.concatenate([east, west], axis=0)
+
+
+def place_columns(both, select):
+    chosen = select[...].astype(jnp.bfloat16)
+    return lax.dot_general(
+        jnp.concatenate(halves(both), axis=0),
+        jnp.concatenate([chosen, chosen], axis=0),
+        (((0,), (0,)), ((), ())),
+        preferred_element_type=jnp.float32,
+    )
+
+
+def pack_rows_kernel(disp, prev, moduli, density, bins, masks, beside, out):
+    start = 0
+    for ref in (disp, prev, moduli, density):
+        for i in range(ref.shape[0]):
+            out[start + i] = ref[i, -EDGE:, :]
+        start += ref.shape[0]
+    for n in range(BINS):
+        at = n % 2 * HALO
+        out[start + n // 2, at : at + HALO, :] = bins[n, -HALO:, :]
+    width = out.shape[2]
+    both = both_sides(masks, beside)
+    first = start * (disp.shape[1] - EDGE)
+    base = first // width * width
+    corner = pltpu.roll(both[:, base : base + 2 * width], 2 * width - (first - base), 1)
+    out[start + BINS // 2] = corner[:, :width]
+    out[start + BINS // 2 + 1] = corner[:, width:]
 
 
 def shift(value, amount, axis):
@@ -107,35 +131,9 @@
     return c - b - 3.0 * a, 4.0 * (a - c), b - a + 3.0 * c
 
 
-def step_kernel(
-    facts, disp, prev, moduli, density, bins, behind, beside, select,
-    updated, middle, tail, operand, field, coef, strip, mid,
-):
-    rows, width = disp.shape[1], disp.shape[2]
-    tall, wide = rows + EDGE, 2 * width
-    peers = beside.shape[0]
-    halo_at = beside.shape[2] - 2 * width
-    east = west = beside[0]
-    for slot in range(1, peers):
-        east = jnp.where(facts[slot : slot + 1, :1] > 0.5, beside[slot], east)
-        west = jnp.where(facts[peers + slot : peers + slot + 1, :1] > 0.5, beside[slot], west)
-    both = jnp.concatenate([east, west], axis=0)
-    chosen = select[...].astype(jnp.bfloat16)
-    strip[...] = lax.dot_general(
-        jnp.concatenate(halves(both), axis=0),
-        jnp.concatenate([chosen, chosen], axis=0),
-        (((0,), (0,)), ((), ())),
-        preferred_element_type=jnp.float32,
-    )
-    start = 0
-    for ref in (disp, prev, moduli, density):
-        for i in range(ref.shape[0]):
-            n = start + i
-            field[n, :rows, :width] = ref[i]
-            field[n, rows:, :width] = behind[n]
-            field[n, :rows, width:] = strip[n * rows : (n + 1) * rows, :]
-            field[n, rows:, width:] = strip[halo_at + n * EDGE : halo_at + (n + 1) * EDGE, :]
-        start += ref.shape[0]
+def two_steps(field, coef, mid, keep_middle, keep_updated):
+    _, tall, wide = field.shape
+    width = wide // 2
 
     def tiled(tile, shape=(tall, wide)):
         line = jnp.concatenate([tile] * (shape[1] // tile.shape[1]), axis=1)
@@ -222,28 +220,70 @@
                 total = (forces[c][layer] + along_z[layer]) * for_x(coef[layer, 10])
                 store(n, 2.0 * for_x(source(n)) - for_x(older(n)) - total)
 
-    is_tail = lax.broadcasted_iota(jnp.int32, (EDGE, width), 0) >= HALO
-    tops = {}
-
-    def keep(ref, n, value):
-        ref[n] = value[:rows]
-        if n % 3 == 2:
-            last = jnp.where(is_tail, value[rows:], value[rows - EDGE : rows])
-            tops.setdefault(n // 3, []).append(jnp.concatenate([value[: rows - EDGE], last], axis=0))
+    advance(lambda n: field[n], lambda n: field[9 + n], keep_middle, False)
+    advance(lambda n: mid[n], lambda n: field[n], keep_updated, True)
+
+
+def own_rows_kernel(masks, disp, prev, moduli, density, beside, select, updated, middle, head, field, coef, strip, mid):
+    rows, width = disp.shape[1], disp.shape[2]
+    strip[...] = place_columns(both_sides(masks, beside), select)
+    planes = field.shape[0]
+    start = 0
+    for ref in (disp, prev, moduli, density):
+        for i in range(ref.shape[0]):
+            n = start + i
+            field[n, :, :width] = ref[i]
+            for tile in range(rows // EDGE):
+                at = (tile * planes + n) * EDGE
+                field[n, tile * EDGE : (tile + 1) * EDGE, width:] = strip[at : at + EDGE, :]
+            head[n] = field[n, :EDGE, :]
+        start += ref.shape[0]
 
     def keep_middle(n, value):
         mid[n] = value
-        tail[(9 + n) * HALO : (10 + n) * HALO, :] = value[rows + HALO :, :width]
-        keep(middle, n, value[:, :width])
+        middle[n] = value[:, :width]
 
     def keep_updated(n, value):
-        tail[n * HALO : (n + 1) * HALO, :] = value[rows + HALO :]
-        keep(updated, n, value)
-
-    advance(lambda n: field[n], lambda n: field[9 + n], keep_middle, False)
-    advance(lambda n: mid[n], lambda n: field[n], keep_updated, True)
-
-    angles = facts[2 * peers : 2 * peers + 8]
+        updated[n] = value
+
+    two_steps(field, coef, mid, keep_middle, keep_updated)
+
+
+def joint_rows_kernel(
+    facts, updated, middle, head, behind, bins, select, near, tail, operand, field, coef, mid,
+):
+    rows, width = updated.shape[1], updated.shape[2]
+    planes = field.shape[0]
+    corner = jnp.concatenate([behind[planes + BINS // 2], behind[planes + BINS // 2 + 1]], axis=1)
+    strip = place_columns(corner, select)
+    for n in range(planes):
+        field[n, :EDGE, :] = head[n]
+        field[n, EDGE:, :width] = behind[n]
+        field[n, EDGE:, width:] = strip[n * EDGE : (n + 1) * EDGE]
+    is_near = lax.broadcasted_iota(jnp.int32, (EDGE, width), 0) < HALO
+    tops = {}
+
+    def keep(k, whole, n, value):
+        near[k * 9 + n] = value[:EDGE]
+        at = (k * 9 + n) * HALO
+        tail[at : at + HALO, :] = value[EDGE + HALO :]
+        if n % 3 == 2:
+            first = jnp.where(is_near, value[:EDGE], whole[n, :EDGE, :])
+            last = jnp.where(is_near, whole[n, rows - EDGE :, :], value[EDGE:])
+            tops.setdefault(n // 3, []).append(
+                jnp.concatenate([first, whole[n, EDGE : rows - EDGE, :], last], axis=0)
+            )
+
+    def keep_middle(n, value):
+        mid[n] = value
+        keep(1, middle, n, value[:, :width])
+
+    def keep_updated(n, value):
+        keep(0, updated, n, value)
+
+    two_steps(field, coef, mid, keep_middle, keep_updated)
+
+    angles = facts[EDGE:]
     cosines, sines = jnp.cos(angles), jnp.sin(angles)
     low = lax.broadcasted_iota(jnp.int32, (rows, width), 1) < width // 2
     half = width // 2
@@ -252,9 +292,9 @@
             one, two = tops[c]
             item = b * 3 + c
             old = []
-            rest = behind[start + item]
+            rest = behind[planes + item]
             for n, other in ((2 * item, pltpu.roll(rest, HALO, 0)), (2 * item + 1, rest)):
-                last = jnp.where(is_tail, other, bins[n, rows - EDGE :])
+                last = jnp.where(is_near, bins[n, rows - EDGE :], other)
                 old.append(jnp.concatenate([bins[n, : rows - EDGE], last], axis=0))
             real = old[0] + cosines[b : b + 1] * one + cosines[2 + b : 3 + b] * two
             imag = old[1] - sines[b : b + 1] * one - sines[2 + b : 3 + b] * two
@@ -319,11 +359,13 @@
             out[item, part] = waves[part * rows : (part + 1) * rows, item * width : (item + 1) * width]
 
 
-def set_in_kernel(updated, middle, tail, updated_out, middle_out):
+def set_in_kernel(updated, middle, near, tail, updated_out, middle_out):
     for k, (ref, out) in enumerate(((updated, updated_out), (middle, middle_out))):
         for n in range(ref.shape[0]):
-            out[n] = ref[n]
-            out[n, -HALO:, :] = tail[(k * ref.shape[0] + n) * HALO : (k * ref.shape[0] + n + 1) * HALO, :]
+            at = k * ref.shape[0] + n
+            out[n, HALO:-HALO, :] = ref[n, HALO:-HALO, :]
+            out[n, :HALO, :] = near[at, :HALO, :]
+            out[n, -HALO:, :] = tail[at * HALO : (at + 1) * HALO, :]
 
 
 def exchange(value):
@@ -354,63 +396,66 @@
     arrays = [a.reshape((-1,) + block) for a in (displacement, previous, moduli, density, bins)]
     planes = sum(a.shape[0] for a in arrays) - BINS
     packed = -(-planes * rows // width) * width
-    total = packed + 2 * width
     select = jnp.asarray(edge_columns(width))
     peers = lax.axis_size("gy")
     distance = jnp.arange(peers) - lax.axis_index("gy")
+    masks = jnp.concatenate(
+        [(distance == 1) | (distance == 1 - peers), (distance == -1) | (distance == peers - 1)]
+    )
+    masks = masks.astype(jnp.float32)
     steps = jnp.arange(1, 3).astype(jnp.float32)
-    facts = jnp.concatenate(
-        [
-            (distance == 1) | (distance == 1 - peers),
-            (distance == -1) | (distance == peers - 1),
-            (phase[None, :] + steps[:, None] * omega[None, :]).reshape(-1),
-            jnp.full((4,), lax.axis_index("gx")),
-        ],
-        dtype=jnp.float32,
-    )
+    angles = (phase[None, :] + steps[:, None] * omega[None, :]).reshape(-1)
+    facts = jnp.concatenate([masks, angles, jnp.full((4,), lax.axis_index("gx"))], dtype=jnp.float32)
     facts = jnp.broadcast_to(facts[:, None], (facts.shape[0], width))
+    masks = jnp.broadcast_to(masks[:, None], (2 * peers, width))
     vmem = pl.BlockSpec(memory_space=pltpu.VMEM)
     hbm = pl.BlockSpec(memory_space=pltpu.HBM)
     params = pltpu.CompilerParams(vmem_limit_bytes=48 * 1024 * 1024)
-
+    wide = 2 * width
+
+    sides = pl.pallas_call(
+        pack_columns_kernel,
+        out_shape=pltpu.VMEM((peers, HALO, packed), jnp.float32),
+        in_specs=[hbm] * 4 + [vmem] * 2,
+        out_specs=vmem,
+        scratch_shapes=[pltpu.VMEM((planes,) + block, jnp.float32), pltpu.SemaphoreType.DMA((4,))],
+        compiler_params=pltpu.CompilerParams(vmem_limit_bytes=60 * 1024 * 1024),
+    )(*arrays[:4], masks, select)
+    beside = exchange_gy(sides)
     edge = pl.pallas_call(
         pack_rows_kernel,
-        out_shape=pltpu.VMEM((planes + BINS // 2, EDGE, width), jnp.float32),
-        in_specs=[hbm] * 5,
-        out_specs=vmem,
-        scratch_shapes=[pltpu.VMEM((BINS, EDGE, width), jnp.float32), pltpu.SemaphoreType.DMA((5,))],
-        compiler_params=pltpu.CompilerParams(vmem_limit_bytes=60 * 1024 * 1024),
-    )(*arrays)
-    main = pl.pallas_call(
-        pack_main_kernel,
-        out_shape=f32(EDGE, packed),
-        in_specs=[vmem] * 5,
+        out_shape=f32(planes + BINS // 2 + 2, EDGE, width),
+        in_specs=[vmem] * 7,
         out_specs=vmem,
         compiler_params=params,
-        cost_estimate=pl.CostEstimate(flops=50_000_000, bytes_accessed=2_000_000, transcendentals=0),
-    )(*arrays[:4], select)
+    )(*arrays, facts, beside)
     behind = pass_on(edge, "gx", 1)
-    sides = pl.pallas_call(
-        pack_columns_kernel,
-        out_shape=f32(peers, HALO, total),
-        in_specs=[vmem] * 4,
-        out_specs=vmem,
-        compiler_params=params,
-    )(facts, main, behind, select)
-    tall, wide = rows + EDGE, 2 * width
-    updated, middle, tail, operand = pl.pallas_call(
-        step_kernel,
-        out_shape=(f32(9, *block), f32(9, *block), f32(18 * HALO, width), f32(3 * groups, width)),
-        in_specs=[vmem] * 9,
-        out_specs=(vmem,) * 4,
+    updated, middle, head = pl.pallas_call(
+        own_rows_kernel,
+        out_shape=(f32(9, *block), f32(9, *block), f32(planes, EDGE, wide)),
+        in_specs=[vmem] * 7,
+        out_specs=(vmem,) * 3,
         scratch_shapes=[
-            pltpu.VMEM((planes, tall, wide), jnp.float32),
-            pltpu.VMEM((3, 11, tall, wide), jnp.float32),
-            pltpu.VMEM((total, width), jnp.float32),
-            pltpu.VMEM((9, tall, wide), jnp.float32),
+            pltpu.VMEM((planes, rows, wide), jnp.float32),
+            pltpu.VMEM((3, 11, rows, wide), jnp.float32),
+            pltpu.VMEM((packed, width), jnp.float32),
+            pltpu.VMEM((9, rows, wide), jnp.float32),
         ],
         compiler_params=params,
-    )(facts, *arrays, behind, exchange_gy(sides), select)
+        cost_estimate=pl.CostEstimate(flops=50_000_000, bytes_accessed=2_000_000, transcendentals=0),
+    )(facts, *arrays[:4], beside, select)
+    near, tail, operand = pl.pallas_call(
+        joint_rows_kernel,
+        out_shape=(f32(18, EDGE, width), f32(18 * HALO, width), f32(3 * groups, width)),
+        in_specs=[vmem] * 7,
+        out_specs=(vmem,) * 3,
+        scratch_shapes=[
+            pltpu.VMEM((planes, 2 * EDGE, wide), jnp.float32),
+            pltpu.VMEM((3, 11, 2 * EDGE, wide), jnp.float32),
+            pltpu.VMEM((9, 2 * EDGE, wide), jnp.float32),
+        ],
+        compiler_params=params,
+    )(facts, updated, middle, head, behind, arrays[4], select)
 
     stacked = np.concatenate(fourier_tables(groups), axis=0)
     high = stacked.astype(ml_dtypes.bfloat16)
@@ -426,11 +471,11 @@
     updated, middle = pl.pallas_call(
         set_in_kernel,
         out_shape=(f32(9, *block), f32(9, *block)),
-        in_specs=[vmem] * 3,
+        in_specs=[vmem] * 4,
         out_specs=(vmem,) * 2,
         compiler_params=params,
         cost_estimate=pl.CostEstimate(flops=1_000_000, bytes_accessed=1_200_000, transcendentals=0),
-    )(updated, middle, pass_on(tail, "gx", -1))
+    )(updated, middle, near, pass_on(tail, "gx", -1))
     scale = (groups * rows) ** -0.5
     c, s = (t * scale for t in fourier_tables(rows))
     straight = jnp.asarray(np.block([[c, s], [-s, c]]), jnp.float32)

time: 77.2 us -> 78.5 us (1.017)
  blocking collectives: 41.6 us -> 29.8 us
  starting transfers between devices: 13.7 us -> 21.4 us
  waiting for transfers between devices: 11.8 us -> 15.2 us
  Pallas kernels: 7.24 us -> 9.8 us
    all_to_all x1 -> x0, blocking collectives: 9.59 us -> none  [exchange_gy(): return lax.all_to_all(value, 'gy', split_axis=0, concat_axis=0, tiled=True)]
    all_to_all x0 -> x1, starting transfers between devices: none -> 7.79 us  [exchange_gy(): return lax.all_to_all(value, 'gy', split_axis=0, concat_axis=0, tiled=True)]
    all_to_all x0 -> x1, waiting for transfers between devices: none -> 6.58 us  [exchange_gy(): return lax.all_to_all(value, 'gy', split_axis=0, concat_axis=0, tiled=True)]
    ppermute x2, waiting for transfers between devices: 5.89 us -> 2.65 us  [pass_on(): lax.ppermute(value, axis, [(i, (i + step) % peers) for i in range(peers)])]
    pallas_call x4, Pallas kernels: 4.52 us -> 7.1 us  [the longest x1 2.74 us: on_device(): pl.pallas_call(pack_columns_kernel, out_shape=pltpu.VMEM((peers, HALO, pa...]
    all_to_all x1, blocking collectives: 32.1 us -> 29.8 us  [exchange(): lax.all_to_all(shaped, 'gx', split_axis=0, concat_axis=0, tiled=True)]
    unnamed x22, local copies, waits for them, and re-layouts: 1.28 us -> 0.05 us
  transfers between devices with their start and end apart: 3 -> 4, of which waited for: 3 -> 3; matrix products, arithmetic and copies ran while one was open for 0% -> 0% of each run, Pallas kernels for 1% -> 4%
where the time goes in v6:
time: 78.5 us; the launch traced here: 78 us
  blocking collectives  29.8 us (38%)
  starting transfers between devices  21.4 us (27%)
  waiting for transfers between devices  15.2 us (19%)
  Pallas kernels  9.8 us (12%)
  local copies, waits for them, and re-layouts  0.87 us (1%)
  between operations  0.79 us (1%)
    all_to_all x1, blocking collectives, exchange(): lax.all_to_all(shaped, 'gx', split_axis=0, concat_axis=0, tiled=True)  29.8 us
    all_to_all x1, starting transfers between devices, exchange_gy(): return lax.all_to_all(value, 'gy', split_axis=0, concat_axis=0, tiled=True)  7.79 us
    ppermute x2, starting transfers between devices, pass_on(): lax.ppermute(value, axis, [(i, (i + step) % peers) for i in range(peers)])  7.36 us
    all_to_all x1, waiting for transfers between devices, exchange_gy(): return lax.all_to_all(value, 'gy', split_axis=0, concat_axis=0, tiled=True)  6.58 us
    all_to_all x1, starting transfers between devices, exchange(): lax.all_to_all(shaped, 'gx', split_axis=0, concat_axis=0, tiled=True)  6.23 us
    all_to_all x1, waiting for transfers between devices, exchange(): lax.all_to_all(shaped, 'gx', split_axis=0, concat_axis=0, tiled=True)  5.92 us
    pallas_call x1, Pallas kernels, on_device(): pl.pallas_call(pack_columns_kernel, out_shape=pltpu.VMEM((peers, HALO, pa...  2.74 us
    pallas_call x1, Pallas kernels, on_device(): pl.pallas_call(own_rows_kernel, out_shape=(f32(9, *block), f32(9, *block)...  2.69 us
  transfers between devices with their start and end apart: 4, of which 3 were waited for; matrix products, arithmetic and copies ran while one was open for 0% of the time, Pallas kernels for 4%

profile of v6, /device:TPU:1, one launch (start us, length us, event | category | flops | bytes accessed | tf_op | source)
XLA Modules:
  0.0 78.0 jit_solution(9660711690641793732)
XLA Ops:
  0.6 0.1 add_convert_fusion
  0.7 0.7 broadcast_in_dim.8.masks
  1.4 0.0 copy-start.9
  1.4 0.0 copy-start.10
  1.4 0.0 copy-start
  1.4 0.0 copy-start.1
  1.4 0.0 copy-start.3
  1.4 0.0 copy-start.4
  1.4 2.7 %shard_map.130 = f32[4,4,896]{2,1,0:T(4,128)} custom-call(f32[9,32,128]{2,1,0:T(8,128)} %bitcast.11, f32[9,32,128]{2,1,0:T(8,128)} %bitcast.14, f32[6,32,128]{2,1,0:T(8,128)} %bitcast.17, f32[3,32,128]{2,1,0:T(8,128)} %density.5, f32[8,128]{1,0:T(8,128)} %broadcast_in_dim.8.masks, f32[8,128]{1,0:T(8,128)} %constant.26.clone.select), custom_call_target="tpu_custom_call" | custom-call | tf_op jit(solution)/shard_map/pallas_call | solution.py:416
  4.2 0.0 copy-start.2
  4.2 7.8 %all-to-all-start = ((f32[4,4,896]{2,1,0:T(4,128)}), f32[4,4,896]{2,1,0:T(4,128)S(1)}, u32[]{:S(2)}, u32[]{:S(2)}) async-start(f32[4,4,896]{2,1,0:T(4,128)} %shard_map.130), calls=%async_computation | async-start | bytes 114688 | tf_op jit(solution)/shard_map/all_to_all | solution.py:379
  12.0 0.0 copy-done.9
  12.0 0.0 copy-done.10
  12.0 0.1 multiply_add_fusion
  12.1 0.1 add.22
  12.2 0.1 pad_maximum_fusion
  12.2 6.6 %all-to-all-done.beside = f32[4,4,896]{2,1,0:T(4,128)S(1)} async-done(((f32[4,4,896]{2,1,0:T(4,128)}), f32[4,4,896]{2,1,0:T(4,128)S(1)}, u32[]{:S(2)}, u32[]{:S(2)}) %all-to-all-start) | async-done | bytes 57376 | tf_op jit(solution)/shard_map/all_to_all | solution.py:379
  18.8 0.1 broadcast_in_dim.7.masks.facts
  18.9 0.0 copy-done
  18.9 0.0 copy-done.1
  18.9 0.0 copy-done.3
  18.9 0.0 copy-done.4
  18.9 0.0 copy-done.2
  18.9 0.0 copy-start.6
  18.9 0.1 shard_map.132
  19.0 4.4 %collective-permute-start = (f32[35,8,128]{2,1,0:T(8,128)S(1)}, f32[35,8,128]{2,1,0:T(8,128)S(1)}, u32[]{:S(2)}, u32[]{:S(2)}) collective-permute-start(f32[35,8,128]{2,1,0:T(8,128)S(1)} %shard_map.132), channel_id=1, source_target_pairs={{0,4},{4,8},{8,12},{12,16},{16,20},{20,24},{24,28},{28,32},{32,36}... | collective-permute-start | bytes 430088 | tf_op jit(solution)/shard_map/ppermute | solution.py:384
  23.5 0.0 copy-done.6
  23.5 2.7 %shard_map.131 = (f32[9,32,128]{2,1,0:T(8,128)S(1)}, f32[9,32,128]{2,1,0:T(8,128)S(1)}, f32[27,8,256]{2,1,0:T(8,128)S(1)}) custom-call(f32[16,128]{1,0:T(8,128)S(1)} %broadcast_in_dim.7.masks.facts, f32[9,32,128]{2,1,0:T(8,128)S(1)} %bitcast.13, f32[9,32,128]{2,1,0:T(8,128)S(1)} %bitcast.16, f32[6,32,128]{2,1,0:T(8,128)S(1)} %bitcast.19, ...), custom_call_target="tpu_custom_call" | custom-call | flops 50000000 | bytes 2000000 | tf_op jit(solution)/shard_map/pallas_call | solution.py:433
  26.2 0.0 collective-permute-done.behind
  26.2 1.5 %shard_map.133 = (f32[18,8,128]{2,1,0:T(8,128)S(1)}, f32[72,128]{1,0:T(8,128)S(1)}, f32[384,128]{1,0:T(8,128)S(1)}) custom-call(f32[16,128]{1,0:T(8,128)S(1)} %broadcast_in_dim.7.masks.facts, f32[9,32,128]{2,1,0:T(8,128)S(1)} %get-tuple-element.13.updated, f32[9,32,128]{2,1,0:T(8,128)S(1)} %get-tuple-element.14.middle, ...), custom_call_target="tpu_custom_call" | custom-call | tf_op jit(solution)/shard_map/pallas_call | solution.py:447
  27.8 0.0 copy-start.5
  27.8 29.8 %all_to_all.15 = f32[128,1,384]{2,1,0:T(1,128)S(1)} all-to-all(f32[128,1,384]{2,1,0:T(1,128)S(1)} %bitcast.24), channel_id=1, replica_groups=mesh['gx'=128,'gy'=4] {'gx'}, dimensions={0} | all-to-all | bytes 393216 | tf_op jit(solution)/shard_map/all_to_all | solution.py:375
  57.6 0.0 copy-done.5
  57.6 1.0 %shard_map.134 = (f32[384,128]{1,0:T(8,128)}, f32[72,128]{1,0:T(8,128)S(1)}) custom-call(f32[384,128]{1,0:T(8,128)S(1)} %bitcast.21, bf16[256,384]{1,0:T(8,128)(2,1)S(1)} %copy-done.5, f32[72,128]{1,0:T(8,128)S(1)} %get-tuple-element.18.tail), custom_call_target="tpu_custom_call" | custom-call | tf_op jit(solution)/shard_map/pallas_call | solution.py:464
  58.6 6.2 %all-to-all-start.2 = ((f32[128,1,384]{2,1,0:T(1,128)}), f32[128,1,384]{2,1,0:T(1,128)S(1)}, u32[]{:S(2)}, u32[]{:S(2)}) async-start(f32[128,1,384]{2,1,0:T(1,128)} %bitcast.8), calls=%async_computation.2 | async-start | bytes 393216 | tf_op jit(solution)/shard_map/all_to_all | solution.py:375
  64.8 2.9 %collective-permute-start.1 = (f32[72,128]{1,0:T(8,128)S(1)}, f32[72,128]{1,0:T(8,128)S(1)}, u32[]{:S(2)}, u32[]{:S(2)}) collective-permute-start(f32[72,128]{1,0:T(8,128)S(1)} %get-tuple-element.19), channel_id=1, source_target_pairs={{0,508},{4,0},{8,4},{12,8},{16,12},{20,16},{24,20},{28,24},{32,28}... | collective-permute-start | bytes 110600 | tf_op jit(solution)/shard_map/ppermute | solution.py:384
  67.7 2.7 %collective-permute-done.1.tail = f32[72,128]{1,0:T(8,128)S(1)} collective-permute-done((f32[72,128]{1,0:T(8,128)S(1)}, f32[72,128]{1,0:T(8,128)S(1)}, u32[]{:S(2)}, u32[]{:S(2)}) %collective-permute-start.1) | collective-permute-done | bytes 36896 | tf_op jit(solution)/shard_map/ppermute | solution.py:384
  70.4 0.0 copy-start.7
  70.4 0.0 copy-start.8
  70.4 0.7 shard_map.135
  71.1 5.9 %all-to-all-done.2 = f32[128,1,384]{2,1,0:T(1,128)S(1)} async-done(((f32[128,1,384]{2,1,0:T(1,128)}), f32[128,1,384]{2,1,0:T(1,128)S(1)}, u32[]{:S(2)}, u32[]{:S(2)}) %all-to-all-start.2) | async-done | bytes 196640 | tf_op jit(solution)/shard_map/all_to_all | solution.py:375
  77.0 0.0 copy-done.7
  77.0 0.0 copy-done.8
  77.0 1.0 %shard_map.136 = f32[6,2,32,128]{3,2,1,0:T(8,128)} custom-call(f32[16,128]{1,0:T(8,128)S(1)} %broadcast_in_dim.7.masks.facts, f32[384,128]{1,0:T(8,128)S(1)} %bitcast.20, f32[64,64]{1,0:T(8,128)S(1)} %copy-done.8, f32[64,64]{1,0:T(8,128)S(1)} %copy-done.7), custom_call_target="tpu_custom_call" | custom-call | tf_op jit(solution)/shard_map/pallas_call | solution.py:483
  (3 shorter events, 0.0 us)
Async XLA Ops:
  1.4 10.6 %copy-start.9 = (f32[2]{0:T(128)S(1)}, f32[2]{0:T(128)}, u32[]{:S(2)}) copy-start(f32[2]{0:T(128)} %param.16) | copy-start | bytes 28
  1.4 10.6 %copy-start.10 = (f32[2]{0:T(128)S(1)}, f32[2]{0:T(128)}, u32[]{:S(2)}) copy-start(f32[2]{0:T(128)} %param.17) | copy-start | bytes 28
  1.4 17.5 %copy-start = (f32[3,3,32,128]{3,2,1,0:T(8,128)S(1)}, f32[3,3,32,128]{3,2,1,0:T(8,128)}, u32[]{:S(2)}) copy-start(f32[3,3,32,128]{3,2,1,0:T(8,128)} %param.11) | copy-start | bytes 442372
  1.4 17.5 %copy-start.1 = (f32[3,3,32,128]{3,2,1,0:T(8,128)S(1)}, f32[3,3,32,128]{3,2,1,0:T(8,128)}, u32[]{:S(2)}) copy-start(f32[3,3,32,128]{3,2,1,0:T(8,128)} %param.12) | copy-start | bytes 442372
  1.4 17.5 %copy-start.3 = (f32[2,3,2,32,128]{4,3,2,1,0:T(8,128)S(1)}, f32[2,3,2,32,128]{4,3,2,1,0:T(8,128)}, u32[]{:S(2)}) copy-start(f32[2,3,2,32,128]{4,3,2,1,0:T(8,128)} %param.15) | copy-start | bytes 589828
  1.4 17.5 %copy-start.4 = (f32[3,32,128]{2,1,0:T(8,128)S(1)}, f32[3,32,128]{2,1,0:T(8,128)}, u32[]{:S(2)}) copy-start(f32[3,32,128]{2,1,0:T(8,128)} %density.5) | copy-start | bytes 147460
  4.2 14.7 %copy-start.2 = (f32[2,3,32,128]{3,2,1,0:T(8,128)S(1)}, f32[2,3,32,128]{3,2,1,0:T(8,128)}, u32[]{:S(2)}) copy-start(f32[2,3,32,128]{3,2,1,0:T(8,128)} %param.13) | copy-start | bytes 294916
  4.2 14.6 %all-to-all-start = ((f32[4,4,896]{2,1,0:T(4,128)}), f32[4,4,896]{2,1,0:T(4,128)S(1)}, u32[]{:S(2)}, u32[]{:S(2)}) async-start(f32[4,4,896]{2,1,0:T(4,128)} %shard_map.130), calls=%async_computation | async-start | bytes 114688 | tf_op jit(solution)/shard_map/all_to_all | solution.py:379
  18.9 4.6 %copy-start.6 = (f32[8,128]{1,0:T(8,128)S(1)}, f32[8,128]{1,0:T(8,128)}, u32[]{:S(2)}) copy-start(f32[8,128]{1,0:T(8,128)} %constant.26.clone.select) | copy-start | bytes 12292
  19.0 7.2 %collective-permute-start = (f32[35,8,128]{2,1,0:T(8,128)S(1)}, f32[35,8,128]{2,1,0:T(8,128)S(1)}, u32[]{:S(2)}, u32[]{:S(2)}) collective-permute-start(f32[35,8,128]{2,1,0:T(8,128)S(1)} %shard_map.132), channel_id=1, source_target_pairs={{0,4},{4,8},{8,12},{12,16},{16,20},{20,24},{24,28},{28,32},{32,36}... | collective-permute-start | bytes 430088 | tf_op jit(solution)/shard_map/ppermute | solution.py:384
  27.8 29.8 %copy-start.5 = (bf16[256,384]{1,0:T(8,128)(2,1)S(1)}, bf16[256,384]{1,0:T(8,128)(2,1)}, u32[]{:S(2)}) copy-start(bf16[256,384]{1,0:T(8,128)(2,1)} %constant.27.clone.table) | copy-start | bytes 589828
  58.6 18.5 %all-to-all-start.2 = ((f32[128,1,384]{2,1,0:T(1,128)}), f32[128,1,384]{2,1,0:T(1,128)S(1)}, u32[]{:S(2)}, u32[]{:S(2)}) async-start(f32[128,1,384]{2,1,0:T(1,128)} %bitcast.8), calls=%async_computation.2 | async-start | bytes 393216 | tf_op jit(solution)/shard_map/all_to_all | solution.py:375
  64.8 5.6 %collective-permute-start.1 = (f32[72,128]{1,0:T(8,128)S(1)}, f32[72,128]{1,0:T(8,128)S(1)}, u32[]{:S(2)}, u32[]{:S(2)}) collective-permute-start(f32[72,128]{1,0:T(8,128)S(1)} %get-tuple-element.19), channel_id=1, source_target_pairs={{0,508},{4,0},{8,4},{12,8},{16,12},{20,16},{24,20},{28,24},{32,28}... | collective-permute-start | bytes 110600 | tf_op jit(solution)/shard_map/ppermute | solution.py:384
  70.4 6.7 %copy-start.7 = (f32[64,64]{1,0:T(8,128)S(1)}, f32[64,64]{1,0:T(8,128)}, u32[]{:S(2)}) copy-start(f32[64,64]{1,0:T(8,128)} %constant.29.clone.turned) | copy-start | bytes 49156
  70.4 6.7 %copy-start.8 = (f32[64,64]{1,0:T(8,128)S(1)}, f32[64,64]{1,0:T(8,128)}, u32[]{:S(2)}) copy-start(f32[64,64]{1,0:T(8,128)} %constant.28.clone.straight) | copy-start | bytes 49156

commit v7 on v6

--- a/solution.py
+++ b/solution.py
@@ -14,11 +14,9 @@
 
 
 def edge_columns(width):
-    table = np.zeros((EDGE, width), np.float32)
-    for h in range(HALO):
-        table[h, h] = 1.0
-        table[HALO + h, width - HALO + h] = 1.0
-    return table
+    side = lax.broadcasted_iota(jnp.int32, (EDGE, width), 0)
+    lane = lax.broadcasted_iota(jnp.int32, (EDGE, width), 1)
+    return (lane == jnp.where(side < HALO, side, side + width - EDGE)).astype(jnp.float32).astype(jnp.bfloat16)
 
 
 def fourier_tables(length):
@@ -32,8 +30,8 @@
     return high, (value - high.astype(jnp.float32)).astype(jnp.bfloat16)
 
 
-def pick_columns(select, rows):
-    chosen = select[...].astype(jnp.bfloat16)
+def pick_columns(rows):
+    chosen = edge_columns(rows.shape[1])
     return lax.dot_general(
         jnp.concatenate([chosen, chosen], axis=1),
         jnp.concatenate(halves(rows), axis=1),
@@ -49,7 +47,7 @@
     )
 
 
-def pack_columns_kernel(disp, prev, moduli, density, masks, select, out, whole, sems):
+def pack_columns_kernel(disp, prev, moduli, density, out, whole, sems):
     copies = []
     start = 0
     for n, ref in enumerate((disp, prev, moduli, density)):
@@ -62,23 +60,24 @@
     peers, _, total = out.shape
     rows = row_tiles(whole[...])
     fill = jnp.zeros((total - rows.shape[0], rows.shape[1]), jnp.float32)
-    packed = pick_columns(select, jnp.concatenate([rows, fill], axis=0))
-    for slot in range(peers):
-        after, before = (masks[n : n + 1, :1] > 0.5 for n in (slot, peers + slot))
-        out[slot] = jnp.where(after, packed[HALO:], jnp.where(before, packed[:HALO], 0.0))
-
-
-def both_sides(masks, beside):
+    packed = pick_columns(jnp.concatenate([rows, fill], axis=0))
+    me = lax.axis_index("gy")
+    for step in range(peers):
+        slot = lax.rem(me + step, peers)
+        if step in (1, peers - 1):
+            out[slot] = packed[HALO:] if step == 1 else packed[:HALO]
+        else:
+            out[slot] = jnp.zeros(out.shape[1:], jnp.float32)
+
+
+def both_sides(beside):
     peers = beside.shape[0]
-    east = west = beside[0]
-    for slot in range(1, peers):
-        east = jnp.where(masks[slot : slot + 1, :1] > 0.5, beside[slot], east)
-        west = jnp.where(masks[peers + slot : peers + slot + 1, :1] > 0.5, beside[slot], west)
-    return jnp.concatenate([east, west], axis=0)
-
-
-def place_columns(both, select):
-    chosen = select[...].astype(jnp.bfloat16)
+    me = lax.axis_index("gy")
+    return jnp.concatenate([beside[lax.rem(me + 1, peers)], beside[lax.rem(me + peers - 1, peers)]], axis=0)
+
+
+def place_columns(both, width):
+    chosen = edge_columns(width)
     return lax.dot_general(
         jnp.concatenate(halves(both), axis=0),
         jnp.concatenate([chosen, chosen], axis=0),
@@ -87,18 +86,15 @@
     )
 
 
-def pack_rows_kernel(disp, prev, moduli, density, bins, masks, beside, out):
-    start = 0
-    for ref in (disp, prev, moduli, density):
-        for i in range(ref.shape[0]):
-            out[start + i] = ref[i, -EDGE:, :]
-        start += ref.shape[0]
+def pack_rows_kernel(whole, bins, beside, out):
+    start, rows, width = whole.shape
+    for n in range(start):
+        out[n] = whole[n, -EDGE:, :]
     for n in range(BINS):
         at = n % 2 * HALO
         out[start + n // 2, at : at + HALO, :] = bins[n, -HALO:, :]
-    width = out.shape[2]
-    both = both_sides(masks, beside)
-    first = start * (disp.shape[1] - EDGE)
+    both = both_sides(beside)
+    first = start * (rows - EDGE)
     base = first // width * width
     corner = pltpu.roll(both[:, base : base + 2 * width], 2 * width - (first - base), 1)
     out[start + BINS // 2] = corner[:, :width]
@@ -224,20 +220,15 @@
     advance(lambda n: mid[n], lambda n: field[n], keep_updated, True)
 
 
-def own_rows_kernel(masks, disp, prev, moduli, density, beside, select, updated, middle, head, field, coef, strip, mid):
-    rows, width = disp.shape[1], disp.shape[2]
-    strip[...] = place_columns(both_sides(masks, beside), select)
-    planes = field.shape[0]
-    start = 0
-    for ref in (disp, prev, moduli, density):
-        for i in range(ref.shape[0]):
-            n = start + i
-            field[n, :, :width] = ref[i]
-            for tile in range(rows // EDGE):
-                at = (tile * planes + n) * EDGE
-                field[n, tile * EDGE : (tile + 1) * EDGE, width:] = strip[at : at + EDGE, :]
-            head[n] = field[n, :EDGE, :]
-        start += ref.shape[0]
+def own_rows_kernel(whole, beside, updated, middle, head, field, coef, strip, mid):
+    planes, rows, width = whole.shape
+    strip[...] = place_columns(both_sides(beside), width)
+    for n in range(planes):
+        field[n, :, :width] = whole[n]
+        for tile in range(rows // EDGE):
+            at = (tile * planes + n) * EDGE
+            field[n, tile * EDGE : (tile + 1) * EDGE, width:] = strip[at : at + EDGE, :]
+        head[n] = field[n, :EDGE, :]
 
     def keep_middle(n, value):
         mid[n] = value
@@ -250,12 +241,12 @@
 
 
 def joint_rows_kernel(
-    facts, updated, middle, head, behind, bins, select, near, tail, operand, field, coef, mid,
+    angles, updated, middle, head, behind, bins, near, tail, operand, field, coef, mid,
 ):
     rows, width = updated.shape[1], updated.shape[2]
     planes = field.shape[0]
     corner = jnp.concatenate([behind[planes + BINS // 2], behind[planes + BINS // 2 + 1]], axis=1)
-    strip = place_columns(corner, select)
+    strip = place_columns(corner, width)
     for n in range(planes):
         field[n, :EDGE, :] = head[n]
         field[n, EDGE:, :width] = behind[n]
@@ -283,8 +274,7 @@
 
     two_steps(field, coef, mid, keep_middle, keep_updated)
 
-    angles = facts[EDGE:]
-    cosines, sines = jnp.cos(angles), jnp.sin(angles)
+    cosines, sines = jnp.cos(angles[...]), jnp.sin(angles[...])
     low = lax.broadcasted_iota(jnp.int32, (rows, width), 1) < width // 2
     half = width // 2
     for b in range(2):
@@ -325,7 +315,7 @@
     out[pl.ds(2, count, stride=3), :] = by_cos[:, 2 * width :] + jnp.where(low, turned, -turned)
 
 
-def second_transform_kernel(facts, received, straight, turned, out):
+def second_transform_kernel(received, straight, turned, out):
     items, parts, rows, width = out.shape
     half = width // 2
     count = received.shape[0] // 3
@@ -344,7 +334,7 @@
     joined = jnp.concatenate([jnp.concatenate(real, axis=1), jnp.concatenate(imag, axis=1)], axis=0)
     slot = lax.broadcasted_iota(jnp.int32, straight.shape, 1) % rows
     node = jnp.where(slot < rows - HALO, slot, slot - rows).astype(jnp.float32)
-    place = facts[facts.shape[0] - 1 :, : slot.shape[1]]
+    place = lax.axis_index("gx").astype(jnp.float32)
     angle = node * place * (2.0 * np.pi / (rows * count))
     matrix = straight[...] * jnp.cos(angle) + turned[...] * jnp.sin(angle)
     left, left_rest = halves(matrix)
@@ -396,44 +386,40 @@
     arrays = [a.reshape((-1,) + block) for a in (displacement, previous, moduli, density, bins)]
     planes = sum(a.shape[0] for a in arrays) - BINS
     packed = -(-planes * rows // width) * width
-    select = jnp.asarray(edge_columns(width))
     peers = lax.axis_size("gy")
-    distance = jnp.arange(peers) - lax.axis_index("gy")
-    masks = jnp.concatenate(
-        [(distance == 1) | (distance == 1 - peers), (distance == -1) | (distance == peers - 1)]
-    )
-    masks = masks.astype(jnp.float32)
-    steps = jnp.arange(1, 3).astype(jnp.float32)
-    angles = (phase[None, :] + steps[:, None] * omega[None, :]).reshape(-1)
-    facts = jnp.concatenate([masks, angles, jnp.full((4,), lax.axis_index("gx"))], dtype=jnp.float32)
-    facts = jnp.broadcast_to(facts[:, None], (facts.shape[0], width))
-    masks = jnp.broadcast_to(masks[:, None], (2 * peers, width))
     vmem = pl.BlockSpec(memory_space=pltpu.VMEM)
     hbm = pl.BlockSpec(memory_space=pltpu.HBM)
     params = pltpu.CompilerParams(vmem_limit_bytes=48 * 1024 * 1024)
     wide = 2 * width
 
-    sides = pl.pallas_call(
+    sides, whole = pl.pallas_call(
         pack_columns_kernel,
-        out_shape=pltpu.VMEM((peers, HALO, packed), jnp.float32),
-        in_specs=[hbm] * 4 + [vmem] * 2,
-        out_specs=vmem,
-        scratch_shapes=[pltpu.VMEM((planes,) + block, jnp.float32), pltpu.SemaphoreType.DMA((4,))],
+        out_shape=(
+            pltpu.VMEM((peers, HALO, packed), jnp.float32),
+            pltpu.VMEM((planes,) + block, jnp.float32),
+        ),
+        in_specs=[hbm] * 4,
+        out_specs=(vmem,) * 2,
+        scratch_shapes=[pltpu.SemaphoreType.DMA((4,))],
         compiler_params=pltpu.CompilerParams(vmem_limit_bytes=60 * 1024 * 1024),
-    )(*arrays[:4], masks, select)
+    )(*arrays[:4])
     beside = exchange_gy(sides)
     edge = pl.pallas_call(
         pack_rows_kernel,
         out_shape=f32(planes + BINS // 2 + 2, EDGE, width),
-        in_specs=[vmem] * 7,
+        in_specs=[vmem] * 3,
         out_specs=vmem,
         compiler_params=params,
-    )(*arrays, facts, beside)
+    )(whole, arrays[4], beside)
+    edge, omega, phase = lax.optimization_barrier((edge, omega, phase))
+    steps = np.arange(1, 3, dtype=np.float32)
+    angles = (phase[None, :] + steps[:, None] * omega[None, :]).reshape(-1)
+    angles = jnp.broadcast_to(angles[:, None], (angles.shape[0], width))
     behind = pass_on(edge, "gx", 1)
     updated, middle, head = pl.pallas_call(
         own_rows_kernel,
         out_shape=(f32(9, *block), f32(9, *block), f32(planes, EDGE, wide)),
-        in_specs=[vmem] * 7,
+        in_specs=[vmem] * 2,
         out_specs=(vmem,) * 3,
         scratch_shapes=[
             pltpu.VMEM((planes, rows, wide), jnp.float32),
@@ -443,11 +429,11 @@
         ],
         compiler_params=params,
         cost_estimate=pl.CostEstimate(flops=50_000_000, bytes_accessed=2_000_000, transcendentals=0),
-    )(facts, *arrays[:4], beside, select)
+    )(whole, beside)
     near, tail, operand = pl.pallas_call(
         joint_rows_kernel,
         out_shape=(f32(18, EDGE, width), f32(18 * HALO, width), f32(3 * groups, width)),
-        in_specs=[vmem] * 7,
+        in_specs=[vmem] * 6,
         out_specs=(vmem,) * 3,
         scratch_shapes=[
             pltpu.VMEM((planes, 2 * EDGE, wide), jnp.float32),
@@ -455,7 +441,7 @@
             pltpu.VMEM((9, 2 * EDGE, wide), jnp.float32),
         ],
         compiler_params=params,
-    )(facts, updated, middle, head, behind, arrays[4], select)
+    )(angles, updated, middle, head, behind, arrays[4])
 
     stacked = np.concatenate(fourier_tables(groups), axis=0)
     high = stacked.astype(ml_dtypes.bfloat16)
@@ -483,10 +469,10 @@
     spectrum = pl.pallas_call(
         second_transform_kernel,
         out_shape=f32(items, 2, *block),
-        in_specs=[vmem] * 4,
+        in_specs=[vmem] * 3,
         out_specs=vmem,
         compiler_params=params,
-    )(facts, exchange(sections), straight, turned)
+    )(exchange(sections), straight, turned)
     return (
         updated.reshape(displacement.shape),
         middle.reshape(displacement.shape),

time: 78.5 us -> 75.8 us (0.966)
  blocking collectives: 29.8 us -> 43.9 us
  starting transfers between devices: 21.4 us -> 13.6 us
  waiting for transfers between devices: 15.2 us -> 8.58 us
  Pallas kernels: 9.8 us -> 8.37 us
    all_to_all x0 -> x1, blocking collectives: none -> 14.3 us  [exchange_gy(): return lax.all_to_all(value, 'gy', split_axis=0, concat_axis=0, tiled=True)]
    all_to_all x1 -> x0, starting transfers between devices: 7.79 us -> none  [exchange_gy(): return lax.all_to_all(value, 'gy', split_axis=0, concat_axis=0, tiled=True)]
    all_to_all x1 -> x0, waiting for transfers between devices: 6.58 us -> none  [exchange_gy(): return lax.all_to_all(value, 'gy', split_axis=0, concat_axis=0, tiled=True)]
    pallas_call x1, Pallas kernels: 2.74 us -> 1.37 us  [on_device(): pl.pallas_call(pack_columns_kernel, out_shape=(pltpu.VMEM((peers, HALO, p...]
  transfers between devices with their start and end apart: 4 -> 3, of which waited for: 3 -> 2; matrix products, arithmetic and copies ran while one was open for 0% -> 0% of each run, Pallas kernels for 4% -> 5%
where the time goes in v7:
time: 75.8 us; the launch traced here: 75.4 us
  blocking collectives  43.9 us (58%)
  starting transfers between devices  13.6 us (18%)
  waiting for transfers between devices  8.58 us (11%)
  Pallas kernels  8.37 us (11%)
    all_to_all x1, blocking collectives, exchange(): lax.all_to_all(shaped, 'gx', split_axis=0, concat_axis=0, tiled=True)  29.6 us
    all_to_all x1, blocking collectives, exchange_gy(): return lax.all_to_all(value, 'gy', split_axis=0, concat_axis=0, tiled=True)  14.3 us
    ppermute x2, starting transfers between devices, pass_on(): lax.ppermute(value, axis, [(i, (i + step) % peers) for i in range(peers)])  7.34 us
    all_to_all x1, starting transfers between devices, exchange(): lax.all_to_all(shaped, 'gx', split_axis=0, concat_axis=0, tiled=True)  6.22 us
    all_to_all x1, waiting for transfers between devices, exchange(): lax.all_to_all(shaped, 'gx', split_axis=0, concat_axis=0, tiled=True)  5.92 us
    pallas_call x1, Pallas kernels, on_device(): pl.pallas_call(own_rows_kernel, out_shape=(f32(9, *block), f32(9, *block)...  2.66 us
    ppermute x2, waiting for transfers between devices, pass_on(): lax.ppermute(value, axis, [(i, (i + step) % peers) for i in range(peers)])  2.65 us
    pallas_call x1, Pallas kernels, on_device(): pl.pallas_call(joint_rows_kernel, out_shape=(f32(18, EDGE, width), f32(18...  1.54 us
  transfers between devices with their start and end apart: 3, of which 2 were waited for; matrix products, arithmetic and copies ran while one was open for 0% of the time, Pallas kernels for 5%

profile of v7, /device:TPU:1, one launch (start us, length us, event | category | flops | bytes accessed | tf_op | source)
XLA Modules:
  0.0 75.4 jit_solution(17861656359731684120)
XLA Ops:
  0.6 0.0 copy-start
  0.6 1.4 %shard_map.130 = (f32[4,4,896]{2,1,0:T(4,128)S(1)}, f32[27,32,128]{2,1,0:T(8,128)S(1)}) custom-call(f32[9,32,128]{2,1,0:T(8,128)} %bitcast.17, f32[9,32,128]{2,1,0:T(8,128)} %bitcast.18, f32[6,32,128]{2,1,0:T(8,128)} %bitcast.19, f32[3,32,128]{2,1,0:T(8,128)} %density.1), custom_call_target="tpu_custom_call" | custom-call | tf_op jit(solution)/shard_map/pallas_call | solution.py:395
  2.0 14.3 %all_to_all.15.beside = f32[4,4,896]{2,1,0:T(4,128)S(1)} all-to-all(f32[4,4,896]{2,1,0:T(4,128)S(1)} %get-tuple-element.19), channel_id=1, replica_groups=mesh['gx'=128,'gy'=4] {'gy'}, dimensions={0} | all-to-all | bytes 114688 | tf_op jit(solution)/shard_map/all_to_all | solution.py:369
  16.3 0.0 copy-done
  16.3 0.0 copy-start.4
  16.3 0.0 copy-start.5
  16.3 0.0 copy-start.6
  16.3 0.1 shard_map.132
  16.4 4.4 %collective-permute-start = (f32[35,8,128]{2,1,0:T(8,128)S(1)}, f32[35,8,128]{2,1,0:T(8,128)S(1)}, u32[]{:S(2)}, u32[]{:S(2)}) collective-permute-start(f32[35,8,128]{2,1,0:T(8,128)S(1)} %shard_map.132), channel_id=1, source_target_pairs={{0,4},{4,8},{8,12},{12,16},{16,20},{20,24},{24,28},{28,32},{32,36}... | collective-permute-start | bytes 430088 | tf_op jit(solution)/shard_map/ppermute | solution.py:374
  20.8 0.0 copy-done.4
  20.8 0.0 copy-done.5
  20.8 0.0 copy-done.6
  20.9 0.1 multiply_add_fusion
  20.9 0.1 add.17
  21.0 2.7 %shard_map.131 = (f32[9,32,128]{2,1,0:T(8,128)S(1)}, f32[9,32,128]{2,1,0:T(8,128)S(1)}, f32[27,8,256]{2,1,0:T(8,128)S(1)}) custom-call(f32[27,32,128]{2,1,0:T(8,128)S(1)} %get-tuple-element.18.whole, f32[4,4,896]{2,1,0:T(4,128)S(1)} %all_to_all.15.beside), custom_call_target="tpu_custom_call" | custom-call | flops 50000000 | bytes 2000000 | tf_op jit(solution)/shard_map/pallas_call | solution.py:419
  23.7 0.0 collective-permute-done.behind
  23.7 0.1 broadcast_in_dim.2.angles
  23.8 1.5 %shard_map.133 = (f32[18,8,128]{2,1,0:T(8,128)S(1)}, f32[72,128]{1,0:T(8,128)S(1)}, f32[384,128]{1,0:T(8,128)S(1)}) custom-call(f32[4,128]{1,0:T(4,128)S(1)} %broadcast_in_dim.2.angles, f32[9,32,128]{2,1,0:T(8,128)S(1)} %get-tuple-element.20.updated, f32[9,32,128]{2,1,0:T(8,128)S(1)} %get-tuple-element.21.middle, f32[27,8,256]{2,1,0:T(8,128)S(1)} %get-tuple-element.24.head, ...), custom_call_target="tpu_custom_call" | custom-call | tf_op jit(solution)/shard_map/pallas_call | solution.py:433
  25.3 0.0 copy-start.1
  25.3 29.6 %all_to_all.16 = f32[128,1,384]{2,1,0:T(1,128)S(1)} all-to-all(f32[128,1,384]{2,1,0:T(1,128)S(1)} %bitcast.15), channel_id=1, replica_groups=mesh['gx'=128,'gy'=4] {'gx'}, dimensions={0} | all-to-all | bytes 393216 | tf_op jit(solution)/shard_map/all_to_all | solution.py:365
  55.0 0.0 copy-done.1
  55.0 1.0 %shard_map.134 = (f32[384,128]{1,0:T(8,128)}, f32[72,128]{1,0:T(8,128)S(1)}) custom-call(f32[384,128]{1,0:T(8,128)S(1)} %bitcast.12, bf16[256,384]{1,0:T(8,128)(2,1)S(1)} %copy-done.1, f32[72,128]{1,0:T(8,128)S(1)} %get-tuple-element.28.tail), custom_call_target="tpu_custom_call" | custom-call | tf_op jit(solution)/shard_map/pallas_call | solution.py:450
  56.0 6.2 %all-to-all-start.2 = ((f32[128,1,384]{2,1,0:T(1,128)}), f32[128,1,384]{2,1,0:T(1,128)S(1)}, u32[]{:S(2)}, u32[]{:S(2)}) async-start(f32[128,1,384]{2,1,0:T(1,128)} %bitcast.8), calls=%async_computation.2 | async-start | bytes 393216 | tf_op jit(solution)/shard_map/all_to_all | solution.py:365
  62.2 2.9 %collective-permute-start.1 = (f32[72,128]{1,0:T(8,128)S(1)}, f32[72,128]{1,0:T(8,128)S(1)}, u32[]{:S(2)}, u32[]{:S(2)}) collective-permute-start(f32[72,128]{1,0:T(8,128)S(1)} %get-tuple-element.29), channel_id=1, source_target_pairs={{0,508},{4,0},{8,4},{12,8},{16,12},{20,16},{24,20},{28,24},{32,28}... | collective-permute-start | bytes 110600 | tf_op jit(solution)/shard_map/ppermute | solution.py:374
  65.1 2.7 %collective-permute-done.1.tail = f32[72,128]{1,0:T(8,128)S(1)} collective-permute-done((f32[72,128]{1,0:T(8,128)S(1)}, f32[72,128]{1,0:T(8,128)S(1)}, u32[]{:S(2)}, u32[]{:S(2)}) %collective-permute-start.1) | collective-permute-done | bytes 36896 | tf_op jit(solution)/shard_map/ppermute | solution.py:374
  67.8 0.0 copy-start.2
  67.8 0.0 copy-start.3
  67.8 0.7 shard_map.135
  68.5 5.9 %all-to-all-done.2 = f32[128,1,384]{2,1,0:T(1,128)S(1)} async-done(((f32[128,1,384]{2,1,0:T(1,128)}), f32[128,1,384]{2,1,0:T(1,128)S(1)}, u32[]{:S(2)}, u32[]{:S(2)}) %all-to-all-start.2) | async-done | bytes 196640 | tf_op jit(solution)/shard_map/all_to_all | solution.py:365
  74.5 0.0 copy-done.2
  74.5 0.0 copy-done.3
  74.5 1.0 %shard_map.136 = f32[6,2,32,128]{3,2,1,0:T(8,128)} custom-call(f32[384,128]{1,0:T(8,128)S(1)} %bitcast.11, f32[64,64]{1,0:T(8,128)S(1)} %copy-done.2, f32[64,64]{1,0:T(8,128)S(1)} %copy-done.3), custom_call_target="tpu_custom_call" | custom-call | tf_op jit(solution)/shard_map/pallas_call | solution.py:469
Async XLA Ops:
  0.6 15.7 %copy-start = (f32[2,3,2,32,128]{4,3,2,1,0:T(8,128)S(1)}, f32[2,3,2,32,128]{4,3,2,1,0:T(8,128)}, u32[]{:S(2)}) copy-start(f32[2,3,2,32,128]{4,3,2,1,0:T(8,128)} %param.15) | copy-start | bytes 589828
  16.3 4.5 %copy-start.4 = (f32[2]{0:T(128)S(1)}, f32[2]{0:T(128)}, u32[]{:S(2)}) copy-start(f32[2]{0:T(128)} %param.16) | copy-start | bytes 28
  16.3 4.5 %copy-start.5 = (f32[2]{0:T(128)S(1)}, f32[2]{0:T(128)}, u32[]{:S(2)}) copy-start(f32[2]{0:T(128)} %param.17) | copy-start | bytes 28
  16.3 4.5 %copy-start.6 = (f32[2]{0:T(128)S(1)}, f32[2]{0:T(128)}, u32[]{:S(2)}) copy-start(f32[2]{0:T(128)} %constant.17) | copy-start | bytes 28
  16.4 7.3 %collective-permute-start = (f32[35,8,128]{2,1,0:T(8,128)S(1)}, f32[35,8,128]{2,1,0:T(8,128)S(1)}, u32[]{:S(2)}, u32[]{:S(2)}) collective-permute-start(f32[35,8,128]{2,1,0:T(8,128)S(1)} %shard_map.132), channel_id=1, source_target_pairs={{0,4},{4,8},{8,12},{12,16},{16,20},{20,24},{24,28},{28,32},{32,36}... | collective-permute-start | bytes 430088 | tf_op jit(solution)/shard_map/ppermute | solution.py:374
  25.3 29.7 %copy-start.1 = (bf16[256,384]{1,0:T(8,128)(2,1)S(1)}, bf16[256,384]{1,0:T(8,128)(2,1)}, u32[]{:S(2)}) copy-start(bf16[256,384]{1,0:T(8,128)(2,1)} %constant.9.clone.table) | copy-start | bytes 589828
  56.0 18.5 %all-to-all-start.2 = ((f32[128,1,384]{2,1,0:T(1,128)}), f32[128,1,384]{2,1,0:T(1,128)S(1)}, u32[]{:S(2)}, u32[]{:S(2)}) async-start(f32[128,1,384]{2,1,0:T(1,128)} %bitcast.8), calls=%async_computation.2 | async-start | bytes 393216 | tf_op jit(solution)/shard_map/all_to_all | solution.py:365
  62.2 5.6 %collective-permute-start.1 = (f32[72,128]{1,0:T(8,128)S(1)}, f32[72,128]{1,0:T(8,128)S(1)}, u32[]{:S(2)}, u32[]{:S(2)}) collective-permute-start(f32[72,128]{1,0:T(8,128)S(1)} %get-tuple-element.29), channel_id=1, source_target_pairs={{0,508},{4,0},{8,4},{12,8},{16,12},{20,16},{24,20},{28,24},{32,28}... | collective-permute-start | bytes 110600 | tf_op jit(solution)/shard_map/ppermute | solution.py:374
  67.8 6.7 %copy-start.2 = (f32[64,64]{1,0:T(8,128)S(1)}, f32[64,64]{1,0:T(8,128)}, u32[]{:S(2)}) copy-start(f32[64,64]{1,0:T(8,128)} %constant.10.clone.straight) | copy-start | bytes 49156
  67.8 6.7 %copy-start.3 = (f32[64,64]{1,0:T(8,128)S(1)}, f32[64,64]{1,0:T(8,128)}, u32[]{:S(2)}) copy-start(f32[64,64]{1,0:T(8,128)} %constant.11.clone.turned) | copy-start | bytes 49156

commit v8 on v7

--- a/solution.py
+++ b/solution.py
@@ -1,3 +1,5 @@
+import functools
+
 import jax
 import jax.numpy as jnp
 import ml_dtypes
@@ -31,13 +33,9 @@
 
 
 def pick_columns(rows):
-    chosen = edge_columns(rows.shape[1])
-    return lax.dot_general(
-        jnp.concatenate([chosen, chosen], axis=1),
-        jnp.concatenate(halves(rows), axis=1),
-        (((1,), (1,)), ((), ())),
-        preferred_element_type=jnp.float32,
-    )
+    width = rows.shape[1]
+    turned = [rows[at : at + width].T for at in range(0, rows.shape[0], width)]
+    return jnp.concatenate([jnp.concatenate([t[:HALO], t[-HALO:]], axis=0) for t in turned], axis=1)
 
 
 def row_tiles(whole):
@@ -220,8 +218,10 @@
     advance(lambda n: mid[n], lambda n: field[n], keep_updated, True)
 
 
-def own_rows_kernel(whole, beside, updated, middle, head, field, coef, strip, mid):
+def own_rows_kernel(angles, whole, beside, updated, middle, head, waves, field, coef, strip, mid):
     planes, rows, width = whole.shape
+    waves[: angles.shape[0], :] = jnp.cos(angles[...])
+    waves[angles.shape[0] :, :] = jnp.sin(angles[...])
     strip[...] = place_columns(both_sides(beside), width)
     for n in range(planes):
         field[n, :, :width] = whole[n]
@@ -241,7 +241,7 @@
 
 
 def joint_rows_kernel(
-    angles, updated, middle, head, behind, bins, near, tail, operand, field, coef, mid,
+    waves, updated, middle, head, behind, bins, near, tail, operand, field, coef, mid,
 ):
     rows, width = updated.shape[1], updated.shape[2]
     planes = field.shape[0]
@@ -274,7 +274,7 @@
 
     two_steps(field, coef, mid, keep_middle, keep_updated)
 
-    cosines, sines = jnp.cos(angles[...]), jnp.sin(angles[...])
+    cosines, sines = waves[:HALO], waves[HALO:]
     low = lax.broadcasted_iota(jnp.int32, (rows, width), 1) < width // 2
     half = width // 2
     for b in range(2):
@@ -315,7 +315,7 @@
     out[pl.ds(2, count, stride=3), :] = by_cos[:, 2 * width :] + jnp.where(low, turned, -turned)
 
 
-def second_transform_kernel(received, straight, turned, out):
+def second_transform_kernel(received, matrix, out):
     items, parts, rows, width = out.shape
     half = width // 2
     count = received.shape[0] // 3
@@ -332,12 +332,7 @@
             real.append(jnp.where(low, one, pltpu.roll(two, half, 1)))
             imag.append(jnp.where(low, pltpu.roll(one, half, 1), two))
     joined = jnp.concatenate([jnp.concatenate(real, axis=1), jnp.concatenate(imag, axis=1)], axis=0)
-    slot = lax.broadcasted_iota(jnp.int32, straight.shape, 1) % rows
-    node = jnp.where(slot < rows - HALO, slot, slot - rows).astype(jnp.float32)
-    place = lax.axis_index("gx").astype(jnp.float32)
-    angle = node * place * (2.0 * np.pi / (rows * count))
-    matrix = straight[...] * jnp.cos(angle) + turned[...] * jnp.sin(angle)
-    left, left_rest = halves(matrix)
+    left, left_rest = halves(matrix[...])
     high, rest = halves(joined)
     waves = jnp.dot(
         jnp.concatenate([left, left, left_rest], axis=1),
@@ -349,7 +344,12 @@
             out[item, part] = waves[part * rows : (part + 1) * rows, item * width : (item + 1) * width]
 
 
-def set_in_kernel(updated, middle, near, tail, updated_out, middle_out):
+def set_in_kernel(rows, count, updated, middle, near, tail, straight, turned, updated_out, middle_out, matrix):
+    slot = lax.broadcasted_iota(jnp.int32, straight.shape, 1) % rows
+    node = jnp.where(slot < rows - HALO, slot, slot - rows).astype(jnp.float32)
+    place = lax.axis_index("gx").astype(jnp.float32)
+    angle = node * place * (2.0 * np.pi / (rows * count))
+    matrix[...] = straight[...] * jnp.cos(angle) + turned[...] * jnp.sin(angle)
     for k, (ref, out) in enumerate(((updated, updated_out), (middle, middle_out))):
         for n in range(ref.shape[0]):
             at = k * ref.shape[0] + n
@@ -416,11 +416,11 @@
     angles = (phase[None, :] + steps[:, None] * omega[None, :]).reshape(-1)
     angles = jnp.broadcast_to(angles[:, None], (angles.shape[0], width))
     behind = pass_on(edge, "gx", 1)
-    updated, middle, head = pl.pallas_call(
+    updated, middle, head, waves = pl.pallas_call(
         own_rows_kernel,
-        out_shape=(f32(9, *block), f32(9, *block), f32(planes, EDGE, wide)),
-        in_specs=[vmem] * 2,
-        out_specs=(vmem,) * 3,
+        out_shape=(f32(9, *block), f32(9, *block), f32(planes, EDGE, wide), f32(EDGE, width)),
+        in_specs=[vmem] * 3,
+        out_specs=(vmem,) * 4,
         scratch_shapes=[
             pltpu.VMEM((planes, rows, wide), jnp.float32),
             pltpu.VMEM((3, 11, rows, wide), jnp.float32),
@@ -429,7 +429,7 @@
         ],
         compiler_params=params,
         cost_estimate=pl.CostEstimate(flops=50_000_000, bytes_accessed=2_000_000, transcendentals=0),
-    )(whole, beside)
+    )(angles, whole, beside)
     near, tail, operand = pl.pallas_call(
         joint_rows_kernel,
         out_shape=(f32(18, EDGE, width), f32(18 * HALO, width), f32(3 * groups, width)),
@@ -441,7 +441,7 @@
             pltpu.VMEM((9, 2 * EDGE, wide), jnp.float32),
         ],
         compiler_params=params,
-    )(angles, updated, middle, head, behind, arrays[4])
+    )(waves, updated, middle, head, behind, arrays[4])
 
     stacked = np.concatenate(fourier_tables(groups), axis=0)
     high = stacked.astype(ml_dtypes.bfloat16)
@@ -454,25 +454,25 @@
         out_specs=(vmem,) * 2,
         compiler_params=params,
     )(exchange(operand), table, tail)
-    updated, middle = pl.pallas_call(
-        set_in_kernel,
-        out_shape=(f32(9, *block), f32(9, *block)),
-        in_specs=[vmem] * 4,
-        out_specs=(vmem,) * 2,
-        compiler_params=params,
-        cost_estimate=pl.CostEstimate(flops=1_000_000, bytes_accessed=1_200_000, transcendentals=0),
-    )(updated, middle, near, pass_on(tail, "gx", -1))
     scale = (groups * rows) ** -0.5
     c, s = (t * scale for t in fourier_tables(rows))
     straight = jnp.asarray(np.block([[c, s], [-s, c]]), jnp.float32)
     turned = jnp.asarray(np.block([[-s, c], [-c, -s]]), jnp.float32)
+    updated, middle, matrix = pl.pallas_call(
+        functools.partial(set_in_kernel, rows, groups),
+        out_shape=(f32(9, *block), f32(9, *block), f32(2 * rows, 2 * rows)),
+        in_specs=[vmem] * 6,
+        out_specs=(vmem,) * 3,
+        compiler_params=params,
+        cost_estimate=pl.CostEstimate(flops=1_000_000, bytes_accessed=1_200_000, transcendentals=0),
+    )(updated, middle, near, pass_on(tail, "gx", -1), straight, turned)
     spectrum = pl.pallas_call(
         second_transform_kernel,
         out_shape=f32(items, 2, *block),
-        in_specs=[vmem] * 3,
+        in_specs=[vmem] * 2,
         out_specs=vmem,
         compiler_params=params,
-    )(exchange(sections), straight, turned)
+    )(exchange(sections), matrix)
     return (
         updated.reshape(displacement.shape),
         middle.reshape(displacement.shape),

time: 75.8 us -> 75.7 us (level)
  no operation moved by 1% of the time
where the time goes in v8:
time: 75.7 us; the launch traced here: 75.4 us
  blocking collectives  43.8 us (58%)
  starting transfers between devices  13.7 us (18%)
  waiting for transfers between devices  8.57 us (11%)
  Pallas kernels  8.28 us (11%)
    all_to_all x1, blocking collectives, exchange(): lax.all_to_all(shaped, 'gx', split_axis=0, concat_axis=0, tiled=True)  29.6 us
    all_to_all x1, blocking collectives, exchange_gy(): return lax.all_to_all(value, 'gy', split_axis=0, concat_axis=0, tiled=True)  14.3 us
    ppermute x2, starting transfers between devices, pass_on(): lax.ppermute(value, axis, [(i, (i + step) % peers) for i in range(peers)])  7.34 us
    all_to_all x1, starting transfers between devices, exchange(): lax.all_to_all(shaped, 'gx', split_axis=0, concat_axis=0, tiled=True)  6.35 us
    all_to_all x1, waiting for transfers between devices, exchange(): lax.all_to_all(shaped, 'gx', split_axis=0, concat_axis=0, tiled=True)  5.92 us
    pallas_call x1, Pallas kernels, on_device(): pl.pallas_call(own_rows_kernel, out_shape=(f32(9, *block), f32(9, *block)...  2.67 us
    ppermute x2, waiting for transfers between devices, pass_on(): lax.ppermute(value, axis, [(i, (i + step) % peers) for i in range(peers)])  2.65 us
    pallas_call x1, Pallas kernels, on_device(): pl.pallas_call(joint_rows_kernel, out_shape=(f32(18, EDGE, width), f32(18...  1.55 us
  transfers between devices with their start and end apart: 3, of which 2 were waited for; matrix products, arithmetic and copies ran while one was open for 0% of the time, Pallas kernels for 5%

profile of v8, /device:TPU:1, one launch (start us, length us, event | category | flops | bytes accessed | tf_op | source)
XLA Modules:
  0.0 75.4 jit_solution(13812630592870075592)
XLA Ops:
  0.6 0.0 copy-start
  0.6 1.3 %shard_map.130 = (f32[4,4,896]{2,1,0:T(4,128)S(1)}, f32[27,32,128]{2,1,0:T(8,128)S(1)}) custom-call(f32[9,32,128]{2,1,0:T(8,128)} %bitcast.17, f32[9,32,128]{2,1,0:T(8,128)} %bitcast.18, f32[6,32,128]{2,1,0:T(8,128)} %bitcast.19, f32[3,32,128]{2,1,0:T(8,128)} %density.1), custom_call_target="tpu_custom_call" | custom-call | tf_op jit(solution)/shard_map/pallas_call | solution.py:395
  2.0 14.3 %all_to_all.15.beside = f32[4,4,896]{2,1,0:T(4,128)S(1)} all-to-all(f32[4,4,896]{2,1,0:T(4,128)S(1)} %get-tuple-element.21), channel_id=1, replica_groups=mesh['gx'=128,'gy'=4] {'gy'}, dimensions={0} | all-to-all | bytes 114688 | tf_op jit(solution)/shard_map/all_to_all | solution.py:369
  16.2 0.0 copy-done
  16.2 0.0 copy-start.4
  16.2 0.0 copy-start.5
  16.3 0.0 copy-start.6
  16.3 0.1 shard_map.131
  16.3 4.4 %collective-permute-start = (f32[35,8,128]{2,1,0:T(8,128)S(1)}, f32[35,8,128]{2,1,0:T(8,128)S(1)}, u32[]{:S(2)}, u32[]{:S(2)}) collective-permute-start(f32[35,8,128]{2,1,0:T(8,128)S(1)} %shard_map.131), channel_id=1, source_target_pairs={{0,4},{4,8},{8,12},{12,16},{16,20},{20,24},{24,28},{28,32},{32,36}... | collective-permute-start | bytes 430088 | tf_op jit(solution)/shard_map/ppermute | solution.py:374
  20.8 0.0 copy-done.4
  20.8 0.0 copy-done.5
  20.8 0.0 copy-done.6
  20.8 0.1 multiply_add_fusion
  20.9 0.1 add.17
  21.0 0.1 broadcast_in_dim.2.angles
  21.0 2.7 %shard_map.132 = (f32[9,32,128]{2,1,0:T(8,128)S(1)}, f32[9,32,128]{2,1,0:T(8,128)S(1)}, f32[27,8,256]{2,1,0:T(8,128)S(1)}, f32[8,128]{1,0:T(8,128)S(1)}) custom-call(f32[4,128]{1,0:T(4,128)S(1)} %broadcast_in_dim.2.angles, f32[27,32,128]{2,1,0:T(8,128)S(1)} %get-tuple-element.20.whole, f32[4,4,896]{2,1,0:T(4,128)S(1)} %all_to_all.15.beside), custom_call_target="tpu_custom_call" | custom-call | flops 50000000 | bytes 2000000 | tf_op jit(solution)/shard_map/pallas_call | solution.py:419
  23.7 0.0 collective-permute-done.behind
  23.7 1.5 %shard_map.133 = (f32[18,8,128]{2,1,0:T(8,128)S(1)}, f32[72,128]{1,0:T(8,128)S(1)}, f32[384,128]{1,0:T(8,128)S(1)}) custom-call(f32[8,128]{1,0:T(8,128)S(1)} %get-tuple-element.26.waves, f32[9,32,128]{2,1,0:T(8,128)S(1)} %get-tuple-element.24.updated, f32[9,32,128]{2,1,0:T(8,128)S(1)} %get-tuple-element.25.middle, f32[27,8,256]{2,1,0:T(8,128)S(1)} %get-tuple-element.27.head, ...), custom_call_target="tpu_custom_call" | custom-call | tf_op jit(solution)/shard_map/pallas_call | solution.py:433
  25.3 0.0 copy-start.1
  25.3 29.6 %all_to_all.16 = f32[128,1,384]{2,1,0:T(1,128)S(1)} all-to-all(f32[128,1,384]{2,1,0:T(1,128)S(1)} %bitcast.15), channel_id=1, replica_groups=mesh['gx'=128,'gy'=4] {'gx'}, dimensions={0} | all-to-all | bytes 393216 | tf_op jit(solution)/shard_map/all_to_all | solution.py:365
  54.9 0.0 copy-done.1
  54.9 1.0 %shard_map.134 = (f32[384,128]{1,0:T(8,128)}, f32[72,128]{1,0:T(8,128)S(1)}) custom-call(f32[384,128]{1,0:T(8,128)S(1)} %bitcast.12, bf16[256,384]{1,0:T(8,128)(2,1)S(1)} %copy-done.1, f32[72,128]{1,0:T(8,128)S(1)} %get-tuple-element.31.tail), custom_call_target="tpu_custom_call" | custom-call | tf_op jit(solution)/shard_map/pallas_call | solution.py:450
  55.9 0.0 copy-start.2
  55.9 0.0 copy-start.3
  55.9 6.4 %all-to-all-start.2 = ((f32[128,1,384]{2,1,0:T(1,128)}), f32[128,1,384]{2,1,0:T(1,128)S(1)}, u32[]{:S(2)}, u32[]{:S(2)}) async-start(f32[128,1,384]{2,1,0:T(1,128)} %bitcast.8), calls=%async_computation.2 | async-start | bytes 393216 | tf_op jit(solution)/shard_map/all_to_all | solution.py:365
  62.2 2.9 %collective-permute-start.1 = (f32[72,128]{1,0:T(8,128)S(1)}, f32[72,128]{1,0:T(8,128)S(1)}, u32[]{:S(2)}, u32[]{:S(2)}) collective-permute-start(f32[72,128]{1,0:T(8,128)S(1)} %get-tuple-element.32), channel_id=1, source_target_pairs={{0,508},{4,0},{8,4},{12,8},{16,12},{20,16},{24,20},{28,24},{32,28}... | collective-permute-start | bytes 110600 | tf_op jit(solution)/shard_map/ppermute | solution.py:374
  65.2 2.7 %collective-permute-done.1.tail = f32[72,128]{1,0:T(8,128)S(1)} collective-permute-done((f32[72,128]{1,0:T(8,128)S(1)}, f32[72,128]{1,0:T(8,128)S(1)}, u32[]{:S(2)}, u32[]{:S(2)}) %collective-permute-start.1) | collective-permute-done | bytes 36896 | tf_op jit(solution)/shard_map/ppermute | solution.py:374
  67.8 0.0 copy-done.2
  67.8 0.0 copy-done.3
  67.8 0.7 shard_map.135
  68.6 5.9 %all-to-all-done.2 = f32[128,1,384]{2,1,0:T(1,128)S(1)} async-done(((f32[128,1,384]{2,1,0:T(1,128)}), f32[128,1,384]{2,1,0:T(1,128)S(1)}, u32[]{:S(2)}, u32[]{:S(2)}) %all-to-all-start.2) | async-done | bytes 196640 | tf_op jit(solution)/shard_map/all_to_all | solution.py:365
  74.5 0.9 %shard_map.136 = f32[6,2,32,128]{3,2,1,0:T(8,128)} custom-call(f32[384,128]{1,0:T(8,128)S(1)} %bitcast.11, f32[64,64]{1,0:T(8,128)S(1)} %get-tuple-element.36.matrix), custom_call_target="tpu_custom_call" | custom-call | tf_op jit(solution)/shard_map/pallas_call | solution.py:469
Async XLA Ops:
  0.6 15.6 %copy-start = (f32[2,3,2,32,128]{4,3,2,1,0:T(8,128)S(1)}, f32[2,3,2,32,128]{4,3,2,1,0:T(8,128)}, u32[]{:S(2)}) copy-start(f32[2,3,2,32,128]{4,3,2,1,0:T(8,128)} %param.15) | copy-start | bytes 589828
  16.2 4.5 %copy-start.4 = (f32[2]{0:T(128)S(1)}, f32[2]{0:T(128)}, u32[]{:S(2)}) copy-start(f32[2]{0:T(128)} %param.16) | copy-start | bytes 28
  16.2 4.5 %copy-start.5 = (f32[2]{0:T(128)S(1)}, f32[2]{0:T(128)}, u32[]{:S(2)}) copy-start(f32[2]{0:T(128)} %param.17) | copy-start | bytes 28
  16.3 4.5 %copy-start.6 = (f32[2]{0:T(128)S(1)}, f32[2]{0:T(128)}, u32[]{:S(2)}) copy-start(f32[2]{0:T(128)} %constant.17) | copy-start | bytes 28
  16.3 7.4 %collective-permute-start = (f32[35,8,128]{2,1,0:T(8,128)S(1)}, f32[35,8,128]{2,1,0:T(8,128)S(1)}, u32[]{:S(2)}, u32[]{:S(2)}) collective-permute-start(f32[35,8,128]{2,1,0:T(8,128)S(1)} %shard_map.131), channel_id=1, source_target_pairs={{0,4},{4,8},{8,12},{12,16},{16,20},{20,24},{24,28},{28,32},{32,36}... | collective-permute-start | bytes 430088 | tf_op jit(solution)/shard_map/ppermute | solution.py:374
  25.3 29.6 %copy-start.1 = (bf16[256,384]{1,0:T(8,128)(2,1)S(1)}, bf16[256,384]{1,0:T(8,128)(2,1)}, u32[]{:S(2)}) copy-start(bf16[256,384]{1,0:T(8,128)(2,1)} %constant.9.clone.table) | copy-start | bytes 589828
  55.9 11.9 %copy-start.2 = (f32[64,64]{1,0:T(8,128)S(1)}, f32[64,64]{1,0:T(8,128)}, u32[]{:S(2)}) copy-start(f32[64,64]{1,0:T(8,128)} %constant.11.clone.turned) | copy-start | bytes 49156
  55.9 11.9 %copy-start.3 = (f32[64,64]{1,0:T(8,128)S(1)}, f32[64,64]{1,0:T(8,128)}, u32[]{:S(2)}) copy-start(f32[64,64]{1,0:T(8,128)} %constant.10.clone.straight) | copy-start | bytes 49156
  55.9 18.6 %all-to-all-start.2 = ((f32[128,1,384]{2,1,0:T(1,128)}), f32[128,1,384]{2,1,0:T(1,128)S(1)}, u32[]{:S(2)}, u32[]{:S(2)}) async-start(f32[128,1,384]{2,1,0:T(1,128)} %bitcast.8), calls=%async_computation.2 | async-start | bytes 393216 | tf_op jit(solution)/shard_map/all_to_all | solution.py:365
  62.2 5.6 %collective-permute-start.1 = (f32[72,128]{1,0:T(8,128)S(1)}, f32[72,128]{1,0:T(8,128)S(1)}, u32[]{:S(2)}, u32[]{:S(2)}) collective-permute-start(f32[72,128]{1,0:T(8,128)S(1)} %get-tuple-element.32), channel_id=1, source_target_pairs={{0,508},{4,0},{8,4},{12,8},{16,12},{20,16},{24,20},{28,24},{32,28}... | collective-permute-start | bytes 110600 | tf_op jit(solution)/shard_map/ppermute | solution.py:374

commit v9 on v8

--- a/solution.py
+++ b/solution.py
@@ -48,9 +48,10 @@
 def pack_columns_kernel(disp, prev, moduli, density, out, whole, sems):
     copies = []
     start = 0
-    for n, ref in enumerate((disp, prev, moduli, density)):
-        copies.append(pltpu.make_async_copy(ref, whole.at[pl.ds(start, ref.shape[0])], sems.at[n]))
-        start += ref.shape[0]
+    for ref in (disp, prev, moduli, density):
+        for i in range(ref.shape[0]):
+            copies.append(pltpu.make_async_copy(ref.at[i], whole.at[start], sems.at[start]))
+            start += 1
     for copy in copies:
         copy.start()
     for copy in copies:
@@ -218,7 +219,27 @@
     advance(lambda n: mid[n], lambda n: field[n], keep_updated, True)
 
 
-def own_rows_kernel(angles, whole, beside, updated, middle, head, waves, field, coef, strip, mid):
+def add_bins(operand, waves, item, old, tops, first, rows):
+    b = item // 3
+    one, two = tops
+    count, width = one.shape
+    half = width // 2
+    real = old[0] + waves[b : b + 1] * one + waves[2 + b : 3 + b] * two
+    imag = old[1] - waves[4 + b : 5 + b] * one - waves[6 + b : 7 + b] * two
+    if item < 4:
+        at = 3 * (item * rows + first)
+        operand[pl.ds(at, count, stride=3), :] = real
+        operand[pl.ds(at + 1, count, stride=3), :] = imag
+    else:
+        low = lax.broadcasted_iota(jnp.int32, (count, width), 1) < half
+        at = 3 * ((item - 4) * rows + first) + 2
+        operand[pl.ds(at, count, stride=3), :] = jnp.where(low, real, pltpu.roll(imag, half, 1))
+        operand[pl.ds(at + 6 * rows, count, stride=3), :] = jnp.where(low, pltpu.roll(real, half, 1), imag)
+
+
+def own_rows_kernel(
+    angles, whole, bins, beside, updated, middle, head, waves, operand, field, coef, strip, mid,
+):
     planes, rows, width = whole.shape
     waves[: angles.shape[0], :] = jnp.cos(angles[...])
     waves[angles.shape[0] :, :] = jnp.sin(angles[...])
@@ -238,10 +259,15 @@
         updated[n] = value
 
     two_steps(field, coef, mid, keep_middle, keep_updated)
+    inner = slice(EDGE, rows - EDGE)
+    for item in range(BINS // 2):
+        top = item % 3 * 3 + 2
+        old = (bins[2 * item, inner], bins[2 * item + 1, inner])
+        add_bins(operand, waves, item, old, (middle[top, inner], updated[top, inner]), EDGE, rows)
 
 
 def joint_rows_kernel(
-    waves, updated, middle, head, behind, bins, near, tail, operand, field, coef, mid,
+    waves, updated, middle, head, behind, bins, begun, near, tail, operand, field, coef, mid,
 ):
     rows, width = updated.shape[1], updated.shape[2]
     planes = field.shape[0]
@@ -261,9 +287,7 @@
         if n % 3 == 2:
             first = jnp.where(is_near, value[:EDGE], whole[n, :EDGE, :])
             last = jnp.where(is_near, whole[n, rows - EDGE :, :], value[EDGE:])
-            tops.setdefault(n // 3, []).append(
-                jnp.concatenate([first, whole[n, EDGE : rows - EDGE, :], last], axis=0)
-            )
+            tops.setdefault(n // 3, []).append((first, last))
 
     def keep_middle(n, value):
         mid[n] = value
@@ -274,29 +298,17 @@
 
     two_steps(field, coef, mid, keep_middle, keep_updated)
 
-    cosines, sines = waves[:HALO], waves[HALO:]
-    low = lax.broadcasted_iota(jnp.int32, (rows, width), 1) < width // 2
-    half = width // 2
-    for b in range(2):
-        for c in range(3):
-            one, two = tops[c]
-            item = b * 3 + c
-            old = []
-            rest = behind[planes + item]
-            for n, other in ((2 * item, pltpu.roll(rest, HALO, 0)), (2 * item + 1, rest)):
-                last = jnp.where(is_near, bins[n, rows - EDGE :], other)
-                old.append(jnp.concatenate([bins[n, : rows - EDGE], last], axis=0))
-            real = old[0] + cosines[b : b + 1] * one + cosines[2 + b : 3 + b] * two
-            imag = old[1] - sines[b : b + 1] * one - sines[2 + b : 3 + b] * two
-            if item < 4:
-                operand[pl.ds(3 * item * rows, rows, stride=3), :] = real
-                operand[pl.ds(3 * item * rows + 1, rows, stride=3), :] = imag
-            else:
-                at = 3 * (item - 4) * rows + 2
-                operand[pl.ds(at, rows, stride=3), :] = jnp.where(low, real, pltpu.roll(imag, half, 1))
-                operand[pl.ds(at + 6 * rows, rows, stride=3), :] = jnp.where(
-                    low, pltpu.roll(real, half, 1), imag
-                )
+    operand[...] = begun[...]
+    for item in range(BINS // 2):
+        rest = behind[planes + item]
+        starts, ends = zip(*tops[item % 3])
+        old = (bins[2 * item, :EDGE], bins[2 * item + 1, :EDGE])
+        add_bins(operand, waves, item, old, starts, 0, rows)
+        old = tuple(
+            jnp.where(is_near, bins[n, rows - EDGE :], other)
+            for n, other in ((2 * item, pltpu.roll(rest, HALO, 0)), (2 * item + 1, rest))
+        )
+        add_bins(operand, waves, item, old, ends, rows - EDGE, rows)
 
 
 def first_transform_kernel(received, table, tail, out, tail_out):
@@ -400,7 +412,7 @@
         ),
         in_specs=[hbm] * 4,
         out_specs=(vmem,) * 2,
-        scratch_shapes=[pltpu.SemaphoreType.DMA((4,))],
+        scratch_shapes=[pltpu.SemaphoreType.DMA((planes,))],
         compiler_params=pltpu.CompilerParams(vmem_limit_bytes=60 * 1024 * 1024),
     )(*arrays[:4])
     beside = exchange_gy(sides)
@@ -416,11 +428,11 @@
     angles = (phase[None, :] + steps[:, None] * omega[None, :]).reshape(-1)
     angles = jnp.broadcast_to(angles[:, None], (angles.shape[0], width))
     behind = pass_on(edge, "gx", 1)
-    updated, middle, head, waves = pl.pallas_call(
+    updated, middle, head, waves, begun = pl.pallas_call(
         own_rows_kernel,
-        out_shape=(f32(9, *block), f32(9, *block), f32(planes, EDGE, wide), f32(EDGE, width)),
-        in_specs=[vmem] * 3,
-        out_specs=(vmem,) * 4,
+        out_shape=(f32(9, *block), f32(9, *block), f32(planes, EDGE, wide), f32(EDGE, width), f32(3 * groups, width)),
+        in_specs=[vmem] * 4,
+        out_specs=(vmem,) * 5,
         scratch_shapes=[
             pltpu.VMEM((planes, rows, wide), jnp.float32),
             pltpu.VMEM((3, 11, rows, wide), jnp.float32),
@@ -429,11 +441,11 @@
         ],
         compiler_params=params,
         cost_estimate=pl.CostEstimate(flops=50_000_000, bytes_accessed=2_000_000, transcendentals=0),
-    )(angles, whole, beside)
+    )(angles, whole, arrays[4], beside)
     near, tail, operand = pl.pallas_call(
         joint_rows_kernel,
         out_shape=(f32(18, EDGE, width), f32(18 * HALO, width), f32(3 * groups, width)),
-        in_specs=[vmem] * 6,
+        in_specs=[vmem] * 7,
         out_specs=(vmem,) * 3,
         scratch_shapes=[
             pltpu.VMEM((planes, 2 * EDGE, wide), jnp.float32),
@@ -441,7 +453,7 @@
             pltpu.VMEM((9, 2 * EDGE, wide), jnp.float32),
         ],
         compiler_params=params,
-    )(waves, updated, middle, head, behind, arrays[4])
+    )(waves, updated, middle, head, behind, arrays[4], begun)
 
     stacked = np.concatenate(fourier_tables(groups), axis=0)
     high = stacked.astype(ml_dtypes.bfloat16)

time: 75.7 us -> 75.8 us (level)
  no operation moved by 1% of the time
where the time goes in v9:
time: 75.8 us; the launch traced here: 75.4 us
  blocking collectives  43.8 us (58%)
  starting transfers between devices  13.7 us (18%)
  waiting for transfers between devices  8.57 us (11%)
  Pallas kernels  8.36 us (11%)
    all_to_all x1, blocking collectives, exchange(): lax.all_to_all(shaped, 'gx', split_axis=0, concat_axis=0, tiled=True)  29.5 us
    all_to_all x1, blocking collectives, exchange_gy(): return lax.all_to_all(value, 'gy', split_axis=0, concat_axis=0, tiled=True)  14.3 us
    ppermute x2, starting transfers between devices, pass_on(): lax.ppermute(value, axis, [(i, (i + step) % peers) for i in range(peers)])  7.34 us
    all_to_all x1, starting transfers between devices, exchange(): lax.all_to_all(shaped, 'gx', split_axis=0, concat_axis=0, tiled=True)  6.35 us
    all_to_all x1, waiting for transfers between devices, exchange(): lax.all_to_all(shaped, 'gx', split_axis=0, concat_axis=0, tiled=True)  5.92 us
    pallas_call x1, Pallas kernels, on_device(): pl.pallas_call(own_rows_kernel, out_shape=(f32(9, *block), f32(9, *block)...  2.71 us
    ppermute x2, waiting for transfers between devices, pass_on(): lax.ppermute(value, axis, [(i, (i + step) % peers) for i in range(peers)])  2.65 us
  transfers between devices with their start and end apart: 3, of which 2 were waited for; matrix products, arithmetic and copies ran while one was open for 0% of the time, Pallas kernels for 5%

profile of v9, /device:TPU:1, one launch (start us, length us, event | category | flops | bytes accessed | tf_op | source)
XLA Modules:
  0.0 75.4 jit_solution(5841551441951171613)
XLA Ops:
  0.6 0.0 copy-start
  0.6 1.4 %shard_map.130 = (f32[4,4,896]{2,1,0:T(4,128)S(1)}, f32[27,32,128]{2,1,0:T(8,128)S(1)}) custom-call(f32[9,32,128]{2,1,0:T(8,128)} %bitcast.18, f32[9,32,128]{2,1,0:T(8,128)} %bitcast.19, f32[6,32,128]{2,1,0:T(8,128)} %bitcast.20, f32[3,32,128]{2,1,0:T(8,128)} %density.1), custom_call_target="tpu_custom_call" | custom-call | tf_op jit(solution)/shard_map/pallas_call | solution.py:407
  2.1 14.3 %all_to_all.15.beside = f32[4,4,896]{2,1,0:T(4,128)S(1)} all-to-all(f32[4,4,896]{2,1,0:T(4,128)S(1)} %get-tuple-element.22), channel_id=1, replica_groups=mesh['gx'=128,'gy'=4] {'gy'}, dimensions={0} | all-to-all | bytes 114688 | tf_op jit(solution)/shard_map/all_to_all | solution.py:381
  16.4 0.0 copy-done
  16.4 0.0 copy-start.4
  16.4 0.0 copy-start.5
  16.4 0.0 copy-start.6
  16.4 0.1 shard_map.131
  16.5 4.4 %collective-permute-start = (f32[35,8,128]{2,1,0:T(8,128)S(1)}, f32[35,8,128]{2,1,0:T(8,128)S(1)}, u32[]{:S(2)}, u32[]{:S(2)}) collective-permute-start(f32[35,8,128]{2,1,0:T(8,128)S(1)} %shard_map.131), channel_id=1, source_target_pairs={{0,4},{4,8},{8,12},{12,16},{16,20},{20,24},{24,28},{28,32},{32,36}... | collective-permute-start | bytes 430088 | tf_op jit(solution)/shard_map/ppermute | solution.py:386
  20.9 0.0 copy-done.4
  20.9 0.0 copy-done.5
  20.9 0.0 copy-done.6
  20.9 0.1 multiply_add_fusion
  21.0 0.1 add.17
  21.1 0.1 broadcast_in_dim.2.angles
  21.1 2.7 %shard_map.132 = (f32[9,32,128]{2,1,0:T(8,128)S(1)}, f32[9,32,128]{2,1,0:T(8,128)S(1)}, f32[27,8,256]{2,1,0:T(8,128)S(1)}, f32[8,128]{1,0:T(8,128)S(1)}, f32[384,128]{1,0:T(8,128)S(1)}) custom-call(f32[4,128]{1,0:T(4,128)S(1)} %broadcast_in_dim.2.angles, f32[27,32,128]{2,1,0:T(8,128)S(1)} %get-tuple-element.21.whole, f32[12,32,128]{2,1,0:T(8,128)S(1)} %bitcast.12, ...), custom_call_target="tpu_custom_call" | custom-call | flops 50000000 | bytes 2000000 | tf_op jit(solution)/shard_map/pallas_call | solution.py:431
  23.9 0.0 collective-permute-done.behind
  23.9 1.5 %shard_map.133 = (f32[18,8,128]{2,1,0:T(8,128)S(1)}, f32[72,128]{1,0:T(8,128)S(1)}, f32[384,128]{1,0:T(8,128)S(1)}) custom-call(f32[8,128]{1,0:T(8,128)S(1)} %get-tuple-element.27.waves, f32[9,32,128]{2,1,0:T(8,128)S(1)} %get-tuple-element.25.updated, f32[9,32,128]{2,1,0:T(8,128)S(1)} %get-tuple-element.26.middle, f32[27,8,256]{2,1,0:T(8,128)S(1)} %get-tuple-element.28.head, ...), custom_call_target="tpu_custom_call" | custom-call | tf_op jit(solution)/shard_map/pallas_call | solution.py:445
  25.4 0.0 copy-start.1
  25.4 29.5 %all_to_all.16 = f32[128,1,384]{2,1,0:T(1,128)S(1)} all-to-all(f32[128,1,384]{2,1,0:T(1,128)S(1)} %bitcast.16), channel_id=1, replica_groups=mesh['gx'=128,'gy'=4] {'gx'}, dimensions={0} | all-to-all | bytes 393216 | tf_op jit(solution)/shard_map/all_to_all | solution.py:377
  54.9 0.0 copy-done.1
  54.9 1.0 %shard_map.134 = (f32[384,128]{1,0:T(8,128)}, f32[72,128]{1,0:T(8,128)S(1)}) custom-call(f32[384,128]{1,0:T(8,128)S(1)} %bitcast.15, bf16[256,384]{1,0:T(8,128)(2,1)S(1)} %copy-done.1, f32[72,128]{1,0:T(8,128)S(1)} %get-tuple-element.33.tail), custom_call_target="tpu_custom_call" | custom-call | tf_op jit(solution)/shard_map/pallas_call | solution.py:462
  55.9 0.0 copy-start.2
  55.9 0.0 copy-start.3
  55.9 6.4 %all-to-all-start.2 = ((f32[128,1,384]{2,1,0:T(1,128)}), f32[128,1,384]{2,1,0:T(1,128)S(1)}, u32[]{:S(2)}, u32[]{:S(2)}) async-start(f32[128,1,384]{2,1,0:T(1,128)} %bitcast.8), calls=%async_computation.2 | async-start | bytes 393216 | tf_op jit(solution)/shard_map/all_to_all | solution.py:377
  62.3 2.9 %collective-permute-start.1 = (f32[72,128]{1,0:T(8,128)S(1)}, f32[72,128]{1,0:T(8,128)S(1)}, u32[]{:S(2)}, u32[]{:S(2)}) collective-permute-start(f32[72,128]{1,0:T(8,128)S(1)} %get-tuple-element.34), channel_id=1, source_target_pairs={{0,508},{4,0},{8,4},{12,8},{16,12},{20,16},{24,20},{28,24},{32,28}... | collective-permute-start | bytes 110600 | tf_op jit(solution)/shard_map/ppermute | solution.py:386
  65.2 2.7 %collective-permute-done.1.tail = f32[72,128]{1,0:T(8,128)S(1)} collective-permute-done((f32[72,128]{1,0:T(8,128)S(1)}, f32[72,128]{1,0:T(8,128)S(1)}, u32[]{:S(2)}, u32[]{:S(2)}) %collective-permute-start.1) | collective-permute-done | bytes 36896 | tf_op jit(solution)/shard_map/ppermute | solution.py:386
  67.9 0.0 copy-done.2
  67.9 0.0 copy-done.3
  67.9 0.7 shard_map.135
  68.6 5.9 %all-to-all-done.2 = f32[128,1,384]{2,1,0:T(1,128)S(1)} async-done(((f32[128,1,384]{2,1,0:T(1,128)}), f32[128,1,384]{2,1,0:T(1,128)S(1)}, u32[]{:S(2)}, u32[]{:S(2)}) %all-to-all-start.2) | async-done | bytes 196640 | tf_op jit(solution)/shard_map/all_to_all | solution.py:377
  74.5 0.9 %shard_map.136 = f32[6,2,32,128]{3,2,1,0:T(8,128)} custom-call(f32[384,128]{1,0:T(8,128)S(1)} %bitcast.14, f32[64,64]{1,0:T(8,128)S(1)} %get-tuple-element.38.matrix), custom_call_target="tpu_custom_call" | custom-call | tf_op jit(solution)/shard_map/pallas_call | solution.py:481
Async XLA Ops:
  0.6 15.7 %copy-start = (f32[2,3,2,32,128]{4,3,2,1,0:T(8,128)S(1)}, f32[2,3,2,32,128]{4,3,2,1,0:T(8,128)}, u32[]{:S(2)}) copy-start(f32[2,3,2,32,128]{4,3,2,1,0:T(8,128)} %param.15) | copy-start | bytes 589828
  16.4 4.5 %copy-start.4 = (f32[2]{0:T(128)S(1)}, f32[2]{0:T(128)}, u32[]{:S(2)}) copy-start(f32[2]{0:T(128)} %param.16) | copy-start | bytes 28
  16.4 4.5 %copy-start.5 = (f32[2]{0:T(128)S(1)}, f32[2]{0:T(128)}, u32[]{:S(2)}) copy-start(f32[2]{0:T(128)} %param.17) | copy-start | bytes 28
  16.4 4.5 %copy-start.6 = (f32[2]{0:T(128)S(1)}, f32[2]{0:T(128)}, u32[]{:S(2)}) copy-start(f32[2]{0:T(128)} %constant.17) | copy-start | bytes 28
  16.5 7.4 %collective-permute-start = (f32[35,8,128]{2,1,0:T(8,128)S(1)}, f32[35,8,128]{2,1,0:T(8,128)S(1)}, u32[]{:S(2)}, u32[]{:S(2)}) collective-permute-start(f32[35,8,128]{2,1,0:T(8,128)S(1)} %shard_map.131), channel_id=1, source_target_pairs={{0,4},{4,8},{8,12},{12,16},{16,20},{20,24},{24,28},{28,32},{32,36}... | collective-permute-start | bytes 430088 | tf_op jit(solution)/shard_map/ppermute | solution.py:386
  25.4 29.5 %copy-start.1 = (bf16[256,384]{1,0:T(8,128)(2,1)S(1)}, bf16[256,384]{1,0:T(8,128)(2,1)}, u32[]{:S(2)}) copy-start(bf16[256,384]{1,0:T(8,128)(2,1)} %constant.9.clone.table) | copy-start | bytes 589828
  55.9 11.9 %copy-start.2 = (f32[64,64]{1,0:T(8,128)S(1)}, f32[64,64]{1,0:T(8,128)}, u32[]{:S(2)}) copy-start(f32[64,64]{1,0:T(8,128)} %constant.11.clone.turned) | copy-start | bytes 49156
  55.9 11.9 %copy-start.3 = (f32[64,64]{1,0:T(8,128)S(1)}, f32[64,64]{1,0:T(8,128)}, u32[]{:S(2)}) copy-start(f32[64,64]{1,0:T(8,128)} %constant.10.clone.straight) | copy-start | bytes 49156
  55.9 18.6 %all-to-all-start.2 = ((f32[128,1,384]{2,1,0:T(1,128)}), f32[128,1,384]{2,1,0:T(1,128)S(1)}, u32[]{:S(2)}, u32[]{:S(2)}) async-start(f32[128,1,384]{2,1,0:T(1,128)} %bitcast.8), calls=%async_computation.2 | async-start | bytes 393216 | tf_op jit(solution)/shard_map/all_to_all | solution.py:377
  62.3 5.6 %collective-permute-start.1 = (f32[72,128]{1,0:T(8,128)S(1)}, f32[72,128]{1,0:T(8,128)S(1)}, u32[]{:S(2)}, u32[]{:S(2)}) collective-permute-start(f32[72,128]{1,0:T(8,128)S(1)} %get-tuple-element.34), channel_id=1, source_target_pairs={{0,508},{4,0},{8,4},{12,8},{16,12},{20,16},{24,20},{28,24},{32,28}... | collective-permute-start | bytes 110600 | tf_op jit(solution)/shard_map/ppermute | solution.py:386

commit v10 on v9

--- a/solution.py
+++ b/solution.py
@@ -48,10 +48,9 @@
 def pack_columns_kernel(disp, prev, moduli, density, out, whole, sems):
     copies = []
     start = 0
-    for ref in (disp, prev, moduli, density):
-        for i in range(ref.shape[0]):
-            copies.append(pltpu.make_async_copy(ref.at[i], whole.at[start], sems.at[start]))
-            start += 1
+    for n, ref in enumerate((disp, prev, moduli, density)):
+        copies.append(pltpu.make_async_copy(ref, whole.at[pl.ds(start, ref.shape[0])], sems.at[n]))
+        start += ref.shape[0]
     for copy in copies:
         copy.start()
     for copy in copies:
@@ -412,7 +411,7 @@
         ),
         in_specs=[hbm] * 4,
         out_specs=(vmem,) * 2,
-        scratch_shapes=[pltpu.SemaphoreType.DMA((planes,))],
+        scratch_shapes=[pltpu.SemaphoreType.DMA((4,))],
         compiler_params=pltpu.CompilerParams(vmem_limit_bytes=60 * 1024 * 1024),
     )(*arrays[:4])
     beside = exchange_gy(sides)

time: 75.8 us -> 75.7 us (level)
  no operation moved by 1% of the time
where the time goes in v10:
time: 75.7 us; the launch traced here: 75.3 us
  blocking collectives  43.8 us (58%)
  starting transfers between devices  13.7 us (18%)
  waiting for transfers between devices  8.57 us (11%)
  Pallas kernels  8.25 us (11%)
    all_to_all x1, blocking collectives, exchange(): lax.all_to_all(shaped, 'gx', split_axis=0, concat_axis=0, tiled=True)  29.5 us
    all_to_all x1, blocking collectives, exchange_gy(): return lax.all_to_all(value, 'gy', split_axis=0, concat_axis=0, tiled=True)  14.3 us
    ppermute x2, starting transfers between devices, pass_on(): lax.ppermute(value, axis, [(i, (i + step) % peers) for i in range(peers)])  7.34 us
    all_to_all x1, starting transfers between devices, exchange(): lax.all_to_all(shaped, 'gx', split_axis=0, concat_axis=0, tiled=True)  6.36 us
    all_to_all x1, waiting for transfers between devices, exchange(): lax.all_to_all(shaped, 'gx', split_axis=0, concat_axis=0, tiled=True)  5.92 us
    pallas_call x1, Pallas kernels, on_device(): pl.pallas_call(own_rows_kernel, out_shape=(f32(9, *block), f32(9, *block)...  2.71 us
    ppermute x2, waiting for transfers between devices, pass_on(): lax.ppermute(value, axis, [(i, (i + step) % peers) for i in range(peers)])  2.65 us
  transfers between devices with their start and end apart: 3, of which 2 were waited for; matrix products, arithmetic and copies ran while one was open for 0% of the time, Pallas kernels for 5%

profile of v10, /device:TPU:1, one launch (start us, length us, event | category | flops | bytes accessed | tf_op | source)
XLA Modules:
  0.0 75.3 jit_solution(12661156309373200732)
XLA Ops:
  0.6 0.0 copy-start
  0.6 1.3 %shard_map.130 = (f32[4,4,896]{2,1,0:T(4,128)S(1)}, f32[27,32,128]{2,1,0:T(8,128)S(1)}) custom-call(f32[9,32,128]{2,1,0:T(8,128)} %bitcast.18, f32[9,32,128]{2,1,0:T(8,128)} %bitcast.19, f32[6,32,128]{2,1,0:T(8,128)} %bitcast.20, f32[3,32,128]{2,1,0:T(8,128)} %density.1), custom_call_target="tpu_custom_call" | custom-call | tf_op jit(solution)/shard_map/pallas_call | solution.py:406
  2.0 14.3 %all_to_all.15.beside = f32[4,4,896]{2,1,0:T(4,128)S(1)} all-to-all(f32[4,4,896]{2,1,0:T(4,128)S(1)} %get-tuple-element.22), channel_id=1, replica_groups=mesh['gx'=128,'gy'=4] {'gy'}, dimensions={0} | all-to-all | bytes 114688 | tf_op jit(solution)/shard_map/all_to_all | solution.py:380
  16.2 0.0 copy-done
  16.2 0.0 copy-start.4
  16.2 0.0 copy-start.5
  16.3 0.0 copy-start.6
  16.3 0.1 shard_map.131
  16.3 4.4 %collective-permute-start = (f32[35,8,128]{2,1,0:T(8,128)S(1)}, f32[35,8,128]{2,1,0:T(8,128)S(1)}, u32[]{:S(2)}, u32[]{:S(2)}) collective-permute-start(f32[35,8,128]{2,1,0:T(8,128)S(1)} %shard_map.131), channel_id=1, source_target_pairs={{0,4},{4,8},{8,12},{12,16},{16,20},{20,24},{24,28},{28,32},{32,36}... | collective-permute-start | bytes 430088 | tf_op jit(solution)/shard_map/ppermute | solution.py:385
  20.8 0.0 copy-done.4
  20.8 0.0 copy-done.5
  20.8 0.0 copy-done.6
  20.8 0.1 multiply_add_fusion
  20.9 0.1 add.17
  21.0 0.1 broadcast_in_dim.2.angles
  21.0 2.7 %shard_map.132 = (f32[9,32,128]{2,1,0:T(8,128)S(1)}, f32[9,32,128]{2,1,0:T(8,128)S(1)}, f32[27,8,256]{2,1,0:T(8,128)S(1)}, f32[8,128]{1,0:T(8,128)S(1)}, f32[384,128]{1,0:T(8,128)S(1)}) custom-call(f32[4,128]{1,0:T(4,128)S(1)} %broadcast_in_dim.2.angles, f32[27,32,128]{2,1,0:T(8,128)S(1)} %get-tuple-element.21.whole, f32[12,32,128]{2,1,0:T(8,128)S(1)} %bitcast.12, ...), custom_call_target="tpu_custom_call" | custom-call | flops 50000000 | bytes 2000000 | tf_op jit(solution)/shard_map/pallas_call | solution.py:430
  23.8 0.0 collective-permute-done.behind
  23.8 1.5 %shard_map.133 = (f32[18,8,128]{2,1,0:T(8,128)S(1)}, f32[72,128]{1,0:T(8,128)S(1)}, f32[384,128]{1,0:T(8,128)S(1)}) custom-call(f32[8,128]{1,0:T(8,128)S(1)} %get-tuple-element.27.waves, f32[9,32,128]{2,1,0:T(8,128)S(1)} %get-tuple-element.25.updated, f32[9,32,128]{2,1,0:T(8,128)S(1)} %get-tuple-element.26.middle, f32[27,8,256]{2,1,0:T(8,128)S(1)} %get-tuple-element.28.head, ...), custom_call_target="tpu_custom_call" | custom-call | tf_op jit(solution)/shard_map/pallas_call | solution.py:444
  25.2 0.0 copy-start.1
  25.3 29.5 %all_to_all.16 = f32[128,1,384]{2,1,0:T(1,128)S(1)} all-to-all(f32[128,1,384]{2,1,0:T(1,128)S(1)} %bitcast.16), channel_id=1, replica_groups=mesh['gx'=128,'gy'=4] {'gx'}, dimensions={0} | all-to-all | bytes 393216 | tf_op jit(solution)/shard_map/all_to_all | solution.py:376
  54.8 0.0 copy-done.1
  54.8 1.0 %shard_map.134 = (f32[384,128]{1,0:T(8,128)}, f32[72,128]{1,0:T(8,128)S(1)}) custom-call(f32[384,128]{1,0:T(8,128)S(1)} %bitcast.15, bf16[256,384]{1,0:T(8,128)(2,1)S(1)} %copy-done.1, f32[72,128]{1,0:T(8,128)S(1)} %get-tuple-element.33.tail), custom_call_target="tpu_custom_call" | custom-call | tf_op jit(solution)/shard_map/pallas_call | solution.py:461
  55.8 0.0 copy-start.2
  55.8 0.0 copy-start.3
  55.8 6.4 %all-to-all-start.2 = ((f32[128,1,384]{2,1,0:T(1,128)}), f32[128,1,384]{2,1,0:T(1,128)S(1)}, u32[]{:S(2)}, u32[]{:S(2)}) async-start(f32[128,1,384]{2,1,0:T(1,128)} %bitcast.8), calls=%async_computation.2 | async-start | bytes 393216 | tf_op jit(solution)/shard_map/all_to_all | solution.py:376
  62.2 2.9 %collective-permute-start.1 = (f32[72,128]{1,0:T(8,128)S(1)}, f32[72,128]{1,0:T(8,128)S(1)}, u32[]{:S(2)}, u32[]{:S(2)}) collective-permute-start(f32[72,128]{1,0:T(8,128)S(1)} %get-tuple-element.34), channel_id=1, source_target_pairs={{0,508},{4,0},{8,4},{12,8},{16,12},{20,16},{24,20},{28,24},{32,28}... | collective-permute-start | bytes 110600 | tf_op jit(solution)/shard_map/ppermute | solution.py:385
  65.1 2.7 %collective-permute-done.1.tail = f32[72,128]{1,0:T(8,128)S(1)} collective-permute-done((f32[72,128]{1,0:T(8,128)S(1)}, f32[72,128]{1,0:T(8,128)S(1)}, u32[]{:S(2)}, u32[]{:S(2)}) %collective-permute-start.1) | collective-permute-done | bytes 36896 | tf_op jit(solution)/shard_map/ppermute | solution.py:385
  67.7 0.0 copy-done.2
  67.7 0.0 copy-done.3
  67.7 0.7 shard_map.135
  68.5 5.9 %all-to-all-done.2 = f32[128,1,384]{2,1,0:T(1,128)S(1)} async-done(((f32[128,1,384]{2,1,0:T(1,128)}), f32[128,1,384]{2,1,0:T(1,128)S(1)}, u32[]{:S(2)}, u32[]{:S(2)}) %all-to-all-start.2) | async-done | bytes 196640 | tf_op jit(solution)/shard_map/all_to_all | solution.py:376
  74.4 0.9 %shard_map.136 = f32[6,2,32,128]{3,2,1,0:T(8,128)} custom-call(f32[384,128]{1,0:T(8,128)S(1)} %bitcast.14, f32[64,64]{1,0:T(8,128)S(1)} %get-tuple-element.38.matrix), custom_call_target="tpu_custom_call" | custom-call | tf_op jit(solution)/shard_map/pallas_call | solution.py:480
Async XLA Ops:
  0.6 15.6 %copy-start = (f32[2,3,2,32,128]{4,3,2,1,0:T(8,128)S(1)}, f32[2,3,2,32,128]{4,3,2,1,0:T(8,128)}, u32[]{:S(2)}) copy-start(f32[2,3,2,32,128]{4,3,2,1,0:T(8,128)} %param.15) | copy-start | bytes 589828
  16.2 4.5 %copy-start.4 = (f32[2]{0:T(128)S(1)}, f32[2]{0:T(128)}, u32[]{:S(2)}) copy-start(f32[2]{0:T(128)} %param.16) | copy-start | bytes 28
  16.2 4.5 %copy-start.5 = (f32[2]{0:T(128)S(1)}, f32[2]{0:T(128)}, u32[]{:S(2)}) copy-start(f32[2]{0:T(128)} %param.17) | copy-start | bytes 28
  16.3 4.5 %copy-start.6 = (f32[2]{0:T(128)S(1)}, f32[2]{0:T(128)}, u32[]{:S(2)}) copy-start(f32[2]{0:T(128)} %constant.17) | copy-start | bytes 28
  16.3 7.4 %collective-permute-start = (f32[35,8,128]{2,1,0:T(8,128)S(1)}, f32[35,8,128]{2,1,0:T(8,128)S(1)}, u32[]{:S(2)}, u32[]{:S(2)}) collective-permute-start(f32[35,8,128]{2,1,0:T(8,128)S(1)} %shard_map.131), channel_id=1, source_target_pairs={{0,4},{4,8},{8,12},{12,16},{16,20},{20,24},{24,28},{28,32},{32,36}... | collective-permute-start | bytes 430088 | tf_op jit(solution)/shard_map/ppermute | solution.py:385
  25.2 29.5 %copy-start.1 = (bf16[256,384]{1,0:T(8,128)(2,1)S(1)}, bf16[256,384]{1,0:T(8,128)(2,1)}, u32[]{:S(2)}) copy-start(bf16[256,384]{1,0:T(8,128)(2,1)} %constant.9.clone.table) | copy-start | bytes 589828
  55.8 11.9 %copy-start.2 = (f32[64,64]{1,0:T(8,128)S(1)}, f32[64,64]{1,0:T(8,128)}, u32[]{:S(2)}) copy-start(f32[64,64]{1,0:T(8,128)} %constant.11.clone.turned) | copy-start | bytes 49156
  55.8 11.9 %copy-start.3 = (f32[64,64]{1,0:T(8,128)S(1)}, f32[64,64]{1,0:T(8,128)}, u32[]{:S(2)}) copy-start(f32[64,64]{1,0:T(8,128)} %constant.10.clone.straight) | copy-start | bytes 49156
  55.8 18.6 %all-to-all-start.2 = ((f32[128,1,384]{2,1,0:T(1,128)}), f32[128,1,384]{2,1,0:T(1,128)S(1)}, u32[]{:S(2)}, u32[]{:S(2)}) async-start(f32[128,1,384]{2,1,0:T(1,128)} %bitcast.8), calls=%async_computation.2 | async-start | bytes 393216 | tf_op jit(solution)/shard_map/all_to_all | solution.py:376
  62.2 5.6 %collective-permute-start.1 = (f32[72,128]{1,0:T(8,128)S(1)}, f32[72,128]{1,0:T(8,128)S(1)}, u32[]{:S(2)}, u32[]{:S(2)}) collective-permute-start(f32[72,128]{1,0:T(8,128)S(1)} %get-tuple-element.34), channel_id=1, source_target_pairs={{0,508},{4,0},{8,4},{12,8},{16,12},{20,16},{24,20},{28,24},{32,28}... | collective-permute-start | bytes 110600 | tf_op jit(solution)/shard_map/ppermute | solution.py:385
